TPU v7x, 32 devices: a whole 2x2x4 slice. The times are simulated.
32 devices in a mesh: loop: 8 (over z, y), rep: 4 (over x, core).
Axes of the slice: x: 2, y: 2, z: 4, core: 2. Of those that a mesh axis runs over, the one named last changes fastest.
Arguments:
- features: bfloat16 [8192, 128], P(('loop', 'rep')), may hold values from -6 to 6
- w_self: bfloat16 [128, 256], replicated, may hold values from -0.5 to 0.5
- w_neigh: bfloat16 [128, 256], replicated, may hold values from -0.5 to 0.5
- bias: float32 [256], replicated, may hold values from -3 to 3
- degree: int32 [8192], P(('loop', 'rep')), may hold values from 1 to 4
- tiles: bfloat16 [8, 4, 8, 16, 128, 128], P('loop', 'rep'), may hold values from -0.09375 to 0.09375
- dst_block: int32 [8, 4, 8, 16], P('loop', 'rep'), may hold values from 0 to 7, as said below
- src_block: int32 [8, 4, 8, 16], P('loop', 'rep'), may hold values from 0 to 1, as said below
- live_count: int32 [8, 4, 8], P('loop', 'rep'), may hold values from 1 to 16, as said below
- cotangent: bfloat16 [8192, 256], P(('loop', 'rep')), may hold values from -6 to 6
Outputs:
- output: bfloat16 [8192, 256], P(('loop', 'rep'))
- grad_input: bfloat16 [8192, 128], P(('loop', 'rep'))
- grad_self: float32 [128, 256], replicated
- grad_neigh: float32 [128, 256], replicated
- grad_bias: float32 [256], replicated
Inputs may be any that keep to these rules, and one draw needn't show every extreme that they name: Within one (p, r, q) the 16 slots name distinct pairs (dst_block, src_block). Within one (p, r, q) the 16 slots name distinct pairs (dst_block, src_block). `live_count`: every device (p, r) has some q with all 16 slots live; slots at or past the count hold tiles that are not part of the graph.
All inputs are finite; a program needn't handle non-finite values.
Results may differ from a plain program's by a relative error of at most 0.0075.
Values may be sent and summed in bfloat16 or wider, within the bound.
No kernel may reach another device: no remote copies, remote signals or barrier semaphores. Data moves between devices by JAX's collectives and lax.ppermute only.
A program may use at most 128 MiB of HBM per device.

v0:
```python
import math

import jax
import jax.numpy as jnp
from jax import lax
from jax.sharding import PartitionSpec as P


def shifted(block, axis, distance):
    devices = range(lax.axis_size(axis))
    route = [((i - distance) % len(devices), i) for i in devices]
    return lax.ppermute(block, axis, route)


def per_device(
    features, w_self, w_neigh, bias, degree, tiles, dst_block, src_block, live_count, cotangent
):
    loop_count = lax.axis_size("loop")
    rep_count = lax.axis_size("rep")
    loop_here = lax.axis_index("loop")
    row_count, feat_width = features.shape
    tile_size = tiles.shape[-1]
    slot_count = tiles.shape[3]
    sub_blocks = row_count // tile_size
    row_blocks = sub_blocks * rep_count
    tile_all = tiles[0, 0]
    dst_all = dst_block[0, 0]
    src_all = src_block[0, 0]
    live_all = jnp.arange(slot_count)[None, :] < live_count[0, 0][:, None]
    place_all = (
        (dst_all[:, :, None] == jnp.arange(row_blocks)[None, None, :]) & live_all[:, :, None]
    ).astype(jnp.float32)
    land_all = (
        (src_all[:, :, None] == jnp.arange(sub_blocks)[None, None, :]) & live_all[:, :, None]
    ).astype(jnp.float32)

    def pick_entry(table, source):
        return lax.dynamic_index_in_dim(table, source, 0, keepdims=False)

    def gather_term(source, panel):
        tile_part = pick_entry(tile_all, source)
        chosen = jnp.take(
            panel.reshape(sub_blocks, tile_size, feat_width), pick_entry(src_all, source), axis=0
        )
        product = jnp.einsum("tij,tjf->tif", tile_part, chosen, preferred_element_type=jnp.float32)
        return jnp.einsum(
            "td,tif->dif", pick_entry(place_all, source), product, precision=lax.Precision.HIGHEST
        )

    running = gather_term(loop_here, features)

    def one_way(step_index, state):
        panel, total = state
        panel = shifted(panel, "loop", 1)
        return (panel, total + gather_term((loop_here - step_index) % loop_count, panel))

    _, running = lax.fori_loop(1, loop_count, one_way, (features, running))
    agg_sum = lax.psum_scatter(
        running.reshape(row_blocks * tile_size, feat_width), "rep", scatter_dimension=0, tiled=True
    )
    degree_f = degree.astype(jnp.float32)[:, None]
    aggregate = (agg_sum / degree_f).astype(jnp.bfloat16)
    preact = (
        jnp.dot(features, w_self, preferred_element_type=jnp.float32)
        + jnp.dot(aggregate, w_neigh, preferred_element_type=jnp.float32)
        + bias
    )
    sigmoid_val = jax.nn.sigmoid(preact)
    output = (preact * sigmoid_val).astype(jnp.bfloat16)
    grad_pre = (
        cotangent.astype(jnp.float32) * sigmoid_val * (1.0 + preact * (1.0 - sigmoid_val))
    ).astype(jnp.bfloat16)
    grad_agg = (
        jnp.einsum("nh,fh->nf", grad_pre, w_neigh, preferred_element_type=jnp.float32) / degree_f
    ).astype(jnp.bfloat16)
    grad_whole = lax.all_gather(grad_agg, "rep", axis=0, tiled=True).reshape(
        row_blocks, tile_size, feat_width
    )
    node_total = row_count * loop_count * rep_count
    grad_scale = 1.0 / math.sqrt(node_total)
    grad_self, grad_neigh, grad_bias = lax.psum(
        (
            jnp.einsum("nf,nh->fh", features, grad_pre, preferred_element_type=jnp.float32)
            * grad_scale,
            jnp.einsum("nf,nh->fh", aggregate, grad_pre, preferred_element_type=jnp.float32)
            * grad_scale,
            jnp.sum(grad_pre.astype(jnp.float32), axis=0) * grad_scale,
        ),
        ("loop", "rep"),
    )
    self_grad = jnp.einsum("nh,fh->nf", grad_pre, w_self, preferred_element_type=jnp.float32)

    def spread_term(source):
        tile_part = pick_entry(tile_all, source)
        chosen = jnp.take(grad_whole, pick_entry(dst_all, source), axis=0)
        product = jnp.einsum("tij,tif->tjf", tile_part, chosen, preferred_element_type=jnp.float32)
        summed = jnp.einsum(
            "ts,tjf->sjf", pick_entry(land_all, source), product, precision=lax.Precision.HIGHEST
        )
        return summed.reshape(row_count, feat_width)

    def carry_along(step_index, total):
        total = shifted(total, "loop", -1)
        return total + spread_term((loop_here + 1 + step_index) % loop_count)

    neigh_grad = lax.fori_loop(
        1, loop_count, carry_along, spread_term((loop_here + 1) % loop_count)
    )
    grad_input = (self_grad + neigh_grad).astype(jnp.bfloat16)
    return (output, grad_input, grad_self, grad_neigh, grad_bias)


def solution(mesh):
    in_specs = (
        P(("loop", "rep"), None),
        P(),
        P(),
        P(),
        P(("loop", "rep")),
        P("loop", "rep", None, None, None, None),
        P("loop", "rep", None, None),
        P("loop", "rep", None, None),
        P("loop", "rep", None),
        P(("loop", "rep"), None),
    )
    out_specs = (P(("loop", "rep"), None), P(("loop", "rep"), None), P(), P(), P())
    return jax.shard_map(
        per_device, mesh=mesh, in_specs=in_specs, out_specs=out_specs, check_vma=False
    )
```

profile of v0, /device:TPU:0, one launch (start us, length us, event | category | flops | bytes accessed | tf_op | source)
XLA Modules:
  0.0 298.5 jit_solution(1597236850227760994)
XLA Ops:
  9.5 1.5 gather_fusion.2
  11.7 1.4 fusion.37
  14.3 74.5 %while.32 = (s32[]{:T(128)}, bf16[256,128]{1,0:T(8,128)(2,1)S(1)}, f32[8,128,128]{2,0,1:T(8,128)S(1)}, s32[]{:T(128)}, f32[8,16,8]{1,2,0:T(8,128)S(1)}, /*index=...) while((s32[]{:T(128)}, bf16[256,128]{1,0:T(8,128)(2,1)S(1)}, ...), condition=%wide.region_1.3_spmd, body=%wide.region_0.2_spmd.sunk | while | flops 92669040 | bytes 5644892 | solution.py:57
  14.3 3.0 %collective-permute-start = (bf16[256,128]{1,0:T(8,128)(2,1)S(1)}, bf16[256,128]{1,0:T(8,128)(2,1)S(1)}, u32[]{:S(2)}, u32[]{:S(2)}) collective-permute-start(bf16[256,128]{1,0:T(8,128)(2,1)S(1)} %get-tuple-element.526), channel_id=1, source_target_pairs={{28,0},{0,4},{4,8},{8,12},{12,16},{16,20},{20,24},{24,28},{29,1},{... | collective-permute-start | bytes 196616 | tf_op jit(solution)/shard_map/while/body/eval_jaxpr/ppermute | solution.py:12
  17.3 5.3 %collective-permute-done = bf16[256,128]{1,0:T(8,128)(2,1)S(1)} collective-permute-done((bf16[256,128]{1,0:T(8,128)(2,1)S(1)}, bf16[256,128]{1,0:T(8,128)(2,1)S(1)}, u32[]{:S(2)}, u32[]{:S(2)}) %collective-permute-start) | collective-permute-done | bytes 65568 | tf_op jit(solution)/shard_map/while/body/eval_jaxpr/ppermute | solution.py:12
  23.2 1.4 fusion.88
  24.7 1.3 convolution_add_fusion.4
  26.1 6.9 %collective-permute-done = bf16[256,128]{1,0:T(8,128)(2,1)S(1)} collective-permute-done((bf16[256,128]{1,0:T(8,128)(2,1)S(1)}, bf16[256,128]{1,0:T(8,128)(2,1)S(1)}, u32[]{:S(2)}, u32[]{:S(2)}) %collective-permute-start) | collective-permute-done | bytes 65568 | tf_op jit(solution)/shard_map/while/body/eval_jaxpr/ppermute | solution.py:12
  33.7 1.4 fusion.88
  35.1 1.3 convolution_add_fusion.4
  36.6 6.9 %collective-permute-done = bf16[256,128]{1,0:T(8,128)(2,1)S(1)} collective-permute-done((bf16[256,128]{1,0:T(8,128)(2,1)S(1)}, bf16[256,128]{1,0:T(8,128)(2,1)S(1)}, u32[]{:S(2)}, u32[]{:S(2)}) %collective-permute-start) | collective-permute-done | bytes 65568 | tf_op jit(solution)/shard_map/while/body/eval_jaxpr/ppermute | solution.py:12
  44.1 1.4 fusion.88
  45.6 1.3 convolution_add_fusion.4
  47.1 6.9 %collective-permute-done = bf16[256,128]{1,0:T(8,128)(2,1)S(1)} collective-permute-done((bf16[256,128]{1,0:T(8,128)(2,1)S(1)}, bf16[256,128]{1,0:T(8,128)(2,1)S(1)}, u32[]{:S(2)}, u32[]{:S(2)}) %collective-permute-start) | collective-permute-done | bytes 65568 | tf_op jit(solution)/shard_map/while/body/eval_jaxpr/ppermute | solution.py:12
  54.6 1.4 fusion.88
  56.0 1.3 convolution_add_fusion.4
  57.5 6.9 %collective-permute-done = bf16[256,128]{1,0:T(8,128)(2,1)S(1)} collective-permute-done((bf16[256,128]{1,0:T(8,128)(2,1)S(1)}, bf16[256,128]{1,0:T(8,128)(2,1)S(1)}, u32[]{:S(2)}, u32[]{:S(2)}) %collective-permute-start) | collective-permute-done | bytes 65568 | tf_op jit(solution)/shard_map/while/body/eval_jaxpr/ppermute | solution.py:12
  65.1 1.4 fusion.88
  66.5 1.3 convolution_add_fusion.4
  68.0 6.9 %collective-permute-done = bf16[256,128]{1,0:T(8,128)(2,1)S(1)} collective-permute-done((bf16[256,128]{1,0:T(8,128)(2,1)S(1)}, bf16[256,128]{1,0:T(8,128)(2,1)S(1)}, u32[]{:S(2)}, u32[]{:S(2)}) %collective-permute-start) | collective-permute-done | bytes 65568 | tf_op jit(solution)/shard_map/while/body/eval_jaxpr/ppermute | solution.py:12
  75.5 1.4 fusion.88
  76.9 1.3 convolution_add_fusion.4
  78.4 6.9 %collective-permute-done = bf16[256,128]{1,0:T(8,128)(2,1)S(1)} collective-permute-done((bf16[256,128]{1,0:T(8,128)(2,1)S(1)}, bf16[256,128]{1,0:T(8,128)(2,1)S(1)}, u32[]{:S(2)}, u32[]{:S(2)}) %collective-permute-start) | collective-permute-done | bytes 65568 | tf_op jit(solution)/shard_map/while/body/eval_jaxpr/ppermute | solution.py:12
  86.0 1.4 fusion.88
  87.4 1.3 convolution_add_fusion.4
  90.7 18.2 %reduce-scatter.2.cloned.1.call-done = f32[256,128]{1,0:T(8,128)} async-done(((f32[1024,128]{1,0:T(8,128)}), f32[256,128]{1,0:T(8,128)}) %reduce-scatter.2.cloned.1.call-update) | async-done | bytes 131088 | tf_op jit(solution)/shard_map/reduce_scatter | solution.py:58
  108.9 2.0 convert_reduce_fusion
  112.0 5.8 %all_gather.3 = bf16[1024,128]{1,0:T(8,128)(2,1)S(1)} all-gather(bf16[256,128]{1,0:T(8,128)(2,1)S(1)} %fusion.30), channel_id=1, replica_groups=mesh['loop'=8,'rep'=4] {'rep'}, dimensions={0}, use_global_device_ids=true | all-gather | bytes 327680 | tf_op jit(solution)/shard_map/all_gather | solution.py:76
  118.4 1.4 fusion.35
  120.9 39.4 %psum.23 = f32[256]{0:T(256)} all-reduce(f32[256]{0:T(256)S(1)} %broadcast_multiply_fusion), channel_id=1, replica_groups=mesh['loop'=8,'rep'=4] {'loop','rep'}, use_global_device_ids=true, to_apply=%region_8.11 | all-reduce | flops 256 | bytes 2048 | tf_op jit(solution)/shard_map/psum | solution.py:81
  161.3 57.6 %while.33 = (s32[]{:T(128)}, f32[256,128]{1,0:T(8,128)S(1)}, s32[]{:T(128)}, f32[8,16,2]{1,2,0:T(2,128)S(1)}, bf16[8,16,128,128]{3,2,1,0:T(8,128)(2,1)}, /*index...) while((s32[]{:T(128)}, f32[256,128]{1,0:T(8,128)S(1)}, ...), condition=%wide.region_4.7_spmd, body=%wide.region_3.6_spmd.sunk | while | flops 73696368 | bytes 5510748 | solution.py:106
  161.3 4.3 %collective-permute-start.1 = (f32[256,128]{1,0:T(8,128)S(1)}, f32[256,128]{1,0:T(8,128)S(1)}, u32[]{:S(2)}, u32[]{:S(2)}) collective-permute-start(f32[256,128]{1,0:T(8,128)S(1)} %get-tuple-element.559), channel_id=1, source_target_pairs={{4,0},{8,4},{12,8},{16,12},{20,16},{24,20},{28,24},{0,28},{5,1},{9... | collective-permute-start | bytes 393224 | tf_op jit(solution)/shard_map/while/body/eval_jaxpr/ppermute | solution.py:12
  166.9 1.4 fusion.93
  169.6 3.9 %collective-permute-start.1 = (f32[256,128]{1,0:T(8,128)S(1)}, f32[256,128]{1,0:T(8,128)S(1)}, u32[]{:S(2)}, u32[]{:S(2)}) collective-permute-start(f32[256,128]{1,0:T(8,128)S(1)} %get-tuple-element.559), channel_id=1, source_target_pairs={{4,0},{8,4},{12,8},{16,12},{20,16},{24,20},{28,24},{0,28},{5,1},{9... | collective-permute-start | bytes 393224 | tf_op jit(solution)/shard_map/while/body/eval_jaxpr/ppermute | solution.py:12
  174.8 1.4 fusion.93
  177.5 3.8 %collective-permute-start.1 = (f32[256,128]{1,0:T(8,128)S(1)}, f32[256,128]{1,0:T(8,128)S(1)}, u32[]{:S(2)}, u32[]{:S(2)}) collective-permute-start(f32[256,128]{1,0:T(8,128)S(1)} %get-tuple-element.559), channel_id=1, source_target_pairs={{4,0},{8,4},{12,8},{16,12},{20,16},{24,20},{28,24},{0,28},{5,1},{9... | collective-permute-start | bytes 393224 | tf_op jit(solution)/shard_map/while/body/eval_jaxpr/ppermute | solution.py:12
  182.7 1.4 fusion.93
  185.4 3.8 %collective-permute-start.1 = (f32[256,128]{1,0:T(8,128)S(1)}, f32[256,128]{1,0:T(8,128)S(1)}, u32[]{:S(2)}, u32[]{:S(2)}) collective-permute-start(f32[256,128]{1,0:T(8,128)S(1)} %get-tuple-element.559), channel_id=1, source_target_pairs={{4,0},{8,4},{12,8},{16,12},{20,16},{24,20},{28,24},{0,28},{5,1},{9... | collective-permute-start | bytes 393224 | tf_op jit(solution)/shard_map/while/body/eval_jaxpr/ppermute | solution.py:12
  190.6 1.4 fusion.93
  193.3 4.0 %collective-permute-start.1 = (f32[256,128]{1,0:T(8,128)S(1)}, f32[256,128]{1,0:T(8,128)S(1)}, u32[]{:S(2)}, u32[]{:S(2)}) collective-permute-start(f32[256,128]{1,0:T(8,128)S(1)} %get-tuple-element.559), channel_id=1, source_target_pairs={{4,0},{8,4},{12,8},{16,12},{20,16},{24,20},{28,24},{0,28},{5,1},{9... | collective-permute-start | bytes 393224 | tf_op jit(solution)/shard_map/while/body/eval_jaxpr/ppermute | solution.py:12
  198.6 1.4 fusion.93
  201.3 5.2 %collective-permute-start.1 = (f32[256,128]{1,0:T(8,128)S(1)}, f32[256,128]{1,0:T(8,128)S(1)}, u32[]{:S(2)}, u32[]{:S(2)}) collective-permute-start(f32[256,128]{1,0:T(8,128)S(1)} %get-tuple-element.559), channel_id=1, source_target_pairs={{4,0},{8,4},{12,8},{16,12},{20,16},{24,20},{28,24},{0,28},{5,1},{9... | collective-permute-start | bytes 393224 | tf_op jit(solution)/shard_map/while/body/eval_jaxpr/ppermute | solution.py:12
  208.0 1.4 fusion.93
  210.6 4.2 %collective-permute-start.1 = (f32[256,128]{1,0:T(8,128)S(1)}, f32[256,128]{1,0:T(8,128)S(1)}, u32[]{:S(2)}, u32[]{:S(2)}) collective-permute-start(f32[256,128]{1,0:T(8,128)S(1)} %get-tuple-element.559), channel_id=1, source_target_pairs={{4,0},{8,4},{12,8},{16,12},{20,16},{24,20},{28,24},{0,28},{5,1},{9... | collective-permute-start | bytes 393224 | tf_op jit(solution)/shard_map/while/body/eval_jaxpr/ppermute | solution.py:12
  216.2 1.4 fusion.93
  219.7 68.7 %all-reduce.3.cloned.1.call-done = (f32[128,256]{0,1:T(8,128)}, f32[128,256]{1,0:T(8,128)}) async-done(((f32[128,256]{0,1:T(8,128)}, f32[128,256]{1,0:T(8,128)}), (f32[128,256]{0,1:T(8,128)}, f32[128,256]{1,0:T(8,128)})) %all-reduce.3.cloned.1.call-update) | async-done | bytes 262160 | tf_op jit(solution)/shard_map/psum | solution.py:81
  288.4 1.7 copy.20
  290.1 1.6 copy.56
  (123 shorter events, 33.6 us)
Async XLA Ops:
  7.2 101.7 %copy-start = (bf16[128,256]{1,0:T(8,128)(2,1)S(1)}, bf16[128,256]{1,0:T(8,128)(2,1)}, u32[]{:S(2)}) copy-start(bf16[128,256]{1,0:T(8,128)(2,1)} %param.20) | copy-start | bytes 196612
  7.2 7.0 %copy-start.3 = (s32[1,1,8,16]{3,2,1,0:T(8,128)S(1)}, s32[1,1,8,16]{3,2,1,0:T(8,128)}, u32[]{:S(2)}) copy-start(s32[1,1,8,16]{3,2,1,0:T(8,128)} %param.25) | copy-start | bytes 1540
  7.2 101.7 %reduce-scatter.2.cloned.1.call-start = ((), (), s32[]{:S(2)}) async-start(), calls=%async_computation.1 | async-start | bytes 655360 | tf_op jit(solution)/shard_map/reduce_scatter | solution.py:58
  14.2 75.5 %copy-start.4 = (s32[256]{0:T(256)S(1)}, s32[256]{0:T(256)}, u32[]{:S(2)}) copy-start(s32[256]{0:T(256)} %param.22) | copy-start | bytes 3076
  14.2 76.3 %copy-start.1 = (bf16[256,128]{1,0:T(8,128)(2,1)S(1)}, bf16[256,128]{1,0:T(8,128)(2,1)}, u32[]{:S(2)}) copy-start(bf16[256,128]{1,0:T(8,128)(2,1)} %param.18) | copy-start | bytes 196612
  14.2 76.3 %copy-start.2 = (bf16[128,256]{1,0:T(8,128)(2,1)S(1)}, bf16[128,256]{1,0:T(8,128)(2,1)}, u32[]{:S(2)}) copy-start(bf16[128,256]{1,0:T(8,128)(2,1)} %param.19) | copy-start | bytes 196612
  14.2 94.7 %copy-start.5 = (bf16[256,256]{1,0:T(8,128)(2,1)S(1)}, bf16[256,256]{1,0:T(8,128)(2,1)}, u32[]{:S(2)}) copy-start(bf16[256,256]{1,0:T(8,128)(2,1)} %param.27) | copy-start | bytes 393220
  14.3 94.7 %copy-start.7 = (f32[256]{0:T(256)S(1)}, f32[256]{0:T(256)}, u32[]{:S(2)}) copy-start(f32[256]{0:T(256)} %param.21) | copy-start | bytes 3076
  14.3 8.3 %collective-permute-start = (bf16[256,128]{1,0:T(8,128)(2,1)S(1)}, bf16[256,128]{1,0:T(8,128)(2,1)S(1)}, u32[]{:S(2)}, u32[]{:S(2)}) collective-permute-start(bf16[256,128]{1,0:T(8,128)(2,1)S(1)} %get-tuple-element.526), channel_id=1, source_target_pairs={{28,0},{0,4},{4,8},{8,12},{12,16},{16,20},{20,24},{24,28},{29,1},{... | collective-permute-start | bytes 196616 | tf_op jit(solution)/shard_map/while/body/eval_jaxpr/ppermute | solution.py:12
  26.0 7.0 %collective-permute-start = (bf16[256,128]{1,0:T(8,128)(2,1)S(1)}, bf16[256,128]{1,0:T(8,128)(2,1)S(1)}, u32[]{:S(2)}, u32[]{:S(2)}) collective-permute-start(bf16[256,128]{1,0:T(8,128)(2,1)S(1)} %get-tuple-element.526), channel_id=1, source_target_pairs={{28,0},{0,4},{4,8},{8,12},{12,16},{16,20},{20,24},{24,28},{29,1},{... | collective-permute-start | bytes 196616 | tf_op jit(solution)/shard_map/while/body/eval_jaxpr/ppermute | solution.py:12
  36.5 7.0 %collective-permute-start = (bf16[256,128]{1,0:T(8,128)(2,1)S(1)}, bf16[256,128]{1,0:T(8,128)(2,1)S(1)}, u32[]{:S(2)}, u32[]{:S(2)}) collective-permute-start(bf16[256,128]{1,0:T(8,128)(2,1)S(1)} %get-tuple-element.526), channel_id=1, source_target_pairs={{28,0},{0,4},{4,8},{8,12},{12,16},{16,20},{20,24},{24,28},{29,1},{... | collective-permute-start | bytes 196616 | tf_op jit(solution)/shard_map/while/body/eval_jaxpr/ppermute | solution.py:12
  46.9 7.0 %collective-permute-start = (bf16[256,128]{1,0:T(8,128)(2,1)S(1)}, bf16[256,128]{1,0:T(8,128)(2,1)S(1)}, u32[]{:S(2)}, u32[]{:S(2)}) collective-permute-start(bf16[256,128]{1,0:T(8,128)(2,1)S(1)} %get-tuple-element.526), channel_id=1, source_target_pairs={{28,0},{0,4},{4,8},{8,12},{12,16},{16,20},{20,24},{24,28},{29,1},{... | collective-permute-start | bytes 196616 | tf_op jit(solution)/shard_map/while/body/eval_jaxpr/ppermute | solution.py:12
  57.4 7.0 %collective-permute-start = (bf16[256,128]{1,0:T(8,128)(2,1)S(1)}, bf16[256,128]{1,0:T(8,128)(2,1)S(1)}, u32[]{:S(2)}, u32[]{:S(2)}) collective-permute-start(bf16[256,128]{1,0:T(8,128)(2,1)S(1)} %get-tuple-element.526), channel_id=1, source_target_pairs={{28,0},{0,4},{4,8},{8,12},{12,16},{16,20},{20,24},{24,28},{29,1},{... | collective-permute-start | bytes 196616 | tf_op jit(solution)/shard_map/while/body/eval_jaxpr/ppermute | solution.py:12
  67.9 7.0 %collective-permute-start = (bf16[256,128]{1,0:T(8,128)(2,1)S(1)}, bf16[256,128]{1,0:T(8,128)(2,1)S(1)}, u32[]{:S(2)}, u32[]{:S(2)}) collective-permute-start(bf16[256,128]{1,0:T(8,128)(2,1)S(1)} %get-tuple-element.526), channel_id=1, source_target_pairs={{28,0},{0,4},{4,8},{8,12},{12,16},{16,20},{20,24},{24,28},{29,1},{... | collective-permute-start | bytes 196616 | tf_op jit(solution)/shard_map/while/body/eval_jaxpr/ppermute | solution.py:12
  78.3 7.0 %collective-permute-start = (bf16[256,128]{1,0:T(8,128)(2,1)S(1)}, bf16[256,128]{1,0:T(8,128)(2,1)S(1)}, u32[]{:S(2)}, u32[]{:S(2)}) collective-permute-start(bf16[256,128]{1,0:T(8,128)(2,1)S(1)} %get-tuple-element.526), channel_id=1, source_target_pairs={{28,0},{0,4},{4,8},{8,12},{12,16},{16,20},{20,24},{24,28},{29,1},{... | collective-permute-start | bytes 196616 | tf_op jit(solution)/shard_map/while/body/eval_jaxpr/ppermute | solution.py:12
  89.7 198.8 %all-reduce.3.cloned.1.call-start = ((), (), s32[]{:S(2)}) async-start(), calls=%async_computation.2 | async-start | bytes 524288 | tf_op jit(solution)/shard_map/psum | solution.py:81
  108.9 51.4 %copy-start.6 = (f32[256,128]{1,0:T(8,128)S(1)}, f32[256,128]{1,0:T(8,128)}, u32[]{:S(2)}) copy-start(f32[256,128]{1,0:T(8,128)} %reduce-scatter.2.cloned.1.call-done) | copy-start | bytes 393220
  161.3 8.3 %collective-permute-start.1 = (f32[256,128]{1,0:T(8,128)S(1)}, f32[256,128]{1,0:T(8,128)S(1)}, u32[]{:S(2)}, u32[]{:S(2)}) collective-permute-start(f32[256,128]{1,0:T(8,128)S(1)} %get-tuple-element.559), channel_id=1, source_target_pairs={{4,0},{8,4},{12,8},{16,12},{20,16},{24,20},{28,24},{0,28},{5,1},{9... | collective-permute-start | bytes 393224 | tf_op jit(solution)/shard_map/while/body/eval_jaxpr/ppermute | solution.py:12
  169.6 7.9 %collective-permute-start.1 = (f32[256,128]{1,0:T(8,128)S(1)}, f32[256,128]{1,0:T(8,128)S(1)}, u32[]{:S(2)}, u32[]{:S(2)}) collective-permute-start(f32[256,128]{1,0:T(8,128)S(1)} %get-tuple-element.559), channel_id=1, source_target_pairs={{4,0},{8,4},{12,8},{16,12},{20,16},{24,20},{28,24},{0,28},{5,1},{9... | collective-permute-start | bytes 393224 | tf_op jit(solution)/shard_map/while/body/eval_jaxpr/ppermute | solution.py:12
  177.5 7.8 %collective-permute-start.1 = (f32[256,128]{1,0:T(8,128)S(1)}, f32[256,128]{1,0:T(8,128)S(1)}, u32[]{:S(2)}, u32[]{:S(2)}) collective-permute-start(f32[256,128]{1,0:T(8,128)S(1)} %get-tuple-element.559), channel_id=1, source_target_pairs={{4,0},{8,4},{12,8},{16,12},{20,16},{24,20},{28,24},{0,28},{5,1},{9... | collective-permute-start | bytes 393224 | tf_op jit(solution)/shard_map/while/body/eval_jaxpr/ppermute | solution.py:12
  185.4 7.8 %collective-permute-start.1 = (f32[256,128]{1,0:T(8,128)S(1)}, f32[256,128]{1,0:T(8,128)S(1)}, u32[]{:S(2)}, u32[]{:S(2)}) collective-permute-start(f32[256,128]{1,0:T(8,128)S(1)} %get-tuple-element.559), channel_id=1, source_target_pairs={{4,0},{8,4},{12,8},{16,12},{20,16},{24,20},{28,24},{0,28},{5,1},{9... | collective-permute-start | bytes 393224 | tf_op jit(solution)/shard_map/while/body/eval_jaxpr/ppermute | solution.py:12
  193.3 8.0 %collective-permute-start.1 = (f32[256,128]{1,0:T(8,128)S(1)}, f32[256,128]{1,0:T(8,128)S(1)}, u32[]{:S(2)}, u32[]{:S(2)}) collective-permute-start(f32[256,128]{1,0:T(8,128)S(1)} %get-tuple-element.559), channel_id=1, source_target_pairs={{4,0},{8,4},{12,8},{16,12},{20,16},{24,20},{28,24},{0,28},{5,1},{9... | collective-permute-start | bytes 393224 | tf_op jit(solution)/shard_map/while/body/eval_jaxpr/ppermute | solution.py:12
  201.3 9.2 %collective-permute-start.1 = (f32[256,128]{1,0:T(8,128)S(1)}, f32[256,128]{1,0:T(8,128)S(1)}, u32[]{:S(2)}, u32[]{:S(2)}) collective-permute-start(f32[256,128]{1,0:T(8,128)S(1)} %get-tuple-element.559), channel_id=1, source_target_pairs={{4,0},{8,4},{12,8},{16,12},{20,16},{24,20},{28,24},{0,28},{5,1},{9... | collective-permute-start | bytes 393224 | tf_op jit(solution)/shard_map/while/body/eval_jaxpr/ppermute | solution.py:12
  210.6 8.2 %collective-permute-start.1 = (f32[256,128]{1,0:T(8,128)S(1)}, f32[256,128]{1,0:T(8,128)S(1)}, u32[]{:S(2)}, u32[]{:S(2)}) collective-permute-start(f32[256,128]{1,0:T(8,128)S(1)} %get-tuple-element.559), channel_id=1, source_target_pairs={{4,0},{8,4},{12,8},{16,12},{20,16},{24,20},{28,24},{0,28},{5,1},{9... | collective-permute-start | bytes 393224 | tf_op jit(solution)/shard_map/while/body/eval_jaxpr/ppermute | solution.py:12
Sparse Core Ops, SparseCore 0:
  89.8 19.0 reduce-scatter.1
  161.4 127.0 all-reduce.2
where the time goes:
time: 300 us; the launch traced here: 299 us
  waiting for transfers between devices  134 us (45%)
  matrix products  47.4 us (16%)
  blocking collectives  45.1 us (15%)
  starting transfers between devices  32.7 us (11%)
  local copies, waits for them, and re-layouts  16.3 us (5%)
  between operations  14.3 us (5%)
  other arithmetic  8.05 us (3%)
    psum x1, waiting for transfers between devices, per_device(): lax.psum((jnp.einsum('nf,nh->fh', features, grad_pre, preferred_element_t...  68.7 us
    ppermute x14, waiting for transfers between devices, shifted(): return lax.ppermute(block, axis, route)  46.7 us
    psum x1, blocking collectives, per_device(): lax.psum((jnp.einsum('nf,nh->fh', features, grad_pre, preferred_element_t...  39.4 us
    ppermute x14, starting transfers between devices, shifted(): return lax.ppermute(block, axis, route)  32.6 us
    reduce_scatter x1, waiting for transfers between devices, per_device(): lax.psum_scatter(running.reshape(row_blocks * tile_size, feat_width), 're...  18.2 us
    dot_general x8, matrix products, spread_term(): jnp.einsum('tij,tif->tjf', tile_part, chosen, preferred_element_type=jnp....  11.4 us
    dot_general x8, matrix products, gather_term(): jnp.einsum('tij,tjf->tif', tile_part, chosen, preferred_element_type=jnp....  11.3 us
    dot_general x8, matrix products, gather_term(): jnp.einsum('td,tif->dif', pick_entry(place_all, source), product, precisi...  10.4 us
  transfers between devices with their start and end apart: 16, of which 10 were waited for; matrix products, arithmetic and copies ran while one was open for 10% of the time, Pallas kernels for 0%

commit v1 on v0

v1 whole, which is shorter than its diff:
```python
import functools
import math

import jax
import jax.numpy as jnp
from jax import lax
from jax.experimental import pallas as pl
from jax.experimental.pallas import tpu as pltpu
from jax.sharding import PartitionSpec as P

VMEM = pl.BlockSpec(memory_space=pltpu.VMEM)
HBM = pl.BlockSpec(memory_space=pltpu.HBM)


def swap(block, axis, mask):
    return lax.ppermute(block, axis, [(i, i ^ mask) for i in range(lax.axis_size(axis))])


def grant(held):
    return min(held + (4 << 20), 56 << 20)


def call(kernel, out_shape, in_specs, args, flops=0):
    moved = sum(math.prod(a.shape) * a.dtype.itemsize for a in (*args, *out_shape))
    return pl.pallas_call(
        kernel,
        out_shape=list(out_shape),
        in_specs=in_specs,
        out_specs=[VMEM] * len(out_shape),
        compiler_params=pltpu.CompilerParams(vmem_limit_bytes=grant(moved)),
        cost_estimate=pl.CostEstimate(flops=flops, bytes_accessed=moved, transcendentals=0),
    )(*args)


def after(value, *earlier):
    return lax.optimization_barrier((value, *earlier))


def in_hbm(value):
    return pltpu.with_memory_space_constraint(value, pltpu.HBM)


def f32(shape):
    return jax.ShapeDtypeStruct(shape, jnp.float32)


def bf16(shape):
    return jax.ShapeDtypeStruct(shape, jnp.bfloat16)


def place_kernel(
    near_count, order, rep_count, sub_blocks, packs, dst_far, src_far, live_far, tiles, *refs
):
    count = len(order)
    sides, refs = (refs[:3], refs[3:]) if packs else ((), refs)
    mats, refs = refs[:count], refs[count:]
    if packs:
        bundle, refs = refs[0], refs[1:]
    dst, src, live, stage, degree, read, done, left = refs
    tile_size = tiles.shape[-1]
    loop_here, rep_here = lax.axis_index("loop"), lax.axis_index("rep")
    moves = [(dst_far, dst), (src_far, src), (live_far, live)]
    if packs:
        width = sides[0].shape[1]
        moves += [
            (sides[1], degree),
            (sides[0], bundle.at[:, pl.ds(0, width)]),
            (sides[2], bundle.at[:, pl.ds(2 * width, bundle.shape[1] - 2 * width)]),
        ]
    moves = [pltpu.make_async_copy(far, near, read.at[k]) for k, (far, near) in enumerate(moves)]
    for move in moves:
        move.start()
    built = [mats[k] if k < near_count else stage.at[k - near_count] for k in range(count)]

    def copy(k, source, slot, row, column):
        rows = pl.ds(pl.multiple_of(row * tile_size, tile_size), tile_size)
        columns = pl.ds(pl.multiple_of(column * tile_size, tile_size), tile_size)
        return pltpu.make_async_copy(
            tiles.at[source, slot], built[k].at[rows, columns], done.at[k]
        )

    backward = list(reversed(range(count)))
    for k in backward:
        built[k][...] = jnp.zeros(built[k].shape, jnp.bfloat16)
        if k == count - 1:
            for move in moves[:3]:
                move.wait()
        source = loop_here ^ order[k]

        def put(slot, carry):
            block, column = dst[source, slot], src[source, slot]
            away = lax.div(block, sub_blocks) ^ rep_here
            panel = (away & 1) * (rep_count // 2) + lax.shift_right_logical(away, 1)
            row = panel * sub_blocks + lax.rem(block, sub_blocks)
            copy(k, source, slot, row, column).start()
            return carry

        lax.fori_loop(0, live[0, source], put, 0)
    if packs:
        for move in moves[3:]:
            move.wait()
        degree_f = jnp.broadcast_to(degree[...].astype(jnp.float32), (width, bundle.shape[0]))
        bundle[:, width : 2 * width] = degree_f.T.astype(jnp.bfloat16)
    for k in backward:

        def finish(slot, carry):
            copy(k, 0, 0, 0, 0).wait()
            return carry

        lax.fori_loop(0, live[0, loop_here ^ order[k]], finish, 0)
        if k >= near_count:
            pltpu.make_async_copy(built[k], mats[k], left.at[k - near_count]).start()
    for k in range(near_count, count):
        pltpu.make_async_copy(built[k], mats[k], left.at[k - near_count]).wait()


def fetched(mats, near_count, stage, done):
    fetches = []
    for k, mat in enumerate(mats[near_count:]):
        half = mat.shape[0] // 2
        for part in range(2):
            rows = pl.ds(part * half, half)
            fetches.append(
                pltpu.make_async_copy(mat.at[rows], stage.at[k, rows], done.at[2 * k + part])
            )
    for fetch in fetches:
        fetch.start()

    def take(j):
        if j < near_count:
            return mats[j]
        for fetch in fetches[2 * (j - near_count) : 2 * (j - near_count) + 2]:
            fetch.wait()
        return stage.at[j - near_count]

    return take


def gather_first_kernel(near_count, count, *refs):
    mats, panels, (out, stage, done) = refs[:count], refs[count:-3], refs[-3:]
    take = fetched(mats, near_count, stage, done)
    total_rows = out.shape[0]
    chunk = min(256, total_rows)
    for j, panel in enumerate(panels):
        mat = take(j)
        for at in range(0, total_rows, chunk):
            rows = slice(at, at + chunk)
            term = jnp.dot(mat[rows, :], panel[...], preferred_element_type=jnp.float32)
            out[rows, :] = term if j == 0 else out[rows, :] + term


def gather_last_kernel(count, *refs):
    mats, panels, (so_far, keep, send) = refs[:count], refs[count : 2 * count], refs[2 * count :]
    half = keep.shape[0]
    chunk = min(256, half)
    for at in range(0, 2 * half, chunk):
        rows = slice(at, at + chunk)
        total = so_far[rows, :]
        for mat, panel in zip(mats, panels):
            total += jnp.dot(mat[rows, :], panel[...], preferred_element_type=jnp.float32)
        if at < half:
            keep[rows, :] = total
        else:
            send[at - half : at - half + chunk, :] = total.astype(jnp.bfloat16)


def add_kernel(kept, arrived, *refs):
    out = refs[-1]
    out[...] = (kept[...].astype(jnp.float32) + arrived[...].astype(jnp.float32)).astype(out.dtype)


def middle_kernel(
    flip, scale, total, term, w_self, w_neigh, bias, *refs
):
    bundles, (output, grad_own, grad_agg, keep, send) = refs[:-5], refs[-5:]
    row_count, width = bundles[0].shape[0], w_neigh.shape[0]
    parts = []
    for j, bundle in enumerate(bundles):
        rows = slice(j * row_count, (j + 1) * row_count)
        there = slice((j ^ flip) * row_count, ((j ^ flip) + 1) * row_count)
        degree_f = bundle[:, width : width + 1].astype(jnp.float32)
        agg = (
            (total[rows, :].astype(jnp.float32) + term[there, :].astype(jnp.float32)) / degree_f
        ).astype(jnp.bfloat16)
        features = bundle[:, :width]
        preact = (
            jnp.dot(
                jnp.concatenate([features, agg], axis=1),
                jnp.concatenate([w_self[...], w_neigh[...]], axis=0),
                preferred_element_type=jnp.float32,
            )
            + bias[...]
        )
        sigmoid_val = jax.nn.sigmoid(preact)
        grad = (
            bundle[:, 2 * width :].astype(jnp.float32)
            * sigmoid_val
            * (1.0 + preact * (1.0 - sigmoid_val))
        ).astype(jnp.bfloat16)
        if j == 0:
            output[...] = (preact * sigmoid_val).astype(jnp.bfloat16)
            grad_own[...] = grad
        back = lax.dot_general(
            grad, w_neigh[...], (((1,), (1,)), ((), ())), preferred_element_type=jnp.float32
        )
        grad_agg[rows, :] = (back / degree_f).astype(jnp.bfloat16)
        grads = [
            lax.dot_general(
                a, grad, (((0,), (0,)), ((), ())), preferred_element_type=jnp.float32
            )
            for a in (features, agg)
        ]
        parts.append((*grads, jnp.sum(grad.astype(jnp.float32), axis=0, keepdims=True)))
    while len(parts) > 1:
        parts = [
            tuple(x + y for x, y in zip(a, b)) for a, b in zip(parts[::2], parts[1::2])
        ]
    by_self, by_neigh, by_bias = (p * scale for p in parts[0])
    first = (lax.axis_index("rep") & 1) == 0
    for out, mine in ((keep, first), (send, jnp.logical_not(first))):
        out[:width, :] = jnp.where(mine, by_self, by_neigh)
        out[width:, :] = jnp.broadcast_to(by_bias, (out.shape[0] - width, by_bias.shape[1]))


def spread(mat, near_t, far_t):
    half = near_t.shape[1]
    total = jnp.dot(near_t, mat[:half, :], preferred_element_type=jnp.float32)
    total += jnp.dot(far_t, mat[half:, :], preferred_element_type=jnp.float32)
    return total.T


def spread_away_kernel(groups, *refs):
    count = sum(groups)
    mats, (near, far), outs = refs[:count], refs[count : count + 2], refs[count + 2 :]
    near_t, far_t = near[...].T, far[...].T
    j = 0
    for size, out in zip(groups, outs):
        rows = out.shape[0] // size
        for k in range(size):
            term = spread(mats[j], near_t, far_t)
            out[k * rows : (k + 1) * rows, :] = term.astype(jnp.bfloat16)
            j += 1


def spread_here_kernel(near_count, count, *refs):
    mats, (near, far, grad_own, w_self) = refs[:count], refs[count : count + 4]
    outs, (stage, done) = refs[count + 4 : -2], refs[-2:]
    take = fetched(mats, near_count, stage, done)
    near_t, far_t = near[...].T, far[...].T
    for j, out in enumerate(outs):
        term = spread(take(j), near_t, far_t)
        if j == count - 1:
            term += lax.dot_general(
                grad_own[...],
                w_self[...],
                (((1,), (1,)), ((), ())),
                preferred_element_type=jnp.float32,
            )
        out[...] = term.astype(out.dtype)


def pair_kernel(last_term, own_term, message, last, own):
    rows = last.shape[0]
    last[...] = (
        last_term[...].astype(jnp.float32) + message[:rows, :].astype(jnp.float32)
    ).astype(last.dtype)
    own[...] = own_term[...] + message[rows:, :].astype(jnp.float32)


def sum_kernel(own, *refs):
    arrived, out = refs[:-1], refs[-1]
    total = own[...]
    for term in arrived:
        total += term[...].astype(jnp.float32)
    out[...] = total.astype(out.dtype)


def finish_kernel(weights, other, grad_self, grad_neigh, grad_bias):
    width = grad_self.shape[0]
    first = (lax.axis_index("rep") & 1) == 0
    mine = weights[:width, :]
    grad_self[...] = jnp.where(first, mine, other[...])
    grad_neigh[...] = jnp.where(first, other[...], mine)
    grad_bias[...] = weights[width : width + 1, :]


def added(kept, arrived, *earlier, dtype=jnp.bfloat16):
    (total,) = call(
        add_kernel,
        [jax.ShapeDtypeStruct(kept.shape, dtype)],
        [VMEM] * 2 + [pl.BlockSpec(memory_space=pl.ANY)] * len(earlier),
        (kept, arrived, *earlier),
    )
    return total


def per_device(
    features, w_self, w_neigh, bias, degree, tiles, dst_block, src_block, live_count, cotangent
):
    loop_count = lax.axis_size("loop")
    rep_count = lax.axis_size("rep")
    row_count, feat_width = features.shape
    hidden = w_self.shape[1]
    tile_size = tiles.shape[-1]
    sub_blocks = row_count // tile_size
    all_rows = row_count * rep_count
    half_rows = all_rows // 2

    far_first = list(range(loop_count - 2, 0, -2))
    panels = {0: features}
    for mask in (*far_first, 1):
        panels[mask] = swap(features, "loop", mask)

    mat_shape = (all_rows, row_count)
    mat_bytes = 2 * all_rows * row_count
    small = loop_count * mat_bytes <= 8 << 20
    late = [m ^ 1 for m in far_first]
    stay = [*far_first, 0]
    far_count = 0 if small else len(stay)
    graph = (dst_block[0, 0], src_block[0, 0], live_count[0], tiles[0, 0])
    sides = (features, degree[None, :], cotangent)

    def place(masks, far, packs):
        near_count = 0 if far else len(masks)
        kind = pltpu.HBM if far else jax.ShapeDtypeStruct
        bundle = [bf16((row_count, 2 * feat_width + hidden))] if packs else []
        operands = graph + sides if packs else graph
        placed = pl.pallas_call(
            functools.partial(place_kernel, near_count, masks, rep_count, sub_blocks, packs),
            out_shape=[kind(mat_shape, jnp.bfloat16)] * len(masks) + bundle,
            in_specs=[HBM] * len(operands),
            out_specs=[HBM if far else VMEM] * len(masks) + [VMEM] * len(bundle),
            scratch_shapes=[pltpu.SMEM(g.shape, jnp.int32) for g in graph[:3]]
            + [
                pltpu.VMEM((len(masks), *mat_shape) if far else (1, 16, 128), jnp.bfloat16),
                pltpu.VMEM((1, row_count), jnp.int32),
                pltpu.SemaphoreType.DMA((6,)),
                pltpu.SemaphoreType.DMA((len(masks),)),
                pltpu.SemaphoreType.DMA((len(masks),)),
            ],
            compiler_params=pltpu.CompilerParams(vmem_limit_bytes=grant(len(masks) * mat_bytes)),
            cost_estimate=pl.CostEstimate(
                flops=0, bytes_accessed=2 * len(masks) * mat_bytes, transcendentals=0
            ),
        )(*map(in_hbm, operands))
        mats = [in_hbm(mat) if far else mat for mat in placed[: len(masks)]]
        return dict(zip(masks, mats)), placed[len(masks) :]

    away_masks = [*late, 1]
    mats, (bundle,) = place(away_masks + stay if small else away_masks, False, True)
    if not small:
        mats |= place(stay, True, False)[0]
    bundles = [bundle] + [swap(bundle, "rep", mask) for mask in range(2, rep_count, 2)]
    arrivals = [*far_first, 1]
    mats[late[0]], *got = after(mats[late[0]], *[panels[m] for m in arrivals])
    panels.update(zip(arrivals, got))
    for mask in far_first:
        panels[mask ^ 1] = swap(panels[mask], "loop", 1)

    early = [1, *stay]
    (running,) = pl.pallas_call(
        functools.partial(gather_first_kernel, len(early) - far_count, len(early)),
        out_shape=[f32((all_rows, feat_width))],
        in_specs=[VMEM] * (len(early) - far_count)
        + [HBM] * far_count
        + [VMEM] * len(early),
        out_specs=[VMEM],
        scratch_shapes=[
            pltpu.VMEM((far_count, *mat_shape) if far_count else (1, 16, 128), jnp.bfloat16),
            pltpu.SemaphoreType.DMA((2 * max(1, far_count),)),
        ],
        compiler_params=pltpu.CompilerParams(vmem_limit_bytes=grant(2 * loop_count * mat_bytes)),
        cost_estimate=pl.CostEstimate(
            flops=2 * len(early) * all_rows * row_count * feat_width,
            bytes_accessed=far_count * mat_bytes,
            transcendentals=0,
        ),
    )(*[mats[m] for m in early], *[panels[m] for m in early])
    keep, send = call(
        functools.partial(gather_last_kernel, len(late)),
        [f32((half_rows, feat_width)), bf16((half_rows, feat_width))],
        [VMEM] * (2 * len(late) + 1),
        [mats[m] for m in late] + [panels[m] for m in late] + [running],
        flops=2 * len(late) * all_rows * row_count * feat_width,
    )
    total = added(keep, swap(send, "rep", 1))
    total, *bundles = after(total, *bundles)
    mask = 2
    while True:
        term = swap(total, "rep", mask)
        if 2 * mask >= rep_count:
            break
        blocks = term.reshape(-1, 2, mask // 2 * row_count, feat_width)[:, ::-1]
        total = (
            total.astype(jnp.float32) + blocks.reshape(half_rows, feat_width).astype(jnp.float32)
        ).astype(jnp.bfloat16)
        mask *= 2

    scale = 1.0 / math.sqrt(row_count * loop_count * rep_count)
    weight_shape = (feat_width + 16, hidden)
    output_shape = (row_count, hidden)
    output, grad_own, grad_agg, keep_w, send_w = call(
        functools.partial(middle_kernel, mask // 2, scale),
        [
            pltpu.VMEM(output_shape, jnp.bfloat16) if small else bf16(output_shape),
            bf16(output_shape),
            bf16((half_rows, feat_width)),
            f32(weight_shape),
            f32(weight_shape),
        ],
        [VMEM] * (5 + len(bundles)),
        (total, term, w_self, w_neigh, bias[None, :], *bundles),
        flops=8 * half_rows * feat_width * hidden,
    )
    grad_far = swap(grad_agg, "rep", 1)
    arrived_w = swap(send_w, "rep", 1)

    away_groups = [1] * (len(far_first) - 1) + [2]
    away = call(
        functools.partial(spread_away_kernel, away_groups),
        [bf16((size * row_count, feat_width)) for size in away_groups],
        [VMEM] * (len(stay) + 2),
        (*[mats[m] for m in away_masks], grad_agg, grad_far),
        flops=2 * len(stay) * all_rows * row_count * feat_width,
    )
    arrived = [swap(message, "loop", 1) for message in away]
    grad_far, *away = after(grad_far, *away)
    kept = pl.pallas_call(
        functools.partial(spread_here_kernel, len(stay) - far_count, len(stay)),
        out_shape=[bf16((row_count, feat_width))] * len(far_first)
        + [f32((row_count, feat_width))],
        in_specs=[VMEM] * (len(stay) - far_count) + [HBM] * far_count + [VMEM] * 4,
        out_specs=[VMEM] * len(stay),
        scratch_shapes=[
            pltpu.VMEM((far_count, *mat_shape) if far_count else (1, 16, 128), jnp.bfloat16),
            pltpu.SemaphoreType.DMA((2 * max(1, far_count),)),
        ],
        compiler_params=pltpu.CompilerParams(vmem_limit_bytes=grant(2 * loop_count * mat_bytes)),
        cost_estimate=pl.CostEstimate(
            flops=2 * len(stay) * all_rows * row_count * feat_width,
            bytes_accessed=far_count * mat_bytes,
            transcendentals=0,
        ),
    )(*[mats[m] for m in stay], grad_agg, grad_far, grad_own, w_self)
    back = [
        swap(added(term, message), "loop", m)
        for m, term, message in zip(far_first[:-1], kept, arrived)
    ]
    last, own = call(
        pair_kernel,
        [bf16((row_count, feat_width)), f32((row_count, feat_width))],
        [VMEM] * 3,
        (*kept[-2:], arrived[-1]),
    )
    back.append(swap(last, "loop", far_first[-1]))
    (grad_input,) = call(
        sum_kernel,
        [bf16((row_count, feat_width))],
        [VMEM] * (1 + len(back)),
        (own, *back),
        flops=4_000_000_000,
    )
    sent_w = added(keep_w, arrived_w)
    mask = loop_count // 2
    while mask:
        arrived_w = swap(sent_w, "loop", mask)
        dtype = jnp.bfloat16 if mask > 1 else jnp.float32
        earlier = [own] if mask == loop_count // 4 else []
        sent_w = added(sent_w, arrived_w, *earlier, dtype=dtype)
        mask //= 2
    other = swap(sent_w[:feat_width], "rep", 1)
    grad_self, grad_neigh, grad_bias = call(
        finish_kernel,
        [f32((feat_width, hidden)), f32((feat_width, hidden)), f32((1, hidden))],
        [VMEM] * 2,
        (sent_w, other),
    )
    return (output, grad_input, grad_self, grad_neigh, grad_bias[0])


def solution(mesh):
    in_specs = (
        P(("loop", "rep"), None),
        P(),
        P(),
        P(),
        P(("loop", "rep")),
        P("loop", "rep", None, None, None, None),
        P("loop", "rep", None, None),
        P("loop", "rep", None, None),
        P("loop", "rep", None),
        P(("loop", "rep"), None),
    )
    out_specs = (P(("loop", "rep"), None), P(("loop", "rep"), None), P(), P(), P())
    return jax.shard_map(
        per_device, mesh=mesh, in_specs=in_specs, out_specs=out_specs, check_vma=False
    )
```

time: 300 us -> 51.7 us (0.17)
  waiting for transfers between devices: 134 us -> 14.3 us
  matrix products: 47.4 us -> 0 us
  blocking collectives: 45.1 us -> 0 us
  local copies, waits for them, and re-layouts: 16.3 us -> 0.69 us
  between operations: 14.3 us -> 0.84 us
  other arithmetic: 8.05 us -> 0 us
  Pallas kernels: 0 us -> 7.6 us
  starting transfers between devices: 32.7 us -> 27.8 us
    psum x1 -> x0, waiting for transfers between devices: 68.7 us -> none  [per_device(): lax.psum((jnp.einsum('nf,nh->fh', features, grad_pre, preferred_element_t...]
    dot_general x38 -> x0, matrix products: 47.4 us -> none  [the longest x8 11.4 us: spread_term(): jnp.einsum('tij,tif->tjf', tile_part, chosen, preferred_element_type=jnp....]
    psum x1 -> x0, blocking collectives: 39.4 us -> none  [per_device(): lax.psum((jnp.einsum('nf,nh->fh', features, grad_pre, preferred_element_t...]
    ppermute x14 -> x22, waiting for transfers between devices: 46.7 us -> 14.3 us  [swap(): lax.ppermute(block, axis, [(i, i ^ mask) for i in range(lax.axis_size(axi...]
    reduce_scatter x1 -> x0, waiting for transfers between devices: 18.2 us -> none  [per_device(): lax.psum_scatter(running.reshape(row_blocks * tile_size, feat_width), 're...]
    gather x16 -> x0, local copies, waits for them, and re-layouts: 11.2 us -> none  [the longest x8 6.01 us: gather_term(): jnp.take(panel.reshape(sub_blocks, tile_size, feat_width), pick_entry(src...]
    pallas_call x0 -> x16, Pallas kernels: none -> 7.6 us  [the longest x13 3.28 us: call(): pl.pallas_call(kernel, out_shape=list(out_shape), in_specs=in_specs, out_...]
    and x16 -> x0, other arithmetic: 6.36 us -> none  [the longest x8 5.58 us: spread_term(): chosen = jnp.take(grad_whole, pick_entry(dst_all, source), axis=0)]
  transfers between devices with their start and end apart: 16 -> 22, of which waited for: 10 -> 9; matrix products, arithmetic and copies ran while one was open for 10% -> 1% of each run, Pallas kernels for 0% -> 12%
where the time goes in v1:
time: 51.7 us; the launch traced here: 51.3 us
  starting transfers between devices  27.8 us (54%)
  waiting for transfers between devices  14.3 us (28%)
  Pallas kernels  7.6 us (15%)
  between operations  0.84 us (2%)
  local copies, waits for them, and re-layouts  0.69 us (1%)
    ppermute x22, starting transfers between devices, swap(): lax.ppermute(block, axis, [(i, i ^ mask) for i in range(lax.axis_size(axi...  27.8 us
    ppermute x22, waiting for transfers between devices, swap(): lax.ppermute(block, axis, [(i, i ^ mask) for i in range(lax.axis_size(axi...  14.3 us
    pallas_call x13, Pallas kernels, call(): pl.pallas_call(kernel, out_shape=list(out_shape), in_specs=in_specs, out_...  3.28 us
    pallas_call x1, Pallas kernels, place(): pl.pallas_call(functools.partial(place_kernel, near_count, masks, rep_cou...  2.88 us
  transfers between devices with their start and end apart: 22, of which 9 were waited for; matrix products, arithmetic and copies ran while one was open for 1% of the time, Pallas kernels for 12%

profile of v1, /device:TPU:0, one launch (start us, length us, event | category | flops | bytes accessed | tf_op | source)
XLA Modules:
  0.0 51.3 jit_solution(7320871144914060155)
XLA Ops:
  0.6 5.1 %collective-permute-start = (bf16[256,128]{1,0:T(8,128)(2,1)}, bf16[256,128]{1,0:T(8,128)(2,1)S(1)}, u32[]{:S(2)}, u32[]{:S(2)}) collective-permute-start(bf16[256,128]{1,0:T(8,128)(2,1)} %refs_9_.1), channel_id=1, source_target_pairs={{0,24},{4,28},{8,16},{12,20},{16,8},{20,12},{24,0},{28,4},{1,25},{... | collective-permute-start | bytes 196616 | tf_op jit(solution)/shard_map/ppermute | solution.py:16
  5.8 0.6 %collective-permute-start.2 = (bf16[256,128]{1,0:T(8,128)(2,1)}, bf16[256,128]{1,0:T(8,128)(2,1)S(1)}, u32[]{:S(2)}, u32[]{:S(2)}) collective-permute-start(bf16[256,128]{1,0:T(8,128)(2,1)} %refs_9_.1), channel_id=1, source_target_pairs={{0,8},{4,12},{8,0},{12,4},{16,24},{20,28},{24,16},{28,20},{1,9},{5... | collective-permute-start | bytes 196616 | tf_op jit(solution)/shard_map/ppermute | solution.py:16
  6.4 1.7 %collective-permute-start.3 = (bf16[256,128]{1,0:T(8,128)(2,1)}, bf16[256,128]{1,0:T(8,128)(2,1)S(1)}, u32[]{:S(2)}, u32[]{:S(2)}) collective-permute-start(bf16[256,128]{1,0:T(8,128)(2,1)} %refs_9_.1), channel_id=1, source_target_pairs={{0,4},{4,0},{8,12},{12,8},{16,20},{20,16},{24,28},{28,24},{1,5},{5... | collective-permute-start | bytes 196616 | tf_op jit(solution)/shard_map/ppermute | solution.py:16
  8.1 2.9 %shard_map.137 = (bf16[1024,256]{1,0:T(8,128)(2,1)S(1)}, bf16[1024,256]{1,0:T(8,128)(2,1)S(1)}, bf16[1024,256]{1,0:T(8,128)(2,1)S(1)}, bf16[1024,256]{1,0:T(8,12...) custom-call(s32[8,16]{1,0:T(8,128)} %bitcast.9, ...), custom_call_target="tpu_custom_call" | custom-call | bytes 8388608 | tf_op jit(solution)/shard_map/pallas_call | solution.py:328
  11.0 0.0 copy-start.1
  11.0 0.0 copy-start.2
  11.0 0.0 copy-start.3
  11.0 1.5 %collective-permute-start.8 = (bf16[256,512]{1,0:T(8,128)(2,1)S(1)}, bf16[256,512]{1,0:T(8,128)(2,1)S(1)}, u32[]{:S(2)}, u32[]{:S(2)}) collective-permute-start(bf16[256,512]{1,0:T(8,128)(2,1)S(1)} %get-tuple-element.59.refs_0_), channel_id=1, source_target_pairs={{0,2},{1,3},{2,0},{3,1},{4,6},{5,7},{6,4},{7,5},{8,10},{9,11},{10,... | collective-permute-start | bytes 786440 | tf_op jit(solution)/shard_map/ppermute | solution.py:16
  12.5 0.0 collective-permute-done.refs_6_
  12.5 0.0 collective-permute-done.1.refs_7_
  12.5 0.0 collective-permute-done.2.refs_8_
  12.5 0.9 %collective-permute-start.4 = (bf16[256,128]{1,0:T(8,128)(2,1)S(1)}, bf16[256,128]{1,0:T(8,128)(2,1)S(1)}, u32[]{:S(2)}, u32[]{:S(2)}) collective-permute-start(bf16[256,128]{1,0:T(8,128)(2,1)S(1)} %collective-permute-done.refs_6_), channel_id=1, source_target_pairs={{0,4},{4,0},{8,12},{12,8},{16,20},{20,16},{24,28},{28,24},{1,5},{5... | collective-permute-start | bytes 196616 | tf_op jit(solution)/shard_map/ppermute | solution.py:16
  13.4 1.2 %collective-permute-start.5 = (bf16[256,128]{1,0:T(8,128)(2,1)S(1)}, bf16[256,128]{1,0:T(8,128)(2,1)S(1)}, u32[]{:S(2)}, u32[]{:S(2)}) collective-permute-start(bf16[256,128]{1,0:T(8,128)(2,1)S(1)} %collective-permute-done.1.refs_7_), channel_id=1, source_target_pairs={{0,4},{4,0},{8,12},{12,8},{16,20},{20,16},{24,28},{28,24},{1,5},{5... | collective-permute-start | bytes 196616 | tf_op jit(solution)/shard_map/ppermute | solution.py:16
  14.6 0.8 %collective-permute-start.6 = (bf16[256,128]{1,0:T(8,128)(2,1)S(1)}, bf16[256,128]{1,0:T(8,128)(2,1)S(1)}, u32[]{:S(2)}, u32[]{:S(2)}) collective-permute-start(bf16[256,128]{1,0:T(8,128)(2,1)S(1)} %collective-permute-done.2.refs_8_), channel_id=1, source_target_pairs={{0,4},{4,0},{8,12},{12,8},{16,20},{20,16},{24,28},{28,24},{1,5},{5... | collective-permute-start | bytes 196616 | tf_op jit(solution)/shard_map/ppermute | solution.py:16
  15.4 0.9 %shard_map.138.refs_6_ = f32[1024,128]{1,0:T(8,128)S(1)} custom-call(bf16[1024,256]{1,0:T(8,128)(2,1)S(1)} %get-tuple-element.49.refs_0_.refs_3_, bf16[1024,256]{1,0:T(8,128)(2,1)S(1)} %get-tuple-element.50.refs_1_.refs_0_, bf16[1024,256]{1,0:T(8,128)(2,1)S(1)} %get-tuple-element.51.refs_2_.refs_1_, bf16[1024,256]{1,0:T(8,128)(2,1)S(1)} %get-tuple-element.52.refs_3_.refs_2_, ...), custom_call_target="tpu_custom_call" | custom-call | flops 335544320 | tf_op jit(solution)/shard_map/pallas_call | solution.py:361
  16.3 1.1 %collective-permute-done.4.refs_3_ = bf16[256,128]{1,0:T(8,128)(2,1)S(1)} collective-permute-done((bf16[256,128]{1,0:T(8,128)(2,1)S(1)}, bf16[256,128]{1,0:T(8,128)(2,1)S(1)}, u32[]{:S(2)}, u32[]{:S(2)}) %collective-permute-start.4) | collective-permute-done | bytes 65568 | tf_op jit(solution)/shard_map/ppermute | solution.py:16
  17.4 0.7 %collective-permute-done.5.refs_4_ = bf16[256,128]{1,0:T(8,128)(2,1)S(1)} collective-permute-done((bf16[256,128]{1,0:T(8,128)(2,1)S(1)}, bf16[256,128]{1,0:T(8,128)(2,1)S(1)}, u32[]{:S(2)}, u32[]{:S(2)}) %collective-permute-start.5) | collective-permute-done | bytes 65568 | tf_op jit(solution)/shard_map/ppermute | solution.py:16
  18.1 0.8 %collective-permute-done.6.refs_5_ = bf16[256,128]{1,0:T(8,128)(2,1)S(1)} collective-permute-done((bf16[256,128]{1,0:T(8,128)(2,1)S(1)}, bf16[256,128]{1,0:T(8,128)(2,1)S(1)}, u32[]{:S(2)}, u32[]{:S(2)}) %collective-permute-start.6) | collective-permute-done | bytes 65568 | tf_op jit(solution)/shard_map/ppermute | solution.py:16
  18.8 0.6 %shard_map.139 = (f32[512,128]{1,0:T(8,128)S(1)}, bf16[512,128]{1,0:T(8,128)(2,1)S(1)}) custom-call(bf16[1024,256]{1,0:T(8,128)(2,1)S(1)} %get-tuple-element.43.refs_0_, bf16[1024,256]{1,0:T(8,128)(2,1)S(1)} %get-tuple-element.44.refs_1_, bf16[1024,256]{1,0:T(8,128)(2,1)S(1)} %get-tuple-element.45.refs_2_, ...), custom_call_target="tpu_custom_call" | custom-call | flops 201326592 | bytes 2686976 | tf_op jit(solution)/shard_map/pallas_call | solution.py:25
  19.4 0.1 collective-permute-start.7
  19.5 1.3 %collective-permute-done.7.arrived = bf16[512,128]{1,0:T(8,128)(2,1)S(1)} collective-permute-done((bf16[512,128]{1,0:T(8,128)(2,1)S(1)}, bf16[512,128]{1,0:T(8,128)(2,1)S(1)}, u32[]{:S(2)}, u32[]{:S(2)}) %collective-permute-start.7) | collective-permute-done | bytes 131104 | tf_op jit(solution)/shard_map/ppermute | solution.py:16
  20.8 0.0 collective-permute-done.8.refs_1_
  20.9 1.5 %collective-permute-start.9 = (bf16[512,128]{1,0:T(8,128)(2,1)S(1)}, bf16[512,128]{1,0:T(8,128)(2,1)S(1)}, u32[]{:S(2)}, u32[]{:S(2)}) collective-permute-start(bf16[512,128]{1,0:T(8,128)(2,1)S(1)} %shard_map.140.total), channel_id=1, source_target_pairs={{0,2},{1,3},{2,0},{3,1},{4,6},{5,7},{6,4},{7,5},{8,10},{9,11},{10,... | collective-permute-start | bytes 393224 | tf_op jit(solution)/shard_map/ppermute | solution.py:16
  22.3 4.1 %collective-permute-done.9.term = bf16[512,128]{1,0:T(8,128)(2,1)S(1)} collective-permute-done((bf16[512,128]{1,0:T(8,128)(2,1)S(1)}, bf16[512,128]{1,0:T(8,128)(2,1)S(1)}, u32[]{:S(2)}, u32[]{:S(2)}) %collective-permute-start.9) | collective-permute-done | bytes 131104 | tf_op jit(solution)/shard_map/ppermute | solution.py:16
  26.5 0.6 %shard_map.141 = (bf16[256,256]{1,0:T(8,128)(2,1)S(1)}, bf16[256,256]{1,0:T(8,128)(2,1)S(1)}, bf16[512,128]{1,0:T(8,128)(2,1)S(1)}, f32[144,256]{1,0:T(8,128)S(1)}, f32[144,256]{1,0:T(8,128)S(1)}) custom-call(bf16[512,128]{1,0:T(8,128)(2,1)S(1)} %shard_map.140.total, bf16[512,128]{1,0:T(8,128)(2,1)S(1)} %collective-permute-done.9.term, ...), custom_call_target="tpu_custom_call" | custom-call | flops 134217728 | bytes 1606656 | tf_op jit(solution)/shard_map/pallas_call | solution.py:25
  27.1 0.1 collective-permute-start.17
  27.2 0.5 collective-permute-start.10
  27.7 0.9 %collective-permute-done.17.arrived = f32[144,256]{1,0:T(8,128)S(1)} collective-permute-done((f32[144,256]{1,0:T(8,128)S(1)}, f32[144,256]{1,0:T(8,128)S(1)}, u32[]{:S(2)}, u32[]{:S(2)}) %collective-permute-start.17) | collective-permute-done | bytes 147488 | tf_op jit(solution)/shard_map/ppermute | solution.py:16
  28.6 2.3 %collective-permute-start.18 = (bf16[144,256]{1,0:T(8,128)(2,1)S(1)}, bf16[144,256]{1,0:T(8,128)(2,1)S(1)}, u32[]{:S(2)}, u32[]{:S(2)}) collective-permute-start(bf16[144,256]{1,0:T(8,128)(2,1)S(1)} %shard_map.148.kept), channel_id=1, source_target_pairs={{0,16},{4,20},{8,24},{12,28},{16,0},{20,4},{24,8},{28,12},{1,17},{... | collective-permute-start | bytes 221192 | tf_op jit(solution)/shard_map/ppermute | solution.py:16
  30.8 0.0 collective-permute-done.10.refs_5_
  30.8 0.5 %shard_map.142 = (bf16[256,128]{1,0:T(8,128)(2,1)S(1)}, bf16[256,128]{1,0:T(8,128)(2,1)S(1)}, bf16[512,128]{1,0:T(8,128)(2,1)S(1)}) custom-call(bf16[1024,256]{1,0:T(8,128)(2,1)S(1)} %get-tuple-element.43.refs_0_, bf16[1024,256]{1,0:T(8,128)(2,1)S(1)} %get-tuple-element.44.refs_1_, bf16[1024,256]{1,0:T(8,128)(2,1)S(1)} %get-tuple-element.45.refs_2_, ...), custom_call_target="tpu_custom_call" | custom-call | flops 268435456 | bytes 2621440 | tf_op jit(solution)/shard_map/pallas_call | solution.py:25
  31.4 0.8 %collective-permute-start.11 = (bf16[512,128]{1,0:T(8,128)(2,1)S(1)}, bf16[512,128]{1,0:T(8,128)(2,1)S(1)}, u32[]{:S(2)}, u32[]{:S(2)}) collective-permute-start(bf16[512,128]{1,0:T(8,128)(2,1)S(1)} %get-tuple-element.65), channel_id=1, source_target_pairs={{0,4},{4,0},{8,12},{12,8},{16,20},{20,16},{24,28},{28,24},{1,5},{5... | collective-permute-start | bytes 393224 | tf_op jit(solution)/shard_map/ppermute | solution.py:16
  32.1 1.8 %collective-permute-done.18.arrived = bf16[144,256]{1,0:T(8,128)(2,1)S(1)} collective-permute-done((bf16[144,256]{1,0:T(8,128)(2,1)S(1)}, bf16[144,256]{1,0:T(8,128)(2,1)S(1)}, u32[]{:S(2)}, u32[]{:S(2)}) %collective-permute-start.18) | collective-permute-done | bytes 73760 | tf_op jit(solution)/shard_map/ppermute | solution.py:16
  33.9 2.2 %collective-permute-start.19 = (bf16[144,256]{1,0:T(8,128)(2,1)S(1)}, bf16[144,256]{1,0:T(8,128)(2,1)S(1)}, u32[]{:S(2)}, u32[]{:S(2)}) collective-permute-start(bf16[144,256]{1,0:T(8,128)(2,1)S(1)} %shard_map.149.kept), channel_id=1, source_target_pairs={{0,8},{4,12},{8,0},{12,4},{16,24},{20,28},{24,16},{28,20},{1,9},{5... | collective-permute-start | bytes 221192 | tf_op jit(solution)/shard_map/ppermute | solution.py:16
  36.1 0.7 %collective-permute-start.14 = (bf16[256,128]{1,0:T(8,128)(2,1)S(1)}, bf16[256,128]{1,0:T(8,128)(2,1)S(1)}, u32[]{:S(2)}, u32[]{:S(2)}) collective-permute-start(bf16[256,128]{1,0:T(8,128)(2,1)S(1)} %get-tuple-element.64), channel_id=1, source_target_pairs={{0,4},{4,0},{8,12},{12,8},{16,20},{20,16},{24,28},{28,24},{1,5},{5... | collective-permute-start | bytes 196616 | tf_op jit(solution)/shard_map/ppermute | solution.py:16
  36.8 1.3 %collective-permute-start.12 = (bf16[256,128]{1,0:T(8,128)(2,1)S(1)}, bf16[256,128]{1,0:T(8,128)(2,1)S(1)}, u32[]{:S(2)}, u32[]{:S(2)}) collective-permute-start(bf16[256,128]{1,0:T(8,128)(2,1)S(1)} %get-tuple-element.63), channel_id=1, source_target_pairs={{0,4},{4,0},{8,12},{12,8},{16,20},{20,16},{24,28},{28,24},{1,5},{5... | collective-permute-start | bytes 196616 | tf_op jit(solution)/shard_map/ppermute | solution.py:16
  38.1 0.6 %shard_map.143 = (bf16[256,128]{1,0:T(8,128)(2,1)S(1)}, bf16[256,128]{1,0:T(8,128)(2,1)S(1)}, bf16[256,128]{1,0:T(8,128)(2,1)S(1)}, f32[256,128]{1,0:T(8,128)S(1)}) custom-call(bf16[1024,256]{1,0:T(8,128)(2,1)S(1)} %get-tuple-element.50.refs_1_.refs_0_, bf16[1024,256]{1,0:T(8,128)(2,1)S(1)} %get-tuple-element.51.refs_2_.refs_1_, ...), custom_call_target="tpu_custom_call" | custom-call | flops 268435456 | tf_op jit(solution)/shard_map/pallas_call | solution.py:428
  38.8 0.0 collective-permute-done.19.arrived
  38.8 2.1 %collective-permute-start.20 = (bf16[144,256]{1,0:T(8,128)(2,1)S(1)}, bf16[144,256]{1,0:T(8,128)(2,1)S(1)}, u32[]{:S(2)}, u32[]{:S(2)}) collective-permute-start(bf16[144,256]{1,0:T(8,128)(2,1)S(1)} %shard_map.150.kept), channel_id=1, source_target_pairs={{0,4},{4,0},{8,12},{12,8},{16,20},{20,16},{24,28},{28,24},{1,5},{5... | collective-permute-start | bytes 221192 | tf_op jit(solution)/shard_map/ppermute | solution.py:16
  40.9 2.8 %collective-permute-start.15 = (bf16[256,128]{1,0:T(8,128)(2,1)S(1)}, bf16[256,128]{1,0:T(8,128)(2,1)S(1)}, u32[]{:S(2)}, u32[]{:S(2)}) collective-permute-start(bf16[256,128]{1,0:T(8,128)(2,1)S(1)} %shard_map.146), channel_id=1, source_target_pairs={{0,16},{4,20},{8,24},{12,28},{16,0},{20,4},{24,8},{28,12},{1,17},{... | collective-permute-start | bytes 196616 | tf_op jit(solution)/shard_map/ppermute | solution.py:16
  43.7 0.5 collective-permute-start.13
  44.2 1.3 %collective-permute-start.16 = (bf16[256,128]{1,0:T(8,128)(2,1)S(1)}, bf16[256,128]{1,0:T(8,128)(2,1)S(1)}, u32[]{:S(2)}, u32[]{:S(2)}) collective-permute-start(bf16[256,128]{1,0:T(8,128)(2,1)S(1)} %get-tuple-element.73), channel_id=1, source_target_pairs={{0,8},{4,12},{8,0},{12,4},{16,24},{20,28},{24,16},{28,20},{1,9},{5... | collective-permute-start | bytes 196616 | tf_op jit(solution)/shard_map/ppermute | solution.py:16
  45.5 0.7 %copy.15 = bf16[256,256]{1,0:T(8,128)(2,1)} copy(bf16[256,256]{1,0:T(8,128)(2,1)S(1)} %get-tuple-element.79) | data formatting | bytes 262144
  46.2 0.1 collective-permute-start.21
  46.3 1.5 %collective-permute-done.15.refs_1_ = bf16[256,128]{1,0:T(8,128)(2,1)S(1)} collective-permute-done((bf16[256,128]{1,0:T(8,128)(2,1)S(1)}, bf16[256,128]{1,0:T(8,128)(2,1)S(1)}, u32[]{:S(2)}, u32[]{:S(2)}) %collective-permute-start.15) | collective-permute-done | bytes 65568 | tf_op jit(solution)/shard_map/ppermute | solution.py:16
  47.7 2.1 %collective-permute-done.13.refs_0_ = bf16[256,128]{1,0:T(8,128)(2,1)S(1)} collective-permute-done((bf16[256,128]{1,0:T(8,128)(2,1)S(1)}, bf16[256,128]{1,0:T(8,128)(2,1)S(1)}, u32[]{:S(2)}, u32[]{:S(2)}) %collective-permute-start.13) | collective-permute-done | bytes 65568 | tf_op jit(solution)/shard_map/ppermute | solution.py:16
  49.9 0.7 %shard_map.147 = bf16[256,128]{1,0:T(8,128)(2,1)} custom-call(f32[256,128]{1,0:T(8,128)S(1)} %get-tuple-element.70.own.refs_0_, bf16[256,128]{1,0:T(8,128)(2,1)S(1)} %collective-permute-done.13.refs_0_, bf16[256,128]{1,0:T(8,128)(2,1)S(1)} %collective-permute-done.15.refs_1_, bf16[256,128]{1,0:T(8,128)(2,1)S(1)} %collective-permute-done.16.refs_2_), custom_call_target="tpu_custom_call" | custom-call | flops 4000000000 | bytes 393216 | tf_op jit(solution)/shard_map/pallas_call | solution.py:25
  50.5 0.7 %shard_map.152 = (f32[128,256]{1,0:T(8,128)}, f32[128,256]{1,0:T(8,128)}, f32[1,256]{1,0:T(1,128)}) custom-call(f32[144,256]{1,0:T(8,128)S(1)} %shard_map.151.weights, f32[128,256]{1,0:T(8,128)S(1)} %collective-permute-done.21.other), custom_call_target="tpu_custom_call" | custom-call | bytes 541696 | tf_op jit(solution)/shard_map/pallas_call | solution.py:25
  (22 shorter events, 0.2 us)
Async XLA Ops:
  0.6 14.8 %copy-start = (bf16[256,128]{1,0:T(8,128)(2,1)S(1)}, bf16[256,128]{1,0:T(8,128)(2,1)}, u32[]{:S(2)}) copy-start(bf16[256,128]{1,0:T(8,128)(2,1)} %refs_9_.1) | copy-start | bytes 196612
  0.6 11.8 %collective-permute-start = (bf16[256,128]{1,0:T(8,128)(2,1)}, bf16[256,128]{1,0:T(8,128)(2,1)S(1)}, u32[]{:S(2)}, u32[]{:S(2)}) collective-permute-start(bf16[256,128]{1,0:T(8,128)(2,1)} %refs_9_.1), channel_id=1, source_target_pairs={{0,24},{4,28},{8,16},{12,20},{16,8},{20,12},{24,0},{28,4},{1,25},{... | collective-permute-start | bytes 196616 | tf_op jit(solution)/shard_map/ppermute | solution.py:16
  5.8 6.7 %collective-permute-start.1 = (bf16[256,128]{1,0:T(8,128)(2,1)}, bf16[256,128]{1,0:T(8,128)(2,1)S(1)}, u32[]{:S(2)}, u32[]{:S(2)}) collective-permute-start(bf16[256,128]{1,0:T(8,128)(2,1)} %refs_9_.1), channel_id=1, source_target_pairs={{0,16},{4,20},{8,24},{12,28},{16,0},{20,4},{24,8},{28,12},{1,17},{... | collective-permute-start | bytes 196616 | tf_op jit(solution)/shard_map/ppermute | solution.py:16
  5.8 6.7 %collective-permute-start.2 = (bf16[256,128]{1,0:T(8,128)(2,1)}, bf16[256,128]{1,0:T(8,128)(2,1)S(1)}, u32[]{:S(2)}, u32[]{:S(2)}) collective-permute-start(bf16[256,128]{1,0:T(8,128)(2,1)} %refs_9_.1), channel_id=1, source_target_pairs={{0,8},{4,12},{8,0},{12,4},{16,24},{20,28},{24,16},{28,20},{1,9},{5... | collective-permute-start | bytes 196616 | tf_op jit(solution)/shard_map/ppermute | solution.py:16
  6.4 6.1 %collective-permute-start.3 = (bf16[256,128]{1,0:T(8,128)(2,1)}, bf16[256,128]{1,0:T(8,128)(2,1)S(1)}, u32[]{:S(2)}, u32[]{:S(2)}) collective-permute-start(bf16[256,128]{1,0:T(8,128)(2,1)} %refs_9_.1), channel_id=1, source_target_pairs={{0,4},{4,0},{8,12},{12,8},{16,20},{20,16},{24,28},{28,24},{1,5},{5... | collective-permute-start | bytes 196616 | tf_op jit(solution)/shard_map/ppermute | solution.py:16
  11.0 15.5 %copy-start.1 = (bf16[128,256]{1,0:T(8,128)(2,1)S(1)}, bf16[128,256]{1,0:T(8,128)(2,1)}, u32[]{:S(2)}) copy-start(bf16[128,256]{1,0:T(8,128)(2,1)} %refs_7_.1) | copy-start | bytes 196612
  11.0 15.5 %copy-start.2 = (bf16[128,256]{1,0:T(8,128)(2,1)S(1)}, bf16[128,256]{1,0:T(8,128)(2,1)}, u32[]{:S(2)}) copy-start(bf16[128,256]{1,0:T(8,128)(2,1)} %w_neigh.1) | copy-start | bytes 196612
  11.0 15.5 %copy-start.3 = (f32[256]{0:T(256)S(1)}, f32[256]{0:T(256)}, u32[]{:S(2)}) copy-start(f32[256]{0:T(256)} %param.13) | copy-start | bytes 3076
  11.0 9.9 %collective-permute-start.8 = (bf16[256,512]{1,0:T(8,128)(2,1)S(1)}, bf16[256,512]{1,0:T(8,128)(2,1)S(1)}, u32[]{:S(2)}, u32[]{:S(2)}) collective-permute-start(bf16[256,512]{1,0:T(8,128)(2,1)S(1)} %get-tuple-element.59.refs_0_), channel_id=1, source_target_pairs={{0,2},{1,3},{2,0},{3,1},{4,6},{5,7},{6,4},{7,5},{8,10},{9,11},{10,... | collective-permute-start | bytes 786440 | tf_op jit(solution)/shard_map/ppermute | solution.py:16
  12.5 4.9 %collective-permute-start.4 = (bf16[256,128]{1,0:T(8,128)(2,1)S(1)}, bf16[256,128]{1,0:T(8,128)(2,1)S(1)}, u32[]{:S(2)}, u32[]{:S(2)}) collective-permute-start(bf16[256,128]{1,0:T(8,128)(2,1)S(1)} %collective-permute-done.refs_6_), channel_id=1, source_target_pairs={{0,4},{4,0},{8,12},{12,8},{16,20},{20,16},{24,28},{28,24},{1,5},{5... | collective-permute-start | bytes 196616 | tf_op jit(solution)/shard_map/ppermute | solution.py:16
  13.4 4.7 %collective-permute-start.5 = (bf16[256,128]{1,0:T(8,128)(2,1)S(1)}, bf16[256,128]{1,0:T(8,128)(2,1)S(1)}, u32[]{:S(2)}, u32[]{:S(2)}) collective-permute-start(bf16[256,128]{1,0:T(8,128)(2,1)S(1)} %collective-permute-done.1.refs_7_), channel_id=1, source_target_pairs={{0,4},{4,0},{8,12},{12,8},{16,20},{20,16},{24,28},{28,24},{1,5},{5... | collective-permute-start | bytes 196616 | tf_op jit(solution)/shard_map/ppermute | solution.py:16
  14.6 4.3 %collective-permute-start.6 = (bf16[256,128]{1,0:T(8,128)(2,1)S(1)}, bf16[256,128]{1,0:T(8,128)(2,1)S(1)}, u32[]{:S(2)}, u32[]{:S(2)}) collective-permute-start(bf16[256,128]{1,0:T(8,128)(2,1)S(1)} %collective-permute-done.2.refs_8_), channel_id=1, source_target_pairs={{0,4},{4,0},{8,12},{12,8},{16,20},{20,16},{24,28},{28,24},{1,5},{5... | collective-permute-start | bytes 196616 | tf_op jit(solution)/shard_map/ppermute | solution.py:16
  19.4 1.4 %collective-permute-start.7 = (bf16[512,128]{1,0:T(8,128)(2,1)S(1)}, bf16[512,128]{1,0:T(8,128)(2,1)S(1)}, u32[]{:S(2)}, u32[]{:S(2)}) collective-permute-start(bf16[512,128]{1,0:T(8,128)(2,1)S(1)} %get-tuple-element.56), channel_id=1, source_target_pairs={{0,1},{1,0},{2,3},{3,2},{4,5},{5,4},{6,7},{7,6},{8,9},{9,8},{10,11... | collective-permute-start | bytes 393224 | tf_op jit(solution)/shard_map/ppermute | solution.py:16
  20.9 5.6 %collective-permute-start.9 = (bf16[512,128]{1,0:T(8,128)(2,1)S(1)}, bf16[512,128]{1,0:T(8,128)(2,1)S(1)}, u32[]{:S(2)}, u32[]{:S(2)}) collective-permute-start(bf16[512,128]{1,0:T(8,128)(2,1)S(1)} %shard_map.140.total), channel_id=1, source_target_pairs={{0,2},{1,3},{2,0},{3,1},{4,6},{5,7},{6,4},{7,5},{8,10},{9,11},{10,... | collective-permute-start | bytes 393224 | tf_op jit(solution)/shard_map/ppermute | solution.py:16
  27.1 1.4 %collective-permute-start.17 = (f32[144,256]{1,0:T(8,128)S(1)}, f32[144,256]{1,0:T(8,128)S(1)}, u32[]{:S(2)}, u32[]{:S(2)}) collective-permute-start(f32[144,256]{1,0:T(8,128)S(1)} %get-tuple-element.75), channel_id=1, source_target_pairs={{0,1},{1,0},{2,3},{3,2},{4,5},{5,4},{6,7},{7,6},{8,9},{9,8},{10,11... | collective-permute-start | bytes 442376 | tf_op jit(solution)/shard_map/ppermute | solution.py:16
  27.2 3.6 %collective-permute-start.10 = (bf16[512,128]{1,0:T(8,128)(2,1)S(1)}, bf16[512,128]{1,0:T(8,128)(2,1)S(1)}, u32[]{:S(2)}, u32[]{:S(2)}) collective-permute-start(bf16[512,128]{1,0:T(8,128)(2,1)S(1)} %get-tuple-element.62.refs_4_), channel_id=1, source_target_pairs={{0,1},{1,0},{2,3},{3,2},{4,5},{5,4},{6,7},{7,6},{8,9},{9,8},{10,11... | collective-permute-start | bytes 393224 | tf_op jit(solution)/shard_map/ppermute | solution.py:16
  28.6 5.3 %collective-permute-start.18 = (bf16[144,256]{1,0:T(8,128)(2,1)S(1)}, bf16[144,256]{1,0:T(8,128)(2,1)S(1)}, u32[]{:S(2)}, u32[]{:S(2)}) collective-permute-start(bf16[144,256]{1,0:T(8,128)(2,1)S(1)} %shard_map.148.kept), channel_id=1, source_target_pairs={{0,16},{4,20},{8,24},{12,28},{16,0},{20,4},{24,8},{28,12},{1,17},{... | collective-permute-start | bytes 221192 | tf_op jit(solution)/shard_map/ppermute | solution.py:16
  31.4 7.4 %collective-permute-start.11 = (bf16[512,128]{1,0:T(8,128)(2,1)S(1)}, bf16[512,128]{1,0:T(8,128)(2,1)S(1)}, u32[]{:S(2)}, u32[]{:S(2)}) collective-permute-start(bf16[512,128]{1,0:T(8,128)(2,1)S(1)} %get-tuple-element.65), channel_id=1, source_target_pairs={{0,4},{4,0},{8,12},{12,8},{16,20},{20,16},{24,28},{28,24},{1,5},{5... | collective-permute-start | bytes 393224 | tf_op jit(solution)/shard_map/ppermute | solution.py:16
  33.9 4.9 %collective-permute-start.19 = (bf16[144,256]{1,0:T(8,128)(2,1)S(1)}, bf16[144,256]{1,0:T(8,128)(2,1)S(1)}, u32[]{:S(2)}, u32[]{:S(2)}) collective-permute-start(bf16[144,256]{1,0:T(8,128)(2,1)S(1)} %shard_map.149.kept), channel_id=1, source_target_pairs={{0,8},{4,12},{8,0},{12,4},{16,24},{20,28},{24,16},{28,20},{1,9},{5... | collective-permute-start | bytes 221192 | tf_op jit(solution)/shard_map/ppermute | solution.py:16
  36.1 4.8 %collective-permute-start.14 = (bf16[256,128]{1,0:T(8,128)(2,1)S(1)}, bf16[256,128]{1,0:T(8,128)(2,1)S(1)}, u32[]{:S(2)}, u32[]{:S(2)}) collective-permute-start(bf16[256,128]{1,0:T(8,128)(2,1)S(1)} %get-tuple-element.64), channel_id=1, source_target_pairs={{0,4},{4,0},{8,12},{12,8},{16,20},{20,16},{24,28},{28,24},{1,5},{5... | collective-permute-start | bytes 196616 | tf_op jit(solution)/shard_map/ppermute | solution.py:16
  36.8 6.9 %collective-permute-start.12 = (bf16[256,128]{1,0:T(8,128)(2,1)S(1)}, bf16[256,128]{1,0:T(8,128)(2,1)S(1)}, u32[]{:S(2)}, u32[]{:S(2)}) collective-permute-start(bf16[256,128]{1,0:T(8,128)(2,1)S(1)} %get-tuple-element.63), channel_id=1, source_target_pairs={{0,4},{4,0},{8,12},{12,8},{16,20},{20,16},{24,28},{28,24},{1,5},{5... | collective-permute-start | bytes 196616 | tf_op jit(solution)/shard_map/ppermute | solution.py:16
  38.8 7.3 %collective-permute-start.20 = (bf16[144,256]{1,0:T(8,128)(2,1)S(1)}, bf16[144,256]{1,0:T(8,128)(2,1)S(1)}, u32[]{:S(2)}, u32[]{:S(2)}) collective-permute-start(bf16[144,256]{1,0:T(8,128)(2,1)S(1)} %shard_map.150.kept), channel_id=1, source_target_pairs={{0,4},{4,0},{8,12},{12,8},{16,20},{20,16},{24,28},{28,24},{1,5},{5... | collective-permute-start | bytes 221192 | tf_op jit(solution)/shard_map/ppermute | solution.py:16
  40.9 6.8 %collective-permute-start.15 = (bf16[256,128]{1,0:T(8,128)(2,1)S(1)}, bf16[256,128]{1,0:T(8,128)(2,1)S(1)}, u32[]{:S(2)}, u32[]{:S(2)}) collective-permute-start(bf16[256,128]{1,0:T(8,128)(2,1)S(1)} %shard_map.146), channel_id=1, source_target_pairs={{0,16},{4,20},{8,24},{12,28},{16,0},{20,4},{24,8},{28,12},{1,17},{... | collective-permute-start | bytes 196616 | tf_op jit(solution)/shard_map/ppermute | solution.py:16
  43.7 6.1 %collective-permute-start.13 = (bf16[256,128]{1,0:T(8,128)(2,1)S(1)}, bf16[256,128]{1,0:T(8,128)(2,1)S(1)}, u32[]{:S(2)}, u32[]{:S(2)}) collective-permute-start(bf16[256,128]{1,0:T(8,128)(2,1)S(1)} %shard_map.145), channel_id=1, source_target_pairs={{0,24},{4,28},{8,16},{12,20},{16,8},{20,12},{24,0},{28,4},{1,25},{... | collective-permute-start | bytes 196616 | tf_op jit(solution)/shard_map/ppermute | solution.py:16
  44.2 5.7 %collective-permute-start.16 = (bf16[256,128]{1,0:T(8,128)(2,1)S(1)}, bf16[256,128]{1,0:T(8,128)(2,1)S(1)}, u32[]{:S(2)}, u32[]{:S(2)}) collective-permute-start(bf16[256,128]{1,0:T(8,128)(2,1)S(1)} %get-tuple-element.73), channel_id=1, source_target_pairs={{0,8},{4,12},{8,0},{12,4},{16,24},{20,28},{24,16},{28,20},{1,9},{5... | collective-permute-start | bytes 196616 | tf_op jit(solution)/shard_map/ppermute | solution.py:16
  46.2 4.4 %collective-permute-start.21 = (f32[128,256]{1,0:T(8,128)S(1)}, f32[128,256]{1,0:T(8,128)S(1)}, u32[]{:S(2)}, u32[]{:S(2)}) collective-permute-start(f32[128,256]{1,0:T(8,128)S(1)} %slice.4), channel_id=1, source_target_pairs={{0,1},{1,0},{2,3},{3,2},{4,5},{5,4},{6,7},{7,6},{8,9},{9,8},{10,11... | collective-permute-start | bytes 393224 | tf_op jit(solution)/shard_map/ppermute | solution.py:16

commit v2 on v1

--- a/solution.py
+++ b/solution.py
@@ -59,6 +59,7 @@
     dst, src, live, stage, degree, read, done, left = refs
     tile_size = tiles.shape[-1]
     loop_here, rep_here = lax.axis_index("loop"), lax.axis_index("rep")
+    sub_bits = sub_blocks.bit_length() - 1
     moves = [(dst_far, dst), (src_far, src), (live_far, live)]
     if packs:
         width = sides[0].shape[1]
@@ -89,9 +90,9 @@
 
         def put(slot, carry):
             block, column = dst[source, slot], src[source, slot]
-            away = lax.div(block, sub_blocks) ^ rep_here
+            away = lax.shift_right_logical(block, sub_bits) ^ rep_here
             panel = (away & 1) * (rep_count // 2) + lax.shift_right_logical(away, 1)
-            row = panel * sub_blocks + lax.rem(block, sub_blocks)
+            row = panel * sub_blocks + (block & (sub_blocks - 1))
             copy(k, source, slot, row, column).start()
             return carry
 
@@ -259,17 +260,17 @@
         out[...] = term.astype(out.dtype)
 
 
-def pair_kernel(last_term, own_term, message, last, own):
-    rows = last.shape[0]
-    last[...] = (
-        last_term[...].astype(jnp.float32) + message[:rows, :].astype(jnp.float32)
-    ).astype(last.dtype)
-    own[...] = own_term[...] + message[rows:, :].astype(jnp.float32)
-
-
-def sum_kernel(own, *refs):
+def pair_kernel(part, term, message, *refs):
+    out = refs[-1]
+    rows = out.shape[0]
+    piece = message[part * rows : (part + 1) * rows, :]
+    out[...] = (term[...].astype(jnp.float32) + piece.astype(jnp.float32)).astype(out.dtype)
+
+
+def sum_kernel(part, own, message, *refs):
     arrived, out = refs[:-1], refs[-1]
-    total = own[...]
+    rows = out.shape[0]
+    total = own[...] + message[part * rows : (part + 1) * rows, :].astype(jnp.float32)
     for term in arrived:
         total += term[...].astype(jnp.float32)
     out[...] = total.astype(out.dtype)
@@ -282,6 +283,21 @@
     grad_self[...] = jnp.where(first, mine, other[...])
     grad_neigh[...] = jnp.where(first, other[...], mine)
     grad_bias[...] = weights[width : width + 1, :]
+
+
+def token_kernel(*refs):
+    refs[-1][...] = jnp.zeros(refs[-1].shape, jnp.float32)
+
+
+def token(values, flops):
+    (out,) = call(
+        token_kernel,
+        [f32((8, 128))],
+        [pl.BlockSpec(memory_space=pl.ANY)] * len(values),
+        values,
+        flops=flops,
+    )
+    return out
 
 
 def added(kept, arrived, *earlier, dtype=jnp.bfloat16):
@@ -413,7 +429,7 @@
         flops=8 * half_rows * feat_width * hidden,
     )
     grad_far = swap(grad_agg, "rep", 1)
-    arrived_w = swap(send_w, "rep", 1)
+    sent_w = added(keep_w, swap(send_w, "rep", 1))
 
     away_groups = [1] * (len(far_first) - 1) + [2]
     away = call(
@@ -442,30 +458,29 @@
             transcendentals=0,
         ),
     )(*[mats[m] for m in stay], grad_agg, grad_far, grad_own, w_self)
-    back = [
-        swap(added(term, message), "loop", m)
-        for m, term, message in zip(far_first[:-1], kept, arrived)
-    ]
-    last, own = call(
-        pair_kernel,
-        [bf16((row_count, feat_width)), f32((row_count, feat_width))],
-        [VMEM] * 3,
-        (*kept[-2:], arrived[-1]),
-    )
-    back.append(swap(last, "loop", far_first[-1]))
+    pieces = [(message, k) for message, size in zip(arrived, away_groups) for k in range(size)]
+    pairs = []
+    for term, (message, part) in zip(kept[:-1], pieces):
+        pairs += call(
+            functools.partial(pair_kernel, part),
+            [bf16((row_count, feat_width))],
+            [VMEM] * 2 + [pl.BlockSpec(memory_space=pl.ANY)] * len(pairs[-1:]),
+            (term, message, *pairs[-1:]),
+        )
+    back = [swap(pair, "loop", m) for m, pair in zip(far_first, pairs)]
+    message, part = pieces[-1]
     (grad_input,) = call(
-        sum_kernel,
+        functools.partial(sum_kernel, part),
         [bf16((row_count, feat_width))],
-        [VMEM] * (1 + len(back)),
-        (own, *back),
-        flops=4_000_000_000,
-    )
-    sent_w = added(keep_w, arrived_w)
+        [VMEM] * (2 + len(back)),
+        (kept[-1], message, *back),
+        flops=0,
+    )
     mask = loop_count // 2
     while mask:
         arrived_w = swap(sent_w, "loop", mask)
         dtype = jnp.bfloat16 if mask > 1 else jnp.float32
-        earlier = [own] if mask == loop_count // 4 else []
+        earlier = {loop_count // 2: [], 2: pairs[2:3], 1: [token(back, 12_000_000_000)]}.get(mask, [])
         sent_w = added(sent_w, arrived_w, *earlier, dtype=dtype)
         mask //= 2
     other = swap(sent_w[:feat_width], "rep", 1)

time: 51.7 us -> 49.5 us (0.957)
  starting transfers between devices: 27.8 us -> 25 us
  waiting for transfers between devices: 14.3 us -> 15 us
    ppermute x22, starting transfers between devices: 27.8 us -> 25 us  [swap(): lax.ppermute(block, axis, [(i, i ^ mask) for i in range(lax.axis_size(axi...]
    ppermute x22, waiting for transfers between devices: 14.3 us -> 15 us  [swap(): lax.ppermute(block, axis, [(i, i ^ mask) for i in range(lax.axis_size(axi...]
    pallas_call x13 -> x14, Pallas kernels: 3.28 us -> 3.28 us  [call(): pl.pallas_call(kernel, out_shape=list(out_shape), in_specs=in_specs, out_...]
  transfers between devices with their start and end apart: 22 -> 22, of which waited for: 9 -> 8; matrix products, arithmetic and copies ran while one was open for 1% -> 1% of each run, Pallas kernels for 12% -> 13%
where the time goes in v2:
time: 49.5 us; the launch traced here: 49.3 us
  starting transfers between devices  25 us (51%)
  waiting for transfers between devices  15 us (30%)
  Pallas kernels  7.76 us (16%)
  between operations  0.84 us (2%)
  local copies, waits for them, and re-layouts  0.69 us (1%)
    ppermute x22, starting transfers between devices, swap(): lax.ppermute(block, axis, [(i, i ^ mask) for i in range(lax.axis_size(axi...  25 us
    ppermute x22, waiting for transfers between devices, swap(): lax.ppermute(block, axis, [(i, i ^ mask) for i in range(lax.axis_size(axi...  15 us
    pallas_call x14, Pallas kernels, call(): pl.pallas_call(kernel, out_shape=list(out_shape), in_specs=in_specs, out_...  3.28 us
    pallas_call x1, Pallas kernels, place(): pl.pallas_call(functools.partial(place_kernel, near_count, masks, rep_cou...  3.03 us
  transfers between devices with their start and end apart: 22, of which 8 were waited for; matrix products, arithmetic and copies ran while one was open for 1% of the time, Pallas kernels for 13%

profile of v2, /device:TPU:0, one launch (start us, length us, event | category | flops | bytes accessed | tf_op | source)
XLA Modules:
  0.0 49.3 jit_solution(10383445894746073497)
XLA Ops:
  0.6 5.1 %collective-permute-start = (bf16[256,128]{1,0:T(8,128)(2,1)}, bf16[256,128]{1,0:T(8,128)(2,1)S(1)}, u32[]{:S(2)}, u32[]{:S(2)}) collective-permute-start(bf16[256,128]{1,0:T(8,128)(2,1)} %refs_9_.1), channel_id=1, source_target_pairs={{0,24},{4,28},{8,16},{12,20},{16,8},{20,12},{24,0},{28,4},{1,25},{... | collective-permute-start | bytes 196616 | tf_op jit(solution)/shard_map/ppermute | solution.py:16
  5.8 0.6 %collective-permute-start.2 = (bf16[256,128]{1,0:T(8,128)(2,1)}, bf16[256,128]{1,0:T(8,128)(2,1)S(1)}, u32[]{:S(2)}, u32[]{:S(2)}) collective-permute-start(bf16[256,128]{1,0:T(8,128)(2,1)} %refs_9_.1), channel_id=1, source_target_pairs={{0,8},{4,12},{8,0},{12,4},{16,24},{20,28},{24,16},{28,20},{1,9},{5... | collective-permute-start | bytes 196616 | tf_op jit(solution)/shard_map/ppermute | solution.py:16
  6.4 1.7 %collective-permute-start.3 = (bf16[256,128]{1,0:T(8,128)(2,1)}, bf16[256,128]{1,0:T(8,128)(2,1)S(1)}, u32[]{:S(2)}, u32[]{:S(2)}) collective-permute-start(bf16[256,128]{1,0:T(8,128)(2,1)} %refs_9_.1), channel_id=1, source_target_pairs={{0,4},{4,0},{8,12},{12,8},{16,20},{20,16},{24,28},{28,24},{1,5},{5... | collective-permute-start | bytes 196616 | tf_op jit(solution)/shard_map/ppermute | solution.py:16
  8.1 3.0 %shard_map.137 = (bf16[1024,256]{1,0:T(8,128)(2,1)S(1)}, bf16[1024,256]{1,0:T(8,128)(2,1)S(1)}, bf16[1024,256]{1,0:T(8,128)(2,1)S(1)}, bf16[1024,256]{1,0:T(8,12...) custom-call(s32[8,16]{1,0:T(8,128)} %bitcast.9, ...), custom_call_target="tpu_custom_call" | custom-call | bytes 8388608 | tf_op jit(solution)/shard_map/pallas_call | solution.py:344
  11.1 0.0 copy-start.1
  11.1 0.0 copy-start.2
  11.1 0.0 copy-start.3
  11.1 1.1 %collective-permute-start.8 = (bf16[256,512]{1,0:T(8,128)(2,1)S(1)}, bf16[256,512]{1,0:T(8,128)(2,1)S(1)}, u32[]{:S(2)}, u32[]{:S(2)}) collective-permute-start(bf16[256,512]{1,0:T(8,128)(2,1)S(1)} %get-tuple-element.57.refs_0_), channel_id=1, source_target_pairs={{0,2},{1,3},{2,0},{3,1},{4,6},{5,7},{6,4},{7,5},{8,10},{9,11},{10,... | collective-permute-start | bytes 786440 | tf_op jit(solution)/shard_map/ppermute | solution.py:16
  12.2 0.0 collective-permute-done.refs_6_
  12.2 0.0 collective-permute-done.1.refs_7_
  12.2 0.0 collective-permute-done.2.refs_8_
  12.2 0.0 collective-permute-done.3.refs_5_
  12.2 0.9 %collective-permute-start.4 = (bf16[256,128]{1,0:T(8,128)(2,1)S(1)}, bf16[256,128]{1,0:T(8,128)(2,1)S(1)}, u32[]{:S(2)}, u32[]{:S(2)}) collective-permute-start(bf16[256,128]{1,0:T(8,128)(2,1)S(1)} %collective-permute-done.refs_6_), channel_id=1, source_target_pairs={{0,4},{4,0},{8,12},{12,8},{16,20},{20,16},{24,28},{28,24},{1,5},{5... | collective-permute-start | bytes 196616 | tf_op jit(solution)/shard_map/ppermute | solution.py:16
  13.1 1.2 %collective-permute-start.5 = (bf16[256,128]{1,0:T(8,128)(2,1)S(1)}, bf16[256,128]{1,0:T(8,128)(2,1)S(1)}, u32[]{:S(2)}, u32[]{:S(2)}) collective-permute-start(bf16[256,128]{1,0:T(8,128)(2,1)S(1)} %collective-permute-done.1.refs_7_), channel_id=1, source_target_pairs={{0,4},{4,0},{8,12},{12,8},{16,20},{20,16},{24,28},{28,24},{1,5},{5... | collective-permute-start | bytes 196616 | tf_op jit(solution)/shard_map/ppermute | solution.py:16
  14.3 0.8 %collective-permute-start.6 = (bf16[256,128]{1,0:T(8,128)(2,1)S(1)}, bf16[256,128]{1,0:T(8,128)(2,1)S(1)}, u32[]{:S(2)}, u32[]{:S(2)}) collective-permute-start(bf16[256,128]{1,0:T(8,128)(2,1)S(1)} %collective-permute-done.2.refs_8_), channel_id=1, source_target_pairs={{0,4},{4,0},{8,12},{12,8},{16,20},{20,16},{24,28},{28,24},{1,5},{5... | collective-permute-start | bytes 196616 | tf_op jit(solution)/shard_map/ppermute | solution.py:16
  15.1 0.8 %shard_map.138.refs_6_ = f32[1024,128]{1,0:T(8,128)S(1)} custom-call(bf16[1024,256]{1,0:T(8,128)(2,1)S(1)} %get-tuple-element.47.refs_0_.refs_3_, bf16[1024,256]{1,0:T(8,128)(2,1)S(1)} %get-tuple-element.48.refs_1_.refs_0_, bf16[1024,256]{1,0:T(8,128)(2,1)S(1)} %get-tuple-element.49.refs_2_.refs_1_, bf16[1024,256]{1,0:T(8,128)(2,1)S(1)} %get-tuple-element.50.refs_3_.refs_2_, ...), custom_call_target="tpu_custom_call" | custom-call | flops 335544320 | tf_op jit(solution)/shard_map/pallas_call | solution.py:377
  16.0 1.2 %collective-permute-done.4.refs_3_ = bf16[256,128]{1,0:T(8,128)(2,1)S(1)} collective-permute-done((bf16[256,128]{1,0:T(8,128)(2,1)S(1)}, bf16[256,128]{1,0:T(8,128)(2,1)S(1)}, u32[]{:S(2)}, u32[]{:S(2)}) %collective-permute-start.4) | collective-permute-done | bytes 65568 | tf_op jit(solution)/shard_map/ppermute | solution.py:16
  17.2 0.8 %collective-permute-done.5.refs_4_ = bf16[256,128]{1,0:T(8,128)(2,1)S(1)} collective-permute-done((bf16[256,128]{1,0:T(8,128)(2,1)S(1)}, bf16[256,128]{1,0:T(8,128)(2,1)S(1)}, u32[]{:S(2)}, u32[]{:S(2)}) %collective-permute-start.5) | collective-permute-done | bytes 65568 | tf_op jit(solution)/shard_map/ppermute | solution.py:16
  18.1 0.7 %collective-permute-done.6.refs_5_ = bf16[256,128]{1,0:T(8,128)(2,1)S(1)} collective-permute-done((bf16[256,128]{1,0:T(8,128)(2,1)S(1)}, bf16[256,128]{1,0:T(8,128)(2,1)S(1)}, u32[]{:S(2)}, u32[]{:S(2)}) %collective-permute-start.6) | collective-permute-done | bytes 65568 | tf_op jit(solution)/shard_map/ppermute | solution.py:16
  18.8 0.6 %shard_map.139 = (f32[512,128]{1,0:T(8,128)S(1)}, bf16[512,128]{1,0:T(8,128)(2,1)S(1)}) custom-call(bf16[1024,256]{1,0:T(8,128)(2,1)S(1)} %get-tuple-element.41.refs_0_, bf16[1024,256]{1,0:T(8,128)(2,1)S(1)} %get-tuple-element.42.refs_1_, bf16[1024,256]{1,0:T(8,128)(2,1)S(1)} %get-tuple-element.43.refs_2_, ...), custom_call_target="tpu_custom_call" | custom-call | flops 201326592 | bytes 2686976 | tf_op jit(solution)/shard_map/pallas_call | solution.py:25
  19.3 0.1 collective-permute-start.7
  19.4 1.3 %collective-permute-done.7.arrived = bf16[512,128]{1,0:T(8,128)(2,1)S(1)} collective-permute-done((bf16[512,128]{1,0:T(8,128)(2,1)S(1)}, bf16[512,128]{1,0:T(8,128)(2,1)S(1)}, u32[]{:S(2)}, u32[]{:S(2)}) %collective-permute-start.7) | collective-permute-done | bytes 131104 | tf_op jit(solution)/shard_map/ppermute | solution.py:16
  20.8 0.0 collective-permute-done.8.refs_1_
  20.8 1.6 %collective-permute-start.9 = (bf16[512,128]{1,0:T(8,128)(2,1)S(1)}, bf16[512,128]{1,0:T(8,128)(2,1)S(1)}, u32[]{:S(2)}, u32[]{:S(2)}) collective-permute-start(bf16[512,128]{1,0:T(8,128)(2,1)S(1)} %shard_map.140.total), channel_id=1, source_target_pairs={{0,2},{1,3},{2,0},{3,1},{4,6},{5,7},{6,4},{7,5},{8,10},{9,11},{10,... | collective-permute-start | bytes 393224 | tf_op jit(solution)/shard_map/ppermute | solution.py:16
  22.3 4.1 %collective-permute-done.9.term = bf16[512,128]{1,0:T(8,128)(2,1)S(1)} collective-permute-done((bf16[512,128]{1,0:T(8,128)(2,1)S(1)}, bf16[512,128]{1,0:T(8,128)(2,1)S(1)}, u32[]{:S(2)}, u32[]{:S(2)}) %collective-permute-start.9) | collective-permute-done | bytes 131104 | tf_op jit(solution)/shard_map/ppermute | solution.py:16
  26.4 0.6 %shard_map.141 = (bf16[256,256]{1,0:T(8,128)(2,1)S(1)}, bf16[256,256]{1,0:T(8,128)(2,1)S(1)}, bf16[512,128]{1,0:T(8,128)(2,1)S(1)}, f32[144,256]{1,0:T(8,128)S(1)}, f32[144,256]{1,0:T(8,128)S(1)}) custom-call(bf16[512,128]{1,0:T(8,128)(2,1)S(1)} %shard_map.140.total, bf16[512,128]{1,0:T(8,128)(2,1)S(1)} %collective-permute-done.9.term, ...), custom_call_target="tpu_custom_call" | custom-call | flops 134217728 | bytes 1606656 | tf_op jit(solution)/shard_map/pallas_call | solution.py:25
  27.0 0.1 collective-permute-start.10
  27.1 0.5 %collective-permute-start.17 = (f32[144,256]{1,0:T(8,128)S(1)}, f32[144,256]{1,0:T(8,128)S(1)}, u32[]{:S(2)}, u32[]{:S(2)}) collective-permute-start(f32[144,256]{1,0:T(8,128)S(1)} %get-tuple-element.71), channel_id=1, source_target_pairs={{0,1},{1,0},{2,3},{3,2},{4,5},{5,4},{6,7},{7,6},{8,9},{9,8},{10,11... | collective-permute-start | bytes 442376 | tf_op jit(solution)/shard_map/ppermute | solution.py:16
  27.6 0.8 %collective-permute-done.10.refs_5_ = bf16[512,128]{1,0:T(8,128)(2,1)S(1)} collective-permute-done((bf16[512,128]{1,0:T(8,128)(2,1)S(1)}, bf16[512,128]{1,0:T(8,128)(2,1)S(1)}, u32[]{:S(2)}, u32[]{:S(2)}) %collective-permute-start.10) | collective-permute-done | bytes 131104 | tf_op jit(solution)/shard_map/ppermute | solution.py:16
  28.5 0.5 %shard_map.142 = (bf16[256,128]{1,0:T(8,128)(2,1)S(1)}, bf16[256,128]{1,0:T(8,128)(2,1)S(1)}, bf16[512,128]{1,0:T(8,128)(2,1)S(1)}) custom-call(bf16[1024,256]{1,0:T(8,128)(2,1)S(1)} %get-tuple-element.41.refs_0_, bf16[1024,256]{1,0:T(8,128)(2,1)S(1)} %get-tuple-element.42.refs_1_, bf16[1024,256]{1,0:T(8,128)(2,1)S(1)} %get-tuple-element.43.refs_2_, ...), custom_call_target="tpu_custom_call" | custom-call | flops 268435456 | bytes 2621440 | tf_op jit(solution)/shard_map/pallas_call | solution.py:25
  29.0 1.0 %collective-permute-start.11 = (bf16[512,128]{1,0:T(8,128)(2,1)S(1)}, bf16[512,128]{1,0:T(8,128)(2,1)S(1)}, u32[]{:S(2)}, u32[]{:S(2)}) collective-permute-start(bf16[512,128]{1,0:T(8,128)(2,1)S(1)} %get-tuple-element.63), channel_id=1, source_target_pairs={{0,4},{4,0},{8,12},{12,8},{16,20},{20,16},{24,28},{28,24},{1,5},{5... | collective-permute-start | bytes 393224 | tf_op jit(solution)/shard_map/ppermute | solution.py:16
  30.1 2.3 %collective-permute-start.18 = (bf16[144,256]{1,0:T(8,128)(2,1)S(1)}, bf16[144,256]{1,0:T(8,128)(2,1)S(1)}, u32[]{:S(2)}, u32[]{:S(2)}) collective-permute-start(bf16[144,256]{1,0:T(8,128)(2,1)S(1)} %shard_map.148.kept), channel_id=1, source_target_pairs={{0,16},{4,20},{8,24},{12,28},{16,0},{20,4},{24,8},{28,12},{1,17},{... | collective-permute-start | bytes 221192 | tf_op jit(solution)/shard_map/ppermute | solution.py:16
  32.4 1.3 %collective-permute-start.12 = (bf16[256,128]{1,0:T(8,128)(2,1)S(1)}, bf16[256,128]{1,0:T(8,128)(2,1)S(1)}, u32[]{:S(2)}, u32[]{:S(2)}) collective-permute-start(bf16[256,128]{1,0:T(8,128)(2,1)S(1)} %get-tuple-element.61), channel_id=1, source_target_pairs={{0,4},{4,0},{8,12},{12,8},{16,20},{20,16},{24,28},{28,24},{1,5},{5... | collective-permute-start | bytes 196616 | tf_op jit(solution)/shard_map/ppermute | solution.py:16
  33.7 0.7 %collective-permute-start.14 = (bf16[256,128]{1,0:T(8,128)(2,1)S(1)}, bf16[256,128]{1,0:T(8,128)(2,1)S(1)}, u32[]{:S(2)}, u32[]{:S(2)}) collective-permute-start(bf16[256,128]{1,0:T(8,128)(2,1)S(1)} %get-tuple-element.62), channel_id=1, source_target_pairs={{0,4},{4,0},{8,12},{12,8},{16,20},{20,16},{24,28},{28,24},{1,5},{5... | collective-permute-start | bytes 196616 | tf_op jit(solution)/shard_map/ppermute | solution.py:16
  34.4 2.6 %collective-permute-done.18.arrived = bf16[144,256]{1,0:T(8,128)(2,1)S(1)} collective-permute-done((bf16[144,256]{1,0:T(8,128)(2,1)S(1)}, bf16[144,256]{1,0:T(8,128)(2,1)S(1)}, u32[]{:S(2)}, u32[]{:S(2)}) %collective-permute-start.18) | collective-permute-done | bytes 73760 | tf_op jit(solution)/shard_map/ppermute | solution.py:16
  37.0 0.1 collective-permute-start.19
  37.1 0.6 %shard_map.143 = (bf16[256,128]{1,0:T(8,128)(2,1)S(1)}, bf16[256,128]{1,0:T(8,128)(2,1)S(1)}, bf16[256,128]{1,0:T(8,128)(2,1)S(1)}, f32[256,128]{1,0:T(8,128)S(1)}) custom-call(bf16[1024,256]{1,0:T(8,128)(2,1)S(1)} %get-tuple-element.48.refs_1_.refs_0_, bf16[1024,256]{1,0:T(8,128)(2,1)S(1)} %get-tuple-element.49.refs_2_.refs_1_, ...), custom_call_target="tpu_custom_call" | custom-call | flops 268435456 | tf_op jit(solution)/shard_map/pallas_call | solution.py:444
  37.7 3.1 %collective-permute-start.13 = (bf16[256,128]{1,0:T(8,128)(2,1)S(1)}, bf16[256,128]{1,0:T(8,128)(2,1)S(1)}, u32[]{:S(2)}, u32[]{:S(2)}) collective-permute-start(bf16[256,128]{1,0:T(8,128)(2,1)S(1)} %shard_map.144.refs_0_), channel_id=1, source_target_pairs={{0,24},{4,28},{8,16},{12,20},{16,8},{20,12},{24,0},{28,4},{1,25},{... | collective-permute-start | bytes 196616 | tf_op jit(solution)/shard_map/ppermute | solution.py:16
  40.8 0.0 collective-permute-done.14.message
  40.9 0.5 collective-permute-start.15
  41.4 1.0 %collective-permute-start.16 = (bf16[256,128]{1,0:T(8,128)(2,1)S(1)}, bf16[256,128]{1,0:T(8,128)(2,1)S(1)}, u32[]{:S(2)}, u32[]{:S(2)}) collective-permute-start(bf16[256,128]{1,0:T(8,128)(2,1)S(1)} %shard_map.146.refs_0_), channel_id=1, source_target_pairs={{0,8},{4,12},{8,0},{12,4},{16,24},{20,28},{24,16},{28,20},{1,9},{5... | collective-permute-start | bytes 196616 | tf_op jit(solution)/shard_map/ppermute | solution.py:16
  42.4 1.4 %collective-permute-start.20 = (bf16[144,256]{1,0:T(8,128)(2,1)S(1)}, bf16[144,256]{1,0:T(8,128)(2,1)S(1)}, u32[]{:S(2)}, u32[]{:S(2)}) collective-permute-start(bf16[144,256]{1,0:T(8,128)(2,1)S(1)} %shard_map.150.kept), channel_id=1, source_target_pairs={{0,4},{4,0},{8,12},{12,8},{16,20},{20,16},{24,28},{28,24},{1,5},{5... | collective-permute-start | bytes 221192 | tf_op jit(solution)/shard_map/ppermute | solution.py:16
  43.7 3.4 %collective-permute-done.15.refs_1_ = bf16[256,128]{1,0:T(8,128)(2,1)S(1)} collective-permute-done((bf16[256,128]{1,0:T(8,128)(2,1)S(1)}, bf16[256,128]{1,0:T(8,128)(2,1)S(1)}, u32[]{:S(2)}, u32[]{:S(2)}) %collective-permute-start.15) | collective-permute-done | bytes 65568 | tf_op jit(solution)/shard_map/ppermute | solution.py:16
  47.2 0.1 collective-permute-start.21
  47.3 0.7 %copy.15 = bf16[256,256]{1,0:T(8,128)(2,1)} copy(bf16[256,256]{1,0:T(8,128)(2,1)S(1)} %get-tuple-element.75) | data formatting | bytes 262144
  47.9 0.7 %shard_map.147 = bf16[256,128]{1,0:T(8,128)(2,1)} custom-call(f32[256,128]{1,0:T(8,128)S(1)} %get-tuple-element.66.own, bf16[512,128]{1,0:T(8,128)(2,1)S(1)} %collective-permute-done.11.message, bf16[256,128]{1,0:T(8,128)(2,1)S(1)} %collective-permute-done.13.refs_0_, bf16[256,128]{1,0:T(8,128)(2,1)S(1)} %collective-permute-done.15.refs_1_, ...), custom_call_target="tpu_custom_call" | custom-call | bytes 524288 | tf_op jit(solution)/shard_map/pallas_call | solution.py:25
  48.6 0.0 collective-permute-done.21.other
  48.6 0.7 %shard_map.153 = (f32[128,256]{1,0:T(8,128)}, f32[128,256]{1,0:T(8,128)}, f32[1,256]{1,0:T(1,128)}) custom-call(f32[144,256]{1,0:T(8,128)S(1)} %shard_map.152.weights, f32[128,256]{1,0:T(8,128)S(1)} %collective-permute-done.21.other), custom_call_target="tpu_custom_call" | custom-call | bytes 541696 | tf_op jit(solution)/shard_map/pallas_call | solution.py:25
  (23 shorter events, 0.2 us)
Async XLA Ops:
  0.6 14.5 %copy-start = (bf16[256,128]{1,0:T(8,128)(2,1)S(1)}, bf16[256,128]{1,0:T(8,128)(2,1)}, u32[]{:S(2)}) copy-start(bf16[256,128]{1,0:T(8,128)(2,1)} %refs_9_.1) | copy-start | bytes 196612
  0.6 11.6 %collective-permute-start = (bf16[256,128]{1,0:T(8,128)(2,1)}, bf16[256,128]{1,0:T(8,128)(2,1)S(1)}, u32[]{:S(2)}, u32[]{:S(2)}) collective-permute-start(bf16[256,128]{1,0:T(8,128)(2,1)} %refs_9_.1), channel_id=1, source_target_pairs={{0,24},{4,28},{8,16},{12,20},{16,8},{20,12},{24,0},{28,4},{1,25},{... | collective-permute-start | bytes 196616 | tf_op jit(solution)/shard_map/ppermute | solution.py:16
  5.8 6.5 %collective-permute-start.1 = (bf16[256,128]{1,0:T(8,128)(2,1)}, bf16[256,128]{1,0:T(8,128)(2,1)S(1)}, u32[]{:S(2)}, u32[]{:S(2)}) collective-permute-start(bf16[256,128]{1,0:T(8,128)(2,1)} %refs_9_.1), channel_id=1, source_target_pairs={{0,16},{4,20},{8,24},{12,28},{16,0},{20,4},{24,8},{28,12},{1,17},{... | collective-permute-start | bytes 196616 | tf_op jit(solution)/shard_map/ppermute | solution.py:16
  5.8 6.5 %collective-permute-start.2 = (bf16[256,128]{1,0:T(8,128)(2,1)}, bf16[256,128]{1,0:T(8,128)(2,1)S(1)}, u32[]{:S(2)}, u32[]{:S(2)}) collective-permute-start(bf16[256,128]{1,0:T(8,128)(2,1)} %refs_9_.1), channel_id=1, source_target_pairs={{0,8},{4,12},{8,0},{12,4},{16,24},{20,28},{24,16},{28,20},{1,9},{5... | collective-permute-start | bytes 196616 | tf_op jit(solution)/shard_map/ppermute | solution.py:16
  6.4 5.8 %collective-permute-start.3 = (bf16[256,128]{1,0:T(8,128)(2,1)}, bf16[256,128]{1,0:T(8,128)(2,1)S(1)}, u32[]{:S(2)}, u32[]{:S(2)}) collective-permute-start(bf16[256,128]{1,0:T(8,128)(2,1)} %refs_9_.1), channel_id=1, source_target_pairs={{0,4},{4,0},{8,12},{12,8},{16,20},{20,16},{24,28},{28,24},{1,5},{5... | collective-permute-start | bytes 196616 | tf_op jit(solution)/shard_map/ppermute | solution.py:16
  11.1 15.3 %copy-start.1 = (bf16[128,256]{1,0:T(8,128)(2,1)S(1)}, bf16[128,256]{1,0:T(8,128)(2,1)}, u32[]{:S(2)}) copy-start(bf16[128,256]{1,0:T(8,128)(2,1)} %refs_7_.1) | copy-start | bytes 196612
  11.1 15.3 %copy-start.2 = (bf16[128,256]{1,0:T(8,128)(2,1)S(1)}, bf16[128,256]{1,0:T(8,128)(2,1)}, u32[]{:S(2)}) copy-start(bf16[128,256]{1,0:T(8,128)(2,1)} %w_neigh.1) | copy-start | bytes 196612
  11.1 15.3 %copy-start.3 = (f32[256]{0:T(256)S(1)}, f32[256]{0:T(256)}, u32[]{:S(2)}) copy-start(f32[256]{0:T(256)} %param.13) | copy-start | bytes 3076
  11.1 9.6 %collective-permute-start.8 = (bf16[256,512]{1,0:T(8,128)(2,1)S(1)}, bf16[256,512]{1,0:T(8,128)(2,1)S(1)}, u32[]{:S(2)}, u32[]{:S(2)}) collective-permute-start(bf16[256,512]{1,0:T(8,128)(2,1)S(1)} %get-tuple-element.57.refs_0_), channel_id=1, source_target_pairs={{0,2},{1,3},{2,0},{3,1},{4,6},{5,7},{6,4},{7,5},{8,10},{9,11},{10,... | collective-permute-start | bytes 786440 | tf_op jit(solution)/shard_map/ppermute | solution.py:16
  12.2 5.0 %collective-permute-start.4 = (bf16[256,128]{1,0:T(8,128)(2,1)S(1)}, bf16[256,128]{1,0:T(8,128)(2,1)S(1)}, u32[]{:S(2)}, u32[]{:S(2)}) collective-permute-start(bf16[256,128]{1,0:T(8,128)(2,1)S(1)} %collective-permute-done.refs_6_), channel_id=1, source_target_pairs={{0,4},{4,0},{8,12},{12,8},{16,20},{20,16},{24,28},{28,24},{1,5},{5... | collective-permute-start | bytes 196616 | tf_op jit(solution)/shard_map/ppermute | solution.py:16
  13.1 5.0 %collective-permute-start.5 = (bf16[256,128]{1,0:T(8,128)(2,1)S(1)}, bf16[256,128]{1,0:T(8,128)(2,1)S(1)}, u32[]{:S(2)}, u32[]{:S(2)}) collective-permute-start(bf16[256,128]{1,0:T(8,128)(2,1)S(1)} %collective-permute-done.1.refs_7_), channel_id=1, source_target_pairs={{0,4},{4,0},{8,12},{12,8},{16,20},{20,16},{24,28},{28,24},{1,5},{5... | collective-permute-start | bytes 196616 | tf_op jit(solution)/shard_map/ppermute | solution.py:16
  14.3 4.4 %collective-permute-start.6 = (bf16[256,128]{1,0:T(8,128)(2,1)S(1)}, bf16[256,128]{1,0:T(8,128)(2,1)S(1)}, u32[]{:S(2)}, u32[]{:S(2)}) collective-permute-start(bf16[256,128]{1,0:T(8,128)(2,1)S(1)} %collective-permute-done.2.refs_8_), channel_id=1, source_target_pairs={{0,4},{4,0},{8,12},{12,8},{16,20},{20,16},{24,28},{28,24},{1,5},{5... | collective-permute-start | bytes 196616 | tf_op jit(solution)/shard_map/ppermute | solution.py:16
  19.3 1.4 %collective-permute-start.7 = (bf16[512,128]{1,0:T(8,128)(2,1)S(1)}, bf16[512,128]{1,0:T(8,128)(2,1)S(1)}, u32[]{:S(2)}, u32[]{:S(2)}) collective-permute-start(bf16[512,128]{1,0:T(8,128)(2,1)S(1)} %get-tuple-element.54), channel_id=1, source_target_pairs={{0,1},{1,0},{2,3},{3,2},{4,5},{5,4},{6,7},{7,6},{8,9},{9,8},{10,11... | collective-permute-start | bytes 393224 | tf_op jit(solution)/shard_map/ppermute | solution.py:16
  20.8 5.6 %collective-permute-start.9 = (bf16[512,128]{1,0:T(8,128)(2,1)S(1)}, bf16[512,128]{1,0:T(8,128)(2,1)S(1)}, u32[]{:S(2)}, u32[]{:S(2)}) collective-permute-start(bf16[512,128]{1,0:T(8,128)(2,1)S(1)} %shard_map.140.total), channel_id=1, source_target_pairs={{0,2},{1,3},{2,0},{3,1},{4,6},{5,7},{6,4},{7,5},{8,10},{9,11},{10,... | collective-permute-start | bytes 393224 | tf_op jit(solution)/shard_map/ppermute | solution.py:16
  27.0 1.4 %collective-permute-start.10 = (bf16[512,128]{1,0:T(8,128)(2,1)S(1)}, bf16[512,128]{1,0:T(8,128)(2,1)S(1)}, u32[]{:S(2)}, u32[]{:S(2)}) collective-permute-start(bf16[512,128]{1,0:T(8,128)(2,1)S(1)} %get-tuple-element.60.refs_4_), channel_id=1, source_target_pairs={{0,1},{1,0},{2,3},{3,2},{4,5},{5,4},{6,7},{7,6},{8,9},{9,8},{10,11... | collective-permute-start | bytes 393224 | tf_op jit(solution)/shard_map/ppermute | solution.py:16
  27.1 2.9 %collective-permute-start.17 = (f32[144,256]{1,0:T(8,128)S(1)}, f32[144,256]{1,0:T(8,128)S(1)}, u32[]{:S(2)}, u32[]{:S(2)}) collective-permute-start(f32[144,256]{1,0:T(8,128)S(1)} %get-tuple-element.71), channel_id=1, source_target_pairs={{0,1},{1,0},{2,3},{3,2},{4,5},{5,4},{6,7},{7,6},{8,9},{9,8},{10,11... | collective-permute-start | bytes 442376 | tf_op jit(solution)/shard_map/ppermute | solution.py:16
  29.0 12.3 %collective-permute-start.11 = (bf16[512,128]{1,0:T(8,128)(2,1)S(1)}, bf16[512,128]{1,0:T(8,128)(2,1)S(1)}, u32[]{:S(2)}, u32[]{:S(2)}) collective-permute-start(bf16[512,128]{1,0:T(8,128)(2,1)S(1)} %get-tuple-element.63), channel_id=1, source_target_pairs={{0,4},{4,0},{8,12},{12,8},{16,20},{20,16},{24,28},{28,24},{1,5},{5... | collective-permute-start | bytes 393224 | tf_op jit(solution)/shard_map/ppermute | solution.py:16
  30.1 6.9 %collective-permute-start.18 = (bf16[144,256]{1,0:T(8,128)(2,1)S(1)}, bf16[144,256]{1,0:T(8,128)(2,1)S(1)}, u32[]{:S(2)}, u32[]{:S(2)}) collective-permute-start(bf16[144,256]{1,0:T(8,128)(2,1)S(1)} %shard_map.148.kept), channel_id=1, source_target_pairs={{0,16},{4,20},{8,24},{12,28},{16,0},{20,4},{24,8},{28,12},{1,17},{... | collective-permute-start | bytes 221192 | tf_op jit(solution)/shard_map/ppermute | solution.py:16
  32.4 5.3 %collective-permute-start.12 = (bf16[256,128]{1,0:T(8,128)(2,1)S(1)}, bf16[256,128]{1,0:T(8,128)(2,1)S(1)}, u32[]{:S(2)}, u32[]{:S(2)}) collective-permute-start(bf16[256,128]{1,0:T(8,128)(2,1)S(1)} %get-tuple-element.61), channel_id=1, source_target_pairs={{0,4},{4,0},{8,12},{12,8},{16,20},{20,16},{24,28},{28,24},{1,5},{5... | collective-permute-start | bytes 196616 | tf_op jit(solution)/shard_map/ppermute | solution.py:16
  33.7 7.2 %collective-permute-start.14 = (bf16[256,128]{1,0:T(8,128)(2,1)S(1)}, bf16[256,128]{1,0:T(8,128)(2,1)S(1)}, u32[]{:S(2)}, u32[]{:S(2)}) collective-permute-start(bf16[256,128]{1,0:T(8,128)(2,1)S(1)} %get-tuple-element.62), channel_id=1, source_target_pairs={{0,4},{4,0},{8,12},{12,8},{16,20},{20,16},{24,28},{28,24},{1,5},{5... | collective-permute-start | bytes 196616 | tf_op jit(solution)/shard_map/ppermute | solution.py:16
  37.0 5.4 %collective-permute-start.19 = (bf16[144,256]{1,0:T(8,128)(2,1)S(1)}, bf16[144,256]{1,0:T(8,128)(2,1)S(1)}, u32[]{:S(2)}, u32[]{:S(2)}) collective-permute-start(bf16[144,256]{1,0:T(8,128)(2,1)S(1)} %shard_map.149.kept), channel_id=1, source_target_pairs={{0,8},{4,12},{8,0},{12,4},{16,24},{20,28},{24,16},{28,20},{1,9},{5... | collective-permute-start | bytes 221192 | tf_op jit(solution)/shard_map/ppermute | solution.py:16
  37.7 9.4 %collective-permute-start.13 = (bf16[256,128]{1,0:T(8,128)(2,1)S(1)}, bf16[256,128]{1,0:T(8,128)(2,1)S(1)}, u32[]{:S(2)}, u32[]{:S(2)}) collective-permute-start(bf16[256,128]{1,0:T(8,128)(2,1)S(1)} %shard_map.144.refs_0_), channel_id=1, source_target_pairs={{0,24},{4,28},{8,16},{12,20},{16,8},{20,12},{24,0},{28,4},{1,25},{... | collective-permute-start | bytes 196616 | tf_op jit(solution)/shard_map/ppermute | solution.py:16
  40.9 6.3 %collective-permute-start.15 = (bf16[256,128]{1,0:T(8,128)(2,1)S(1)}, bf16[256,128]{1,0:T(8,128)(2,1)S(1)}, u32[]{:S(2)}, u32[]{:S(2)}) collective-permute-start(bf16[256,128]{1,0:T(8,128)(2,1)S(1)} %shard_map.145.refs_0_), channel_id=1, source_target_pairs={{0,16},{4,20},{8,24},{12,28},{16,0},{20,4},{24,8},{28,12},{1,17},{... | collective-permute-start | bytes 196616 | tf_op jit(solution)/shard_map/ppermute | solution.py:16
  41.4 5.8 %collective-permute-start.16 = (bf16[256,128]{1,0:T(8,128)(2,1)S(1)}, bf16[256,128]{1,0:T(8,128)(2,1)S(1)}, u32[]{:S(2)}, u32[]{:S(2)}) collective-permute-start(bf16[256,128]{1,0:T(8,128)(2,1)S(1)} %shard_map.146.refs_0_), channel_id=1, source_target_pairs={{0,8},{4,12},{8,0},{12,4},{16,24},{20,28},{24,16},{28,20},{1,9},{5... | collective-permute-start | bytes 196616 | tf_op jit(solution)/shard_map/ppermute | solution.py:16
  42.4 4.8 %collective-permute-start.20 = (bf16[144,256]{1,0:T(8,128)(2,1)S(1)}, bf16[144,256]{1,0:T(8,128)(2,1)S(1)}, u32[]{:S(2)}, u32[]{:S(2)}) collective-permute-start(bf16[144,256]{1,0:T(8,128)(2,1)S(1)} %shard_map.150.kept), channel_id=1, source_target_pairs={{0,4},{4,0},{8,12},{12,8},{16,20},{20,16},{24,28},{28,24},{1,5},{5... | collective-permute-start | bytes 221192 | tf_op jit(solution)/shard_map/ppermute | solution.py:16
  47.2 1.4 %collective-permute-start.21 = (f32[128,256]{1,0:T(8,128)S(1)}, f32[128,256]{1,0:T(8,128)S(1)}, u32[]{:S(2)}, u32[]{:S(2)}) collective-permute-start(f32[128,256]{1,0:T(8,128)S(1)} %slice.4), channel_id=1, source_target_pairs={{0,1},{1,0},{2,3},{3,2},{4,5},{5,4},{6,7},{7,6},{8,9},{9,8},{10,11... | collective-permute-start | bytes 393224 | tf_op jit(solution)/shard_map/ppermute | solution.py:16

commit v3 on v2

--- a/solution.py
+++ b/solution.py
@@ -150,6 +150,16 @@
             out[rows, :] = term if j == 0 else out[rows, :] + term
 
 
+def gather_more_kernel(mat, panel, so_far, out):
+    total_rows = out.shape[0]
+    chunk = min(256, total_rows)
+    for at in range(0, total_rows, chunk):
+        rows = slice(at, at + chunk)
+        out[rows, :] = so_far[rows, :] + jnp.dot(
+            mat[rows, :], panel[...], preferred_element_type=jnp.float32
+        )
+
+
 def gather_last_kernel(count, *refs):
     mats, panels, (so_far, keep, send) = refs[:count], refs[count : 2 * count], refs[2 * count :]
     half = keep.shape[0]
@@ -171,11 +181,10 @@
 
 
 def middle_kernel(
-    flip, scale, total, term, w_self, w_neigh, bias, *refs
+    flip, total, term, w_self, w_neigh, bias, *refs
 ):
-    bundles, (output, grad_own, grad_agg, keep, send) = refs[:-5], refs[-5:]
+    bundles, (output, grad_pre, aggregate, grad_agg) = refs[:-4], refs[-4:]
     row_count, width = bundles[0].shape[0], w_neigh.shape[0]
-    parts = []
     for j, bundle in enumerate(bundles):
         rows = slice(j * row_count, (j + 1) * row_count)
         there = slice((j ^ flip) * row_count, ((j ^ flip) + 1) * row_count)
@@ -200,16 +209,26 @@
         ).astype(jnp.bfloat16)
         if j == 0:
             output[...] = (preact * sigmoid_val).astype(jnp.bfloat16)
-            grad_own[...] = grad
+        grad_pre[rows, :] = grad
+        aggregate[rows, :] = agg
         back = lax.dot_general(
             grad, w_neigh[...], (((1,), (1,)), ((), ())), preferred_element_type=jnp.float32
         )
         grad_agg[rows, :] = (back / degree_f).astype(jnp.bfloat16)
+
+
+def weight_kernel(scale, aggregate, grad_pre, *refs):
+    bundles, (keep, send) = refs[:-2], refs[-2:]
+    row_count, width = bundles[0].shape[0], aggregate.shape[1]
+    parts = []
+    for j, bundle in enumerate(bundles):
+        rows = slice(j * row_count, (j + 1) * row_count)
+        grad = grad_pre[rows, :]
         grads = [
             lax.dot_general(
                 a, grad, (((0,), (0,)), ((), ())), preferred_element_type=jnp.float32
             )
-            for a in (features, agg)
+            for a in (bundle[:, :width], aggregate[rows, :])
         ]
         parts.append((*grads, jnp.sum(grad.astype(jnp.float32), axis=0, keepdims=True)))
     while len(parts) > 1:
@@ -230,34 +249,53 @@
     return total.T
 
 
+def spread_near_kernel(count, *refs):
+    mats, near, outs = refs[:count], refs[count], refs[count + 1 :]
+    near_t = near[...].T
+    for mat, out in zip(mats, outs):
+        half = near.shape[0]
+        out[...] = jnp.dot(near_t, mat[:half, :], preferred_element_type=jnp.float32)
+
+
 def spread_away_kernel(groups, *refs):
     count = sum(groups)
-    mats, (near, far), outs = refs[:count], refs[count : count + 2], refs[count + 2 :]
-    near_t, far_t = near[...].T, far[...].T
+    mats, begun, far, outs = (
+        refs[:count],
+        refs[count : 2 * count],
+        refs[2 * count],
+        refs[2 * count + 1 :],
+    )
+    far_t = far[...].T
+    half = far.shape[0]
     j = 0
     for size, out in zip(groups, outs):
         rows = out.shape[0] // size
         for k in range(size):
-            term = spread(mats[j], near_t, far_t)
-            out[k * rows : (k + 1) * rows, :] = term.astype(jnp.bfloat16)
+            term = begun[j][...] + jnp.dot(
+                far_t, mats[j][half:, :], preferred_element_type=jnp.float32
+            )
+            out[k * rows : (k + 1) * rows, :] = term.T.astype(jnp.bfloat16)
             j += 1
 
 
 def spread_here_kernel(near_count, count, *refs):
-    mats, (near, far, grad_own, w_self) = refs[:count], refs[count : count + 4]
-    outs, (stage, done) = refs[count + 4 : -2], refs[-2:]
+    mats, (near, far, grad_pre, w_self, held) = refs[:count], refs[count : count + 5]
+    outs, (output, stage, done, left) = refs[count + 5 : -4], refs[-4:]
+    leave = pltpu.make_async_copy(held, output, left)
+    leave.start()
     take = fetched(mats, near_count, stage, done)
     near_t, far_t = near[...].T, far[...].T
     for j, out in enumerate(outs):
         term = spread(take(j), near_t, far_t)
         if j == count - 1:
             term += lax.dot_general(
-                grad_own[...],
+                grad_pre[: out.shape[0], :],
                 w_self[...],
                 (((1,), (1,)), ((), ())),
                 preferred_element_type=jnp.float32,
             )
         out[...] = term.astype(out.dtype)
+    leave.wait()
 
 
 def pair_kernel(part, term, message, *refs):
@@ -367,10 +405,10 @@
     if not small:
         mats |= place(stay, True, False)[0]
     bundles = [bundle] + [swap(bundle, "rep", mask) for mask in range(2, rep_count, 2)]
-    arrivals = [*far_first, 1]
+    arrivals = [*far_first[:0:-1], far_first[0], 1]
     mats[late[0]], *got = after(mats[late[0]], *[panels[m] for m in arrivals])
     panels.update(zip(arrivals, got))
-    for mask in far_first:
+    for mask in arrivals[:-1]:
         panels[mask ^ 1] = swap(panels[mask], "loop", 1)
 
     early = [1, *stay]
@@ -392,12 +430,19 @@
             transcendentals=0,
         ),
     )(*[mats[m] for m in early], *[panels[m] for m in early])
+    *sooner, latest = [m ^ 1 for m in arrivals[:-1]]
+    for mask in sooner:
+        (running,) = call(
+            gather_more_kernel,
+            [f32((all_rows, feat_width))],
+            [VMEM] * 3,
+            (mats[mask], panels[mask], running),
+        )
     keep, send = call(
-        functools.partial(gather_last_kernel, len(late)),
+        functools.partial(gather_last_kernel, 1),
         [f32((half_rows, feat_width)), bf16((half_rows, feat_width))],
-        [VMEM] * (2 * len(late) + 1),
-        [mats[m] for m in late] + [panels[m] for m in late] + [running],
-        flops=2 * len(late) * all_rows * row_count * feat_width,
+        [VMEM] * 3,
+        (mats[latest], panels[latest], running),
     )
     total = added(keep, swap(send, "rep", 1))
     total, *bundles = after(total, *bundles)
@@ -415,41 +460,55 @@
     scale = 1.0 / math.sqrt(row_count * loop_count * rep_count)
     weight_shape = (feat_width + 16, hidden)
     output_shape = (row_count, hidden)
-    output, grad_own, grad_agg, keep_w, send_w = call(
-        functools.partial(middle_kernel, mask // 2, scale),
+    output, grad_pre, aggregate, grad_agg = call(
+        functools.partial(middle_kernel, mask // 2),
         [
-            pltpu.VMEM(output_shape, jnp.bfloat16) if small else bf16(output_shape),
             bf16(output_shape),
+            bf16((half_rows, hidden)),
             bf16((half_rows, feat_width)),
-            f32(weight_shape),
-            f32(weight_shape),
+            bf16((half_rows, feat_width)),
         ],
         [VMEM] * (5 + len(bundles)),
         (total, term, w_self, w_neigh, bias[None, :], *bundles),
-        flops=8 * half_rows * feat_width * hidden,
+        flops=4 * half_rows * feat_width * hidden,
     )
     grad_far = swap(grad_agg, "rep", 1)
+    keep_w, send_w = call(
+        functools.partial(weight_kernel, scale),
+        [f32(weight_shape)] * 2,
+        [VMEM] * (2 + len(bundles)),
+        (aggregate, grad_pre, *bundles),
+        flops=4 * half_rows * feat_width * hidden,
+    )
     sent_w = added(keep_w, swap(send_w, "rep", 1))
 
     away_groups = [1] * (len(far_first) - 1) + [2]
+    begun = call(
+        functools.partial(spread_near_kernel, len(away_masks)),
+        [f32((feat_width, row_count))] * len(away_masks),
+        [VMEM] * (len(away_masks) + 1),
+        (*[mats[m] for m in away_masks], grad_agg),
+        flops=len(stay) * all_rows * row_count * feat_width,
+    )
     away = call(
         functools.partial(spread_away_kernel, away_groups),
         [bf16((size * row_count, feat_width)) for size in away_groups],
-        [VMEM] * (len(stay) + 2),
-        (*[mats[m] for m in away_masks], grad_agg, grad_far),
-        flops=2 * len(stay) * all_rows * row_count * feat_width,
+        [VMEM] * (2 * len(away_masks) + 1),
+        (*[mats[m] for m in away_masks], *begun, grad_far),
+        flops=len(stay) * all_rows * row_count * feat_width,
     )
     arrived = [swap(message, "loop", 1) for message in away]
     grad_far, *away = after(grad_far, *away)
     kept = pl.pallas_call(
         functools.partial(spread_here_kernel, len(stay) - far_count, len(stay)),
         out_shape=[bf16((row_count, feat_width))] * len(far_first)
-        + [f32((row_count, feat_width))],
-        in_specs=[VMEM] * (len(stay) - far_count) + [HBM] * far_count + [VMEM] * 4,
-        out_specs=[VMEM] * len(stay),
+        + [f32((row_count, feat_width)), pltpu.HBM(output_shape, jnp.bfloat16)],
+        in_specs=[VMEM] * (len(stay) - far_count) + [HBM] * far_count + [VMEM] * 5,
+        out_specs=[VMEM] * len(stay) + [HBM],
         scratch_shapes=[
             pltpu.VMEM((far_count, *mat_shape) if far_count else (1, 16, 128), jnp.bfloat16),
             pltpu.SemaphoreType.DMA((2 * max(1, far_count),)),
+            pltpu.SemaphoreType.DMA,
         ],
         compiler_params=pltpu.CompilerParams(vmem_limit_bytes=grant(2 * loop_count * mat_bytes)),
         cost_estimate=pl.CostEstimate(
@@ -457,7 +516,9 @@
             bytes_accessed=far_count * mat_bytes,
             transcendentals=0,
         ),
-    )(*[mats[m] for m in stay], grad_agg, grad_far, grad_own, w_self)
+    )(*[mats[m] for m in stay], grad_agg, grad_far, grad_pre, w_self, output)
+    *kept, output = kept
+    arrived_w = swap(sent_w, "loop", loop_count // 2)
     pieces = [(message, k) for message, size in zip(arrived, away_groups) for k in range(size)]
     pairs = []
     for term, (message, part) in zip(kept[:-1], pieces):
@@ -468,21 +529,19 @@
             (term, message, *pairs[-1:]),
         )
     back = [swap(pair, "loop", m) for m, pair in zip(far_first, pairs)]
+    mask = loop_count // 4
+    while mask:
+        sent_w = added(sent_w, arrived_w, *(pairs[2:3] if mask == 1 else []))
+        arrived_w = swap(sent_w, "loop", mask)
+        mask //= 2
+    sent_w = added(sent_w, arrived_w, token(back, 12_000_000_000), dtype=jnp.float32)
     message, part = pieces[-1]
     (grad_input,) = call(
         functools.partial(sum_kernel, part),
         [bf16((row_count, feat_width))],
         [VMEM] * (2 + len(back)),
         (kept[-1], message, *back),
-        flops=0,
-    )
-    mask = loop_count // 2
-    while mask:
-        arrived_w = swap(sent_w, "loop", mask)
-        dtype = jnp.bfloat16 if mask > 1 else jnp.float32
-        earlier = {loop_count // 2: [], 2: pairs[2:3], 1: [token(back, 12_000_000_000)]}.get(mask, [])
-        sent_w = added(sent_w, arrived_w, *earlier, dtype=dtype)
-        mask //= 2
+    )
     other = swap(sent_w[:feat_width], "rep", 1)
     grad_self, grad_neigh, grad_bias = call(
         finish_kernel,

time: 49.5 us -> 49.1 us (level)
  starting transfers between devices: 25 us -> 24.1 us
  Pallas kernels: 7.76 us -> 8.53 us
  local copies, waits for them, and re-layouts: 0.69 us -> 0.03 us
    ppermute x22, starting transfers between devices: 25 us -> 24.1 us  [swap(): lax.ppermute(block, axis, [(i, i ^ mask) for i in range(lax.axis_size(axi...]
    unnamed x9 -> x8, local copies, waits for them, and re-layouts: 0.68 us -> 0.02 us
    pallas_call x14 -> x18, Pallas kernels: 3.28 us -> 3.92 us  [call(): pl.pallas_call(kernel, out_shape=list(out_shape), in_specs=in_specs, out_...]
  transfers between devices with their start and end apart: 22 -> 22, of which waited for: 8 -> 10; matrix products, arithmetic and copies ran while one was open for 1% -> 0% of each run, Pallas kernels for 13% -> 15%
where the time goes in v3:
time: 49.1 us; the launch traced here: 48.9 us
  starting transfers between devices  24.1 us (49%)
  waiting for transfers between devices  15.4 us (31%)
  Pallas kernels  8.53 us (17%)
  between operations  0.83 us (2%)
    ppermute x22, starting transfers between devices, swap(): lax.ppermute(block, axis, [(i, i ^ mask) for i in range(lax.axis_size(axi...  24.1 us
    ppermute x22, waiting for transfers between devices, swap(): lax.ppermute(block, axis, [(i, i ^ mask) for i in range(lax.axis_size(axi...  15.4 us
    pallas_call x18, Pallas kernels, call(): pl.pallas_call(kernel, out_shape=list(out_shape), in_specs=in_specs, out_...  3.92 us
    pallas_call x1, Pallas kernels, place(): pl.pallas_call(functools.partial(place_kernel, near_count, masks, rep_cou...  3.08 us
  transfers between devices with their start and end apart: 22, of which 10 were waited for; matrix products, arithmetic and copies ran while one was open for 0% of the time, Pallas kernels for 15%

profile of v3, /device:TPU:0, one launch (start us, length us, event | category | flops | bytes accessed | tf_op | source)
XLA Modules:
  0.0 48.9 jit_solution(13571334386252414499)
XLA Ops:
  0.6 5.1 %collective-permute-start.2 = (bf16[256,128]{1,0:T(8,128)(2,1)}, bf16[256,128]{1,0:T(8,128)(2,1)S(1)}, u32[]{:S(2)}, u32[]{:S(2)}) collective-permute-start(bf16[256,128]{1,0:T(8,128)(2,1)} %refs_9_.1), channel_id=1, source_target_pairs={{0,24},{4,28},{8,16},{12,20},{16,8},{20,12},{24,0},{28,4},{1,25},{... | collective-permute-start | bytes 196616 | tf_op jit(solution)/shard_map/ppermute | solution.py:16
  5.8 0.0 collective-permute-start.1
  5.8 0.6 %collective-permute-start = (bf16[256,128]{1,0:T(8,128)(2,1)}, bf16[256,128]{1,0:T(8,128)(2,1)S(1)}, u32[]{:S(2)}, u32[]{:S(2)}) collective-permute-start(bf16[256,128]{1,0:T(8,128)(2,1)} %refs_9_.1), channel_id=1, source_target_pairs={{0,8},{4,12},{8,0},{12,4},{16,24},{20,28},{24,16},{28,20},{1,9},{5... | collective-permute-start | bytes 196616 | tf_op jit(solution)/shard_map/ppermute | solution.py:16
  6.4 1.7 %collective-permute-start.3 = (bf16[256,128]{1,0:T(8,128)(2,1)}, bf16[256,128]{1,0:T(8,128)(2,1)S(1)}, u32[]{:S(2)}, u32[]{:S(2)}) collective-permute-start(bf16[256,128]{1,0:T(8,128)(2,1)} %refs_9_.1), channel_id=1, source_target_pairs={{0,4},{4,0},{8,12},{12,8},{16,20},{20,16},{24,28},{28,24},{1,5},{5... | collective-permute-start | bytes 196616 | tf_op jit(solution)/shard_map/ppermute | solution.py:16
  8.1 3.1 %shard_map.137 = (bf16[1024,256]{1,0:T(8,128)(2,1)S(1)}, bf16[1024,256]{1,0:T(8,128)(2,1)S(1)}, bf16[1024,256]{1,0:T(8,128)(2,1)S(1)}, bf16[1024,256]{1,0:T(8,12...) custom-call(s32[8,16]{1,0:T(8,128)} %bitcast.9, ...), custom_call_target="tpu_custom_call" | custom-call | bytes 8388608 | tf_op jit(solution)/shard_map/pallas_call | solution.py:382
  11.2 1.7 %collective-permute-start.8 = (bf16[256,512]{1,0:T(8,128)(2,1)S(1)}, bf16[256,512]{1,0:T(8,128)(2,1)S(1)}, u32[]{:S(2)}, u32[]{:S(2)}) collective-permute-start(bf16[256,512]{1,0:T(8,128)(2,1)S(1)} %get-tuple-element.63.refs_0_), channel_id=1, source_target_pairs={{0,2},{1,3},{2,0},{3,1},{4,6},{5,7},{6,4},{7,5},{8,10},{9,11},{10,... | collective-permute-start | bytes 786440 | tf_op jit(solution)/shard_map/ppermute | solution.py:16
  12.8 0.0 collective-permute-done.2.refs_6_
  12.8 0.0 collective-permute-done.3.refs_5_
  12.8 0.4 collective-permute-start.6
  13.2 1.7 %collective-permute-start.5 = (bf16[256,128]{1,0:T(8,128)(2,1)S(1)}, bf16[256,128]{1,0:T(8,128)(2,1)S(1)}, u32[]{:S(2)}, u32[]{:S(2)}) collective-permute-start(bf16[256,128]{1,0:T(8,128)(2,1)S(1)} %collective-permute-done.1.refs_7_), channel_id=1, source_target_pairs={{0,4},{4,0},{8,12},{12,8},{16,20},{20,16},{24,28},{28,24},{1,5},{5... | collective-permute-start | bytes 196616 | tf_op jit(solution)/shard_map/ppermute | solution.py:16
  14.9 0.3 collective-permute-start.4
  15.2 0.8 %shard_map.138.so_far = f32[1024,128]{1,0:T(8,128)S(1)} custom-call(bf16[1024,256]{1,0:T(8,128)(2,1)S(1)} %get-tuple-element.57.refs_0_.refs_3_, bf16[1024,256]{1,0:T(8,128)(2,1)S(1)} %get-tuple-element.46.refs_1_.refs_0_, bf16[1024,256]{1,0:T(8,128)(2,1)S(1)} %get-tuple-element.47.refs_2_.refs_1_, bf16[1024,256]{1,0:T(8,128)(2,1)S(1)} %get-tuple-element.48.refs_3_.refs_2_, ...), custom_call_target="tpu_custom_call" | custom-call | flops 335544320 | tf_op jit(solution)/shard_map/pallas_call | solution.py:415
  16.1 1.3 %collective-permute-done.6.panel = bf16[256,128]{1,0:T(8,128)(2,1)S(1)} collective-permute-done((bf16[256,128]{1,0:T(8,128)(2,1)S(1)}, bf16[256,128]{1,0:T(8,128)(2,1)S(1)}, u32[]{:S(2)}, u32[]{:S(2)}) %collective-permute-start.6) | collective-permute-done | bytes 65568 | tf_op jit(solution)/shard_map/ppermute | solution.py:16
  17.4 0.3 shard_map.139.so_far
  17.6 0.4 collective-permute-done.5.panel
  18.1 0.3 shard_map.140.refs_2_
  18.4 0.8 %collective-permute-done.4.refs_1_ = bf16[256,128]{1,0:T(8,128)(2,1)S(1)} collective-permute-done((bf16[256,128]{1,0:T(8,128)(2,1)S(1)}, bf16[256,128]{1,0:T(8,128)(2,1)S(1)}, u32[]{:S(2)}, u32[]{:S(2)}) %collective-permute-start.4) | collective-permute-done | bytes 65568 | tf_op jit(solution)/shard_map/ppermute | solution.py:16
  19.2 0.3 shard_map.141
  19.5 0.1 collective-permute-start.7
  19.6 1.3 %collective-permute-done.7.arrived = bf16[512,128]{1,0:T(8,128)(2,1)S(1)} collective-permute-done((bf16[512,128]{1,0:T(8,128)(2,1)S(1)}, bf16[512,128]{1,0:T(8,128)(2,1)S(1)}, u32[]{:S(2)}, u32[]{:S(2)}) %collective-permute-start.7) | collective-permute-done | bytes 131104 | tf_op jit(solution)/shard_map/ppermute | solution.py:16
  20.9 0.0 collective-permute-done.8.refs_1_
  20.9 1.1 %collective-permute-start.9 = (bf16[512,128]{1,0:T(8,128)(2,1)S(1)}, bf16[512,128]{1,0:T(8,128)(2,1)S(1)}, u32[]{:S(2)}, u32[]{:S(2)}) collective-permute-start(bf16[512,128]{1,0:T(8,128)(2,1)S(1)} %shard_map.142.total), channel_id=1, source_target_pairs={{0,2},{1,3},{2,0},{3,1},{4,6},{5,7},{6,4},{7,5},{8,10},{9,11},{10,... | collective-permute-start | bytes 393224 | tf_op jit(solution)/shard_map/ppermute | solution.py:16
  22.1 4.5 %collective-permute-done.9.term = bf16[512,128]{1,0:T(8,128)(2,1)S(1)} collective-permute-done((bf16[512,128]{1,0:T(8,128)(2,1)S(1)}, bf16[512,128]{1,0:T(8,128)(2,1)S(1)}, u32[]{:S(2)}, u32[]{:S(2)}) %collective-permute-start.9) | collective-permute-done | bytes 131104 | tf_op jit(solution)/shard_map/ppermute | solution.py:16
  26.6 0.5 %shard_map.143 = (bf16[256,256]{1,0:T(8,128)(2,1)S(1)}, bf16[512,256]{1,0:T(8,128)(2,1)S(1)}, bf16[512,128]{1,0:T(8,128)(2,1)S(1)}, bf16[512,128]{1,0:T(8,128)(2,1)S(1)}) custom-call(bf16[512,128]{1,0:T(8,128)(2,1)S(1)} %shard_map.142.total, bf16[512,128]{1,0:T(8,128)(2,1)S(1)} %collective-permute-done.9.term, bf16[128,256]{1,0:T(8,128)(2,1)S(1)} %copy-done.1, ...), custom_call_target="tpu_custom_call" | custom-call | flops 67108864 | bytes 1573888 | tf_op jit(solution)/shard_map/pallas_call | solution.py:25
  27.1 0.1 collective-permute-start.10
  27.2 0.3 shard_map.151
  27.5 0.6 %collective-permute-start.17 = (f32[144,256]{1,0:T(8,128)S(1)}, f32[144,256]{1,0:T(8,128)S(1)}, u32[]{:S(2)}, u32[]{:S(2)}) collective-permute-start(f32[144,256]{1,0:T(8,128)S(1)} %get-tuple-element.83), channel_id=1, source_target_pairs={{0,1},{1,0},{2,3},{3,2},{4,5},{5,4},{6,7},{7,6},{8,9},{9,8},{10,11... | collective-permute-start | bytes 442376 | tf_op jit(solution)/shard_map/ppermute | solution.py:16
  28.0 0.3 shard_map.144
  28.3 0.2 collective-permute-done.10.refs_8_.refs_5_
  28.5 0.4 shard_map.145
  28.9 0.8 %collective-permute-start.11 = (bf16[512,128]{1,0:T(8,128)(2,1)S(1)}, bf16[512,128]{1,0:T(8,128)(2,1)S(1)}, u32[]{:S(2)}, u32[]{:S(2)}) collective-permute-start(bf16[512,128]{1,0:T(8,128)(2,1)S(1)} %get-tuple-element.72), channel_id=1, source_target_pairs={{0,4},{4,0},{8,12},{12,8},{16,20},{20,16},{24,28},{28,24},{1,5},{5... | collective-permute-start | bytes 393224 | tf_op jit(solution)/shard_map/ppermute | solution.py:16
  29.7 0.0 collective-permute-done.17.arrived
  29.7 1.8 %collective-permute-start.18 = (bf16[144,256]{1,0:T(8,128)(2,1)S(1)}, bf16[144,256]{1,0:T(8,128)(2,1)S(1)}, u32[]{:S(2)}, u32[]{:S(2)}) collective-permute-start(bf16[144,256]{1,0:T(8,128)(2,1)S(1)} %shard_map.152.kept), channel_id=1, source_target_pairs={{0,16},{4,20},{8,24},{12,28},{16,0},{20,4},{24,8},{28,12},{1,17},{... | collective-permute-start | bytes 221192 | tf_op jit(solution)/shard_map/ppermute | solution.py:16
  31.5 1.0 %collective-permute-start.12 = (bf16[256,128]{1,0:T(8,128)(2,1)S(1)}, bf16[256,128]{1,0:T(8,128)(2,1)S(1)}, u32[]{:S(2)}, u32[]{:S(2)}) collective-permute-start(bf16[256,128]{1,0:T(8,128)(2,1)S(1)} %get-tuple-element.70), channel_id=1, source_target_pairs={{0,4},{4,0},{8,12},{12,8},{16,20},{20,16},{24,28},{28,24},{1,5},{5... | collective-permute-start | bytes 196616 | tf_op jit(solution)/shard_map/ppermute | solution.py:16
  32.5 1.0 %collective-permute-start.14 = (bf16[256,128]{1,0:T(8,128)(2,1)S(1)}, bf16[256,128]{1,0:T(8,128)(2,1)S(1)}, u32[]{:S(2)}, u32[]{:S(2)}) collective-permute-start(bf16[256,128]{1,0:T(8,128)(2,1)S(1)} %get-tuple-element.71), channel_id=1, source_target_pairs={{0,4},{4,0},{8,12},{12,8},{16,20},{20,16},{24,28},{28,24},{1,5},{5... | collective-permute-start | bytes 196616 | tf_op jit(solution)/shard_map/ppermute | solution.py:16
  33.5 3.1 %collective-permute-done.18.arrived = bf16[144,256]{1,0:T(8,128)(2,1)S(1)} collective-permute-done((bf16[144,256]{1,0:T(8,128)(2,1)S(1)}, bf16[144,256]{1,0:T(8,128)(2,1)S(1)}, u32[]{:S(2)}, u32[]{:S(2)}) %collective-permute-start.18) | collective-permute-done | bytes 73760 | tf_op jit(solution)/shard_map/ppermute | solution.py:16
  36.6 0.2 collective-permute-start.19
  36.8 0.7 %shard_map.146 = (bf16[256,128]{1,0:T(8,128)(2,1)S(1)}, bf16[256,128]{1,0:T(8,128)(2,1)S(1)}, bf16[256,128]{1,0:T(8,128)(2,1)S(1)}, f32[256,128]{1,0:T(8,128)S(1)}, bf16[256,256]{1,0:T(8,128)(2,1)}) custom-call(bf16[1024,256]{1,0:T(8,128)(2,1)S(1)} %get-tuple-element.46.refs_1_.refs_0_, bf16[1024,256]{1,0:T(8,128)(2,1)S(1)} %get-tuple-element.47.refs_2_.refs_1_, ...), custom_call_target="tpu_custom_call" | custom-call | flops 268435456 | tf_op jit(solution)/shard_map/pallas_call | solution.py:502
  37.5 3.2 %collective-permute-start.13 = (bf16[256,128]{1,0:T(8,128)(2,1)S(1)}, bf16[256,128]{1,0:T(8,128)(2,1)S(1)}, u32[]{:S(2)}, u32[]{:S(2)}) collective-permute-start(bf16[256,128]{1,0:T(8,128)(2,1)S(1)} %shard_map.147.refs_0_), channel_id=1, source_target_pairs={{0,24},{4,28},{8,16},{12,20},{16,8},{20,12},{24,0},{28,4},{1,25},{... | collective-permute-start | bytes 196616 | tf_op jit(solution)/shard_map/ppermute | solution.py:16
  40.7 0.3 collective-permute-start.15
  41.1 1.1 %collective-permute-start.16 = (bf16[256,128]{1,0:T(8,128)(2,1)S(1)}, bf16[256,128]{1,0:T(8,128)(2,1)S(1)}, u32[]{:S(2)}, u32[]{:S(2)}) collective-permute-start(bf16[256,128]{1,0:T(8,128)(2,1)S(1)} %shard_map.149.refs_0_), channel_id=1, source_target_pairs={{0,8},{4,12},{8,0},{12,4},{16,24},{20,28},{24,16},{28,20},{1,9},{5... | collective-permute-start | bytes 196616 | tf_op jit(solution)/shard_map/ppermute | solution.py:16
  42.2 1.4 %collective-permute-start.20 = (bf16[144,256]{1,0:T(8,128)(2,1)S(1)}, bf16[144,256]{1,0:T(8,128)(2,1)S(1)}, u32[]{:S(2)}, u32[]{:S(2)}) collective-permute-start(bf16[144,256]{1,0:T(8,128)(2,1)S(1)} %shard_map.154.kept), channel_id=1, source_target_pairs={{0,4},{4,0},{8,12},{12,8},{16,20},{20,16},{24,28},{28,24},{1,5},{5... | collective-permute-start | bytes 221192 | tf_op jit(solution)/shard_map/ppermute | solution.py:16
  43.6 0.6 %collective-permute-done.13.refs_0_ = bf16[256,128]{1,0:T(8,128)(2,1)S(1)} collective-permute-done((bf16[256,128]{1,0:T(8,128)(2,1)S(1)}, bf16[256,128]{1,0:T(8,128)(2,1)S(1)}, u32[]{:S(2)}, u32[]{:S(2)}) %collective-permute-start.13) | collective-permute-done | bytes 65568 | tf_op jit(solution)/shard_map/ppermute | solution.py:16
  44.2 2.5 %collective-permute-done.15.refs_1_ = bf16[256,128]{1,0:T(8,128)(2,1)S(1)} collective-permute-done((bf16[256,128]{1,0:T(8,128)(2,1)S(1)}, bf16[256,128]{1,0:T(8,128)(2,1)S(1)}, u32[]{:S(2)}, u32[]{:S(2)}) %collective-permute-start.15) | collective-permute-done | bytes 65568 | tf_op jit(solution)/shard_map/ppermute | solution.py:16
  46.8 0.1 collective-permute-start.21
  46.9 0.7 %shard_map.150 = bf16[256,128]{1,0:T(8,128)(2,1)} custom-call(f32[256,128]{1,0:T(8,128)S(1)} %get-tuple-element.77.own, bf16[512,128]{1,0:T(8,128)(2,1)S(1)} %collective-permute-done.11.message, bf16[256,128]{1,0:T(8,128)(2,1)S(1)} %collective-permute-done.13.refs_0_, bf16[256,128]{1,0:T(8,128)(2,1)S(1)} %collective-permute-done.15.refs_1_, ...), custom_call_target="tpu_custom_call" | custom-call | bytes 524288 | tf_op jit(solution)/shard_map/pallas_call | solution.py:25
  47.5 0.7 %collective-permute-done.21.other = f32[128,256]{1,0:T(8,128)S(1)} collective-permute-done((f32[128,256]{1,0:T(8,128)S(1)}, f32[128,256]{1,0:T(8,128)S(1)}, u32[]{:S(2)}, u32[]{:S(2)}) %collective-permute-start.21) | collective-permute-done | bytes 131104 | tf_op jit(solution)/shard_map/ppermute | solution.py:16
  48.2 0.7 %shard_map.157 = (f32[128,256]{1,0:T(8,128)}, f32[128,256]{1,0:T(8,128)}, f32[1,256]{1,0:T(1,128)}) custom-call(f32[144,256]{1,0:T(8,128)S(1)} %shard_map.156.weights, f32[128,256]{1,0:T(8,128)S(1)} %collective-permute-done.21.other), custom_call_target="tpu_custom_call" | custom-call | bytes 541696 | tf_op jit(solution)/shard_map/pallas_call | solution.py:25
  (26 shorter events, 0.2 us)
Async XLA Ops:
  0.6 14.6 %copy-start = (bf16[256,128]{1,0:T(8,128)(2,1)S(1)}, bf16[256,128]{1,0:T(8,128)(2,1)}, u32[]{:S(2)}) copy-start(bf16[256,128]{1,0:T(8,128)(2,1)} %refs_9_.1) | copy-start | bytes 196612
  0.6 12.2 %collective-permute-start.2 = (bf16[256,128]{1,0:T(8,128)(2,1)}, bf16[256,128]{1,0:T(8,128)(2,1)S(1)}, u32[]{:S(2)}, u32[]{:S(2)}) collective-permute-start(bf16[256,128]{1,0:T(8,128)(2,1)} %refs_9_.1), channel_id=1, source_target_pairs={{0,24},{4,28},{8,16},{12,20},{16,8},{20,12},{24,0},{28,4},{1,25},{... | collective-permute-start | bytes 196616 | tf_op jit(solution)/shard_map/ppermute | solution.py:16
  5.8 7.1 %collective-permute-start.1 = (bf16[256,128]{1,0:T(8,128)(2,1)}, bf16[256,128]{1,0:T(8,128)(2,1)S(1)}, u32[]{:S(2)}, u32[]{:S(2)}) collective-permute-start(bf16[256,128]{1,0:T(8,128)(2,1)} %refs_9_.1), channel_id=1, source_target_pairs={{0,16},{4,20},{8,24},{12,28},{16,0},{20,4},{24,8},{28,12},{1,17},{... | collective-permute-start | bytes 196616 | tf_op jit(solution)/shard_map/ppermute | solution.py:16
  5.8 7.1 %collective-permute-start = (bf16[256,128]{1,0:T(8,128)(2,1)}, bf16[256,128]{1,0:T(8,128)(2,1)S(1)}, u32[]{:S(2)}, u32[]{:S(2)}) collective-permute-start(bf16[256,128]{1,0:T(8,128)(2,1)} %refs_9_.1), channel_id=1, source_target_pairs={{0,8},{4,12},{8,0},{12,4},{16,24},{20,28},{24,16},{28,20},{1,9},{5... | collective-permute-start | bytes 196616 | tf_op jit(solution)/shard_map/ppermute | solution.py:16
  6.4 6.4 %collective-permute-start.3 = (bf16[256,128]{1,0:T(8,128)(2,1)}, bf16[256,128]{1,0:T(8,128)(2,1)S(1)}, u32[]{:S(2)}, u32[]{:S(2)}) collective-permute-start(bf16[256,128]{1,0:T(8,128)(2,1)} %refs_9_.1), channel_id=1, source_target_pairs={{0,4},{4,0},{8,12},{12,8},{16,20},{20,16},{24,28},{28,24},{1,5},{5... | collective-permute-start | bytes 196616 | tf_op jit(solution)/shard_map/ppermute | solution.py:16
  11.2 9.8 %collective-permute-start.8 = (bf16[256,512]{1,0:T(8,128)(2,1)S(1)}, bf16[256,512]{1,0:T(8,128)(2,1)S(1)}, u32[]{:S(2)}, u32[]{:S(2)}) collective-permute-start(bf16[256,512]{1,0:T(8,128)(2,1)S(1)} %get-tuple-element.63.refs_0_), channel_id=1, source_target_pairs={{0,2},{1,3},{2,0},{3,1},{4,6},{5,7},{6,4},{7,5},{8,10},{9,11},{10,... | collective-permute-start | bytes 786440 | tf_op jit(solution)/shard_map/ppermute | solution.py:16
  12.8 4.5 %collective-permute-start.6 = (bf16[256,128]{1,0:T(8,128)(2,1)S(1)}, bf16[256,128]{1,0:T(8,128)(2,1)S(1)}, u32[]{:S(2)}, u32[]{:S(2)}) collective-permute-start(bf16[256,128]{1,0:T(8,128)(2,1)S(1)} %collective-permute-done.refs_8_), channel_id=1, source_target_pairs={{0,4},{4,0},{8,12},{12,8},{16,20},{20,16},{24,28},{28,24},{1,5},{5... | collective-permute-start | bytes 196616 | tf_op jit(solution)/shard_map/ppermute | solution.py:16
  13.2 4.9 %collective-permute-start.5 = (bf16[256,128]{1,0:T(8,128)(2,1)S(1)}, bf16[256,128]{1,0:T(8,128)(2,1)S(1)}, u32[]{:S(2)}, u32[]{:S(2)}) collective-permute-start(bf16[256,128]{1,0:T(8,128)(2,1)S(1)} %collective-permute-done.1.refs_7_), channel_id=1, source_target_pairs={{0,4},{4,0},{8,12},{12,8},{16,20},{20,16},{24,28},{28,24},{1,5},{5... | collective-permute-start | bytes 196616 | tf_op jit(solution)/shard_map/ppermute | solution.py:16
  14.9 4.3 %collective-permute-start.4 = (bf16[256,128]{1,0:T(8,128)(2,1)S(1)}, bf16[256,128]{1,0:T(8,128)(2,1)S(1)}, u32[]{:S(2)}, u32[]{:S(2)}) collective-permute-start(bf16[256,128]{1,0:T(8,128)(2,1)S(1)} %collective-permute-done.2.refs_6_), channel_id=1, source_target_pairs={{0,4},{4,0},{8,12},{12,8},{16,20},{20,16},{24,28},{28,24},{1,5},{5... | collective-permute-start | bytes 196616 | tf_op jit(solution)/shard_map/ppermute | solution.py:16
  15.2 11.3 %copy-start.1 = (bf16[128,256]{1,0:T(8,128)(2,1)S(1)}, bf16[128,256]{1,0:T(8,128)(2,1)}, u32[]{:S(2)}) copy-start(bf16[128,256]{1,0:T(8,128)(2,1)} %refs_7_.1) | copy-start | bytes 196612
  15.2 11.3 %copy-start.2 = (bf16[128,256]{1,0:T(8,128)(2,1)S(1)}, bf16[128,256]{1,0:T(8,128)(2,1)}, u32[]{:S(2)}) copy-start(bf16[128,256]{1,0:T(8,128)(2,1)} %w_neigh.1) | copy-start | bytes 196612
  15.2 11.3 %copy-start.3 = (f32[256]{0:T(256)S(1)}, f32[256]{0:T(256)}, u32[]{:S(2)}) copy-start(f32[256]{0:T(256)} %param.13) | copy-start | bytes 3076
  19.5 1.4 %collective-permute-start.7 = (bf16[512,128]{1,0:T(8,128)(2,1)S(1)}, bf16[512,128]{1,0:T(8,128)(2,1)S(1)}, u32[]{:S(2)}, u32[]{:S(2)}) collective-permute-start(bf16[512,128]{1,0:T(8,128)(2,1)S(1)} %get-tuple-element.60), channel_id=1, source_target_pairs={{0,1},{1,0},{2,3},{3,2},{4,5},{5,4},{6,7},{7,6},{8,9},{9,8},{10,11... | collective-permute-start | bytes 393224 | tf_op jit(solution)/shard_map/ppermute | solution.py:16
  20.9 5.6 %collective-permute-start.9 = (bf16[512,128]{1,0:T(8,128)(2,1)S(1)}, bf16[512,128]{1,0:T(8,128)(2,1)S(1)}, u32[]{:S(2)}, u32[]{:S(2)}) collective-permute-start(bf16[512,128]{1,0:T(8,128)(2,1)S(1)} %shard_map.142.total), channel_id=1, source_target_pairs={{0,2},{1,3},{2,0},{3,1},{4,6},{5,7},{6,4},{7,5},{8,10},{9,11},{10,... | collective-permute-start | bytes 393224 | tf_op jit(solution)/shard_map/ppermute | solution.py:16
  27.1 1.4 %collective-permute-start.10 = (bf16[512,128]{1,0:T(8,128)(2,1)S(1)}, bf16[512,128]{1,0:T(8,128)(2,1)S(1)}, u32[]{:S(2)}, u32[]{:S(2)}) collective-permute-start(bf16[512,128]{1,0:T(8,128)(2,1)S(1)} %get-tuple-element.65.refs_4_), channel_id=1, source_target_pairs={{0,1},{1,0},{2,3},{3,2},{4,5},{5,4},{6,7},{7,6},{8,9},{9,8},{10,11... | collective-permute-start | bytes 393224 | tf_op jit(solution)/shard_map/ppermute | solution.py:16
  27.5 2.2 %collective-permute-start.17 = (f32[144,256]{1,0:T(8,128)S(1)}, f32[144,256]{1,0:T(8,128)S(1)}, u32[]{:S(2)}, u32[]{:S(2)}) collective-permute-start(f32[144,256]{1,0:T(8,128)S(1)} %get-tuple-element.83), channel_id=1, source_target_pairs={{0,1},{1,0},{2,3},{3,2},{4,5},{5,4},{6,7},{7,6},{8,9},{9,8},{10,11... | collective-permute-start | bytes 442376 | tf_op jit(solution)/shard_map/ppermute | solution.py:16
  28.9 12.2 %collective-permute-start.11 = (bf16[512,128]{1,0:T(8,128)(2,1)S(1)}, bf16[512,128]{1,0:T(8,128)(2,1)S(1)}, u32[]{:S(2)}, u32[]{:S(2)}) collective-permute-start(bf16[512,128]{1,0:T(8,128)(2,1)S(1)} %get-tuple-element.72), channel_id=1, source_target_pairs={{0,4},{4,0},{8,12},{12,8},{16,20},{20,16},{24,28},{28,24},{1,5},{5... | collective-permute-start | bytes 393224 | tf_op jit(solution)/shard_map/ppermute | solution.py:16
  29.7 6.9 %collective-permute-start.18 = (bf16[144,256]{1,0:T(8,128)(2,1)S(1)}, bf16[144,256]{1,0:T(8,128)(2,1)S(1)}, u32[]{:S(2)}, u32[]{:S(2)}) collective-permute-start(bf16[144,256]{1,0:T(8,128)(2,1)S(1)} %shard_map.152.kept), channel_id=1, source_target_pairs={{0,16},{4,20},{8,24},{12,28},{16,0},{20,4},{24,8},{28,12},{1,17},{... | collective-permute-start | bytes 221192 | tf_op jit(solution)/shard_map/ppermute | solution.py:16
  31.5 6.0 %collective-permute-start.12 = (bf16[256,128]{1,0:T(8,128)(2,1)S(1)}, bf16[256,128]{1,0:T(8,128)(2,1)S(1)}, u32[]{:S(2)}, u32[]{:S(2)}) collective-permute-start(bf16[256,128]{1,0:T(8,128)(2,1)S(1)} %get-tuple-element.70), channel_id=1, source_target_pairs={{0,4},{4,0},{8,12},{12,8},{16,20},{20,16},{24,28},{28,24},{1,5},{5... | collective-permute-start | bytes 196616 | tf_op jit(solution)/shard_map/ppermute | solution.py:16
  32.5 8.2 %collective-permute-start.14 = (bf16[256,128]{1,0:T(8,128)(2,1)S(1)}, bf16[256,128]{1,0:T(8,128)(2,1)S(1)}, u32[]{:S(2)}, u32[]{:S(2)}) collective-permute-start(bf16[256,128]{1,0:T(8,128)(2,1)S(1)} %get-tuple-element.71), channel_id=1, source_target_pairs={{0,4},{4,0},{8,12},{12,8},{16,20},{20,16},{24,28},{28,24},{1,5},{5... | collective-permute-start | bytes 196616 | tf_op jit(solution)/shard_map/ppermute | solution.py:16
  36.6 5.5 %collective-permute-start.19 = (bf16[144,256]{1,0:T(8,128)(2,1)S(1)}, bf16[144,256]{1,0:T(8,128)(2,1)S(1)}, u32[]{:S(2)}, u32[]{:S(2)}) collective-permute-start(bf16[144,256]{1,0:T(8,128)(2,1)S(1)} %shard_map.153.kept), channel_id=1, source_target_pairs={{0,8},{4,12},{8,0},{12,4},{16,24},{20,28},{24,16},{28,20},{1,9},{5... | collective-permute-start | bytes 221192 | tf_op jit(solution)/shard_map/ppermute | solution.py:16
  37.5 6.7 %collective-permute-start.13 = (bf16[256,128]{1,0:T(8,128)(2,1)S(1)}, bf16[256,128]{1,0:T(8,128)(2,1)S(1)}, u32[]{:S(2)}, u32[]{:S(2)}) collective-permute-start(bf16[256,128]{1,0:T(8,128)(2,1)S(1)} %shard_map.147.refs_0_), channel_id=1, source_target_pairs={{0,24},{4,28},{8,16},{12,20},{16,8},{20,12},{24,0},{28,4},{1,25},{... | collective-permute-start | bytes 196616 | tf_op jit(solution)/shard_map/ppermute | solution.py:16
  40.7 6.0 %collective-permute-start.15 = (bf16[256,128]{1,0:T(8,128)(2,1)S(1)}, bf16[256,128]{1,0:T(8,128)(2,1)S(1)}, u32[]{:S(2)}, u32[]{:S(2)}) collective-permute-start(bf16[256,128]{1,0:T(8,128)(2,1)S(1)} %shard_map.148.refs_0_), channel_id=1, source_target_pairs={{0,16},{4,20},{8,24},{12,28},{16,0},{20,4},{24,8},{28,12},{1,17},{... | collective-permute-start | bytes 196616 | tf_op jit(solution)/shard_map/ppermute | solution.py:16
  41.1 5.6 %collective-permute-start.16 = (bf16[256,128]{1,0:T(8,128)(2,1)S(1)}, bf16[256,128]{1,0:T(8,128)(2,1)S(1)}, u32[]{:S(2)}, u32[]{:S(2)}) collective-permute-start(bf16[256,128]{1,0:T(8,128)(2,1)S(1)} %shard_map.149.refs_0_), channel_id=1, source_target_pairs={{0,8},{4,12},{8,0},{12,4},{16,24},{20,28},{24,16},{28,20},{1,9},{5... | collective-permute-start | bytes 196616 | tf_op jit(solution)/shard_map/ppermute | solution.py:16
  42.2 4.5 %collective-permute-start.20 = (bf16[144,256]{1,0:T(8,128)(2,1)S(1)}, bf16[144,256]{1,0:T(8,128)(2,1)S(1)}, u32[]{:S(2)}, u32[]{:S(2)}) collective-permute-start(bf16[144,256]{1,0:T(8,128)(2,1)S(1)} %shard_map.154.kept), channel_id=1, source_target_pairs={{0,4},{4,0},{8,12},{12,8},{16,20},{20,16},{24,28},{28,24},{1,5},{5... | collective-permute-start | bytes 221192 | tf_op jit(solution)/shard_map/ppermute | solution.py:16
  46.8 1.4 %collective-permute-start.21 = (f32[128,256]{1,0:T(8,128)S(1)}, f32[128,256]{1,0:T(8,128)S(1)}, u32[]{:S(2)}, u32[]{:S(2)}) collective-permute-start(f32[128,256]{1,0:T(8,128)S(1)} %slice.4), channel_id=1, source_target_pairs={{0,1},{1,0},{2,3},{3,2},{4,5},{5,4},{6,7},{7,6},{8,9},{9,8},{10,11... | collective-permute-start | bytes 393224 | tf_op jit(solution)/shard_map/ppermute | solution.py:16

commit v4 on v3

--- a/solution.py
+++ b/solution.py
@@ -531,7 +531,7 @@
     back = [swap(pair, "loop", m) for m, pair in zip(far_first, pairs)]
     mask = loop_count // 4
     while mask:
-        sent_w = added(sent_w, arrived_w, *(pairs[2:3] if mask == 1 else []))
+        sent_w = added(sent_w, arrived_w, *(pairs[2:3] if mask == 1 else kept[:1]))
         arrived_w = swap(sent_w, "loop", mask)
         mask //= 2
     sent_w = added(sent_w, arrived_w, token(back, 12_000_000_000), dtype=jnp.float32)

time: 49.1 us -> 48.5 us (0.988)
  waiting for transfers between devices: 15.4 us -> 14.2 us
  starting transfers between devices: 24.1 us -> 24.7 us
    ppermute x22, waiting for transfers between devices: 15.4 us -> 14.2 us  [swap(): lax.ppermute(block, axis, [(i, i ^ mask) for i in range(lax.axis_size(axi...]
    ppermute x22, starting transfers between devices: 24.1 us -> 24.7 us  [swap(): lax.ppermute(block, axis, [(i, i ^ mask) for i in range(lax.axis_size(axi...]
where the time goes in v4:
time: 48.5 us; the launch traced here: 48.2 us
  starting transfers between devices  24.7 us (51%)
  waiting for transfers between devices  14.2 us (29%)
  Pallas kernels  8.43 us (17%)
  between operations  0.83 us (2%)
    ppermute x22, starting transfers between devices, swap(): lax.ppermute(block, axis, [(i, i ^ mask) for i in range(lax.axis_size(axi...  24.7 us
    ppermute x22, waiting for transfers between devices, swap(): lax.ppermute(block, axis, [(i, i ^ mask) for i in range(lax.axis_size(axi...  14.2 us
    pallas_call x18, Pallas kernels, call(): pl.pallas_call(kernel, out_shape=list(out_shape), in_specs=in_specs, out_...  3.92 us
    pallas_call x1, Pallas kernels, place(): pl.pallas_call(functools.partial(place_kernel, near_count, masks, rep_cou...  2.97 us
  transfers between devices with their start and end apart: 22, of which 10 were waited for; matrix products, arithmetic and copies ran while one was open for 0% of the time, Pallas kernels for 15%

profile of v4, /device:TPU:0, one launch (start us, length us, event | category | flops | bytes accessed | tf_op | source)
XLA Modules:
  0.0 48.2 jit_solution(9965979187579308476)
XLA Ops:
  0.6 5.1 %collective-permute-start.2 = (bf16[256,128]{1,0:T(8,128)(2,1)}, bf16[256,128]{1,0:T(8,128)(2,1)S(1)}, u32[]{:S(2)}, u32[]{:S(2)}) collective-permute-start(bf16[256,128]{1,0:T(8,128)(2,1)} %refs_9_.1), channel_id=1, source_target_pairs={{0,24},{4,28},{8,16},{12,20},{16,8},{20,12},{24,0},{28,4},{1,25},{... | collective-permute-start | bytes 196616 | tf_op jit(solution)/shard_map/ppermute | solution.py:16
  5.8 0.0 collective-permute-start.1
  5.8 0.6 %collective-permute-start = (bf16[256,128]{1,0:T(8,128)(2,1)}, bf16[256,128]{1,0:T(8,128)(2,1)S(1)}, u32[]{:S(2)}, u32[]{:S(2)}) collective-permute-start(bf16[256,128]{1,0:T(8,128)(2,1)} %refs_9_.1), channel_id=1, source_target_pairs={{0,8},{4,12},{8,0},{12,4},{16,24},{20,28},{24,16},{28,20},{1,9},{5... | collective-permute-start | bytes 196616 | tf_op jit(solution)/shard_map/ppermute | solution.py:16
  6.4 1.7 %collective-permute-start.3 = (bf16[256,128]{1,0:T(8,128)(2,1)}, bf16[256,128]{1,0:T(8,128)(2,1)S(1)}, u32[]{:S(2)}, u32[]{:S(2)}) collective-permute-start(bf16[256,128]{1,0:T(8,128)(2,1)} %refs_9_.1), channel_id=1, source_target_pairs={{0,4},{4,0},{8,12},{12,8},{16,20},{20,16},{24,28},{28,24},{1,5},{5... | collective-permute-start | bytes 196616 | tf_op jit(solution)/shard_map/ppermute | solution.py:16
  8.1 3.0 %shard_map.137 = (bf16[1024,256]{1,0:T(8,128)(2,1)S(1)}, bf16[1024,256]{1,0:T(8,128)(2,1)S(1)}, bf16[1024,256]{1,0:T(8,128)(2,1)S(1)}, bf16[1024,256]{1,0:T(8,12...) custom-call(s32[8,16]{1,0:T(8,128)} %bitcast.9, ...), custom_call_target="tpu_custom_call" | custom-call | bytes 8388608 | tf_op jit(solution)/shard_map/pallas_call | solution.py:382
  11.0 1.6 %collective-permute-start.8 = (bf16[256,512]{1,0:T(8,128)(2,1)S(1)}, bf16[256,512]{1,0:T(8,128)(2,1)S(1)}, u32[]{:S(2)}, u32[]{:S(2)}) collective-permute-start(bf16[256,512]{1,0:T(8,128)(2,1)S(1)} %get-tuple-element.63.refs_0_), channel_id=1, source_target_pairs={{0,2},{1,3},{2,0},{3,1},{4,6},{5,7},{6,4},{7,5},{8,10},{9,11},{10,... | collective-permute-start | bytes 786440 | tf_op jit(solution)/shard_map/ppermute | solution.py:16
  12.7 0.0 collective-permute-done.2.refs_6_
  12.7 0.0 collective-permute-done.1.refs_7_
  12.7 0.0 collective-permute-done.3.refs_5_
  12.7 0.4 collective-permute-start.6
  13.1 1.7 %collective-permute-start.5 = (bf16[256,128]{1,0:T(8,128)(2,1)S(1)}, bf16[256,128]{1,0:T(8,128)(2,1)S(1)}, u32[]{:S(2)}, u32[]{:S(2)}) collective-permute-start(bf16[256,128]{1,0:T(8,128)(2,1)S(1)} %collective-permute-done.1.refs_7_), channel_id=1, source_target_pairs={{0,4},{4,0},{8,12},{12,8},{16,20},{20,16},{24,28},{28,24},{1,5},{5... | collective-permute-start | bytes 196616 | tf_op jit(solution)/shard_map/ppermute | solution.py:16
  14.8 0.3 collective-permute-start.4
  15.1 0.9 %shard_map.138.so_far = f32[1024,128]{1,0:T(8,128)S(1)} custom-call(bf16[1024,256]{1,0:T(8,128)(2,1)S(1)} %get-tuple-element.57.refs_0_.refs_3_, bf16[1024,256]{1,0:T(8,128)(2,1)S(1)} %get-tuple-element.46.refs_1_.refs_0_, bf16[1024,256]{1,0:T(8,128)(2,1)S(1)} %get-tuple-element.47.refs_2_.refs_1_, bf16[1024,256]{1,0:T(8,128)(2,1)S(1)} %get-tuple-element.48.refs_3_.refs_2_, ...), custom_call_target="tpu_custom_call" | custom-call | flops 335544320 | tf_op jit(solution)/shard_map/pallas_call | solution.py:415
  16.0 1.4 %collective-permute-done.6.panel = bf16[256,128]{1,0:T(8,128)(2,1)S(1)} collective-permute-done((bf16[256,128]{1,0:T(8,128)(2,1)S(1)}, bf16[256,128]{1,0:T(8,128)(2,1)S(1)}, u32[]{:S(2)}, u32[]{:S(2)}) %collective-permute-start.6) | collective-permute-done | bytes 65568 | tf_op jit(solution)/shard_map/ppermute | solution.py:16
  17.4 0.3 shard_map.139.so_far
  17.6 0.4 collective-permute-done.5.panel
  18.1 0.3 shard_map.140.refs_2_
  18.4 0.7 %collective-permute-done.4.refs_1_ = bf16[256,128]{1,0:T(8,128)(2,1)S(1)} collective-permute-done((bf16[256,128]{1,0:T(8,128)(2,1)S(1)}, bf16[256,128]{1,0:T(8,128)(2,1)S(1)}, u32[]{:S(2)}, u32[]{:S(2)}) %collective-permute-start.4) | collective-permute-done | bytes 65568 | tf_op jit(solution)/shard_map/ppermute | solution.py:16
  19.1 0.3 shard_map.141
  19.3 0.1 collective-permute-start.7
  19.4 1.3 %collective-permute-done.7.arrived = bf16[512,128]{1,0:T(8,128)(2,1)S(1)} collective-permute-done((bf16[512,128]{1,0:T(8,128)(2,1)S(1)}, bf16[512,128]{1,0:T(8,128)(2,1)S(1)}, u32[]{:S(2)}, u32[]{:S(2)}) %collective-permute-start.7) | collective-permute-done | bytes 131104 | tf_op jit(solution)/shard_map/ppermute | solution.py:16
  20.8 1.3 %collective-permute-start.9 = (bf16[512,128]{1,0:T(8,128)(2,1)S(1)}, bf16[512,128]{1,0:T(8,128)(2,1)S(1)}, u32[]{:S(2)}, u32[]{:S(2)}) collective-permute-start(bf16[512,128]{1,0:T(8,128)(2,1)S(1)} %shard_map.142.total), channel_id=1, source_target_pairs={{0,2},{1,3},{2,0},{3,1},{4,6},{5,7},{6,4},{7,5},{8,10},{9,11},{10,... | collective-permute-start | bytes 393224 | tf_op jit(solution)/shard_map/ppermute | solution.py:16
  22.1 4.3 %collective-permute-done.9.term = bf16[512,128]{1,0:T(8,128)(2,1)S(1)} collective-permute-done((bf16[512,128]{1,0:T(8,128)(2,1)S(1)}, bf16[512,128]{1,0:T(8,128)(2,1)S(1)}, u32[]{:S(2)}, u32[]{:S(2)}) %collective-permute-start.9) | collective-permute-done | bytes 131104 | tf_op jit(solution)/shard_map/ppermute | solution.py:16
  26.4 0.5 %shard_map.143 = (bf16[256,256]{1,0:T(8,128)(2,1)S(1)}, bf16[512,256]{1,0:T(8,128)(2,1)S(1)}, bf16[512,128]{1,0:T(8,128)(2,1)S(1)}, bf16[512,128]{1,0:T(8,128)(2,1)S(1)}) custom-call(bf16[512,128]{1,0:T(8,128)(2,1)S(1)} %shard_map.142.total, bf16[512,128]{1,0:T(8,128)(2,1)S(1)} %collective-permute-done.9.term, bf16[128,256]{1,0:T(8,128)(2,1)S(1)} %copy-done.1, ...), custom_call_target="tpu_custom_call" | custom-call | flops 67108864 | bytes 1573888 | tf_op jit(solution)/shard_map/pallas_call | solution.py:25
  27.0 0.1 collective-permute-start.10
  27.0 0.3 shard_map.151
  27.3 0.6 %collective-permute-start.17 = (f32[144,256]{1,0:T(8,128)S(1)}, f32[144,256]{1,0:T(8,128)S(1)}, u32[]{:S(2)}, u32[]{:S(2)}) collective-permute-start(f32[144,256]{1,0:T(8,128)S(1)} %get-tuple-element.83), channel_id=1, source_target_pairs={{0,1},{1,0},{2,3},{3,2},{4,5},{5,4},{6,7},{7,6},{8,9},{9,8},{10,11... | collective-permute-start | bytes 442376 | tf_op jit(solution)/shard_map/ppermute | solution.py:16
  27.9 0.3 shard_map.144
  28.2 0.2 collective-permute-done.10.refs_8_.refs_5_
  28.4 0.4 shard_map.145
  28.8 0.8 %collective-permute-start.11 = (bf16[512,128]{1,0:T(8,128)(2,1)S(1)}, bf16[512,128]{1,0:T(8,128)(2,1)S(1)}, u32[]{:S(2)}, u32[]{:S(2)}) collective-permute-start(bf16[512,128]{1,0:T(8,128)(2,1)S(1)} %get-tuple-element.72), channel_id=1, source_target_pairs={{0,4},{4,0},{8,12},{12,8},{16,20},{20,16},{24,28},{28,24},{1,5},{5... | collective-permute-start | bytes 393224 | tf_op jit(solution)/shard_map/ppermute | solution.py:16
  29.6 2.1 %collective-permute-start.18 = (bf16[144,256]{1,0:T(8,128)(2,1)S(1)}, bf16[144,256]{1,0:T(8,128)(2,1)S(1)}, u32[]{:S(2)}, u32[]{:S(2)}) collective-permute-start(bf16[144,256]{1,0:T(8,128)(2,1)S(1)} %shard_map.152.kept), channel_id=1, source_target_pairs={{0,16},{4,20},{8,24},{12,28},{16,0},{20,4},{24,8},{28,12},{1,17},{... | collective-permute-start | bytes 221192 | tf_op jit(solution)/shard_map/ppermute | solution.py:16
  31.7 1.3 %collective-permute-start.12 = (bf16[256,128]{1,0:T(8,128)(2,1)S(1)}, bf16[256,128]{1,0:T(8,128)(2,1)S(1)}, u32[]{:S(2)}, u32[]{:S(2)}) collective-permute-start(bf16[256,128]{1,0:T(8,128)(2,1)S(1)} %get-tuple-element.70), channel_id=1, source_target_pairs={{0,4},{4,0},{8,12},{12,8},{16,20},{20,16},{24,28},{28,24},{1,5},{5... | collective-permute-start | bytes 196616 | tf_op jit(solution)/shard_map/ppermute | solution.py:16
  33.0 0.7 %collective-permute-start.14 = (bf16[256,128]{1,0:T(8,128)(2,1)S(1)}, bf16[256,128]{1,0:T(8,128)(2,1)S(1)}, u32[]{:S(2)}, u32[]{:S(2)}) collective-permute-start(bf16[256,128]{1,0:T(8,128)(2,1)S(1)} %get-tuple-element.71), channel_id=1, source_target_pairs={{0,4},{4,0},{8,12},{12,8},{16,20},{20,16},{24,28},{28,24},{1,5},{5... | collective-permute-start | bytes 196616 | tf_op jit(solution)/shard_map/ppermute | solution.py:16
  33.7 0.7 %shard_map.146 = (bf16[256,128]{1,0:T(8,128)(2,1)S(1)}, bf16[256,128]{1,0:T(8,128)(2,1)S(1)}, bf16[256,128]{1,0:T(8,128)(2,1)S(1)}, f32[256,128]{1,0:T(8,128)S(1)}, bf16[256,256]{1,0:T(8,128)(2,1)}) custom-call(bf16[1024,256]{1,0:T(8,128)(2,1)S(1)} %get-tuple-element.46.refs_1_.refs_0_, bf16[1024,256]{1,0:T(8,128)(2,1)S(1)} %get-tuple-element.47.refs_2_.refs_1_, ...), custom_call_target="tpu_custom_call" | custom-call | flops 268435456 | tf_op jit(solution)/shard_map/pallas_call | solution.py:502
  34.4 1.9 %collective-permute-done.18.arrived = bf16[144,256]{1,0:T(8,128)(2,1)S(1)} collective-permute-done((bf16[144,256]{1,0:T(8,128)(2,1)S(1)}, bf16[144,256]{1,0:T(8,128)(2,1)S(1)}, u32[]{:S(2)}, u32[]{:S(2)}) %collective-permute-start.18) | collective-permute-done | bytes 73760 | tf_op jit(solution)/shard_map/ppermute | solution.py:16
  36.3 0.3 collective-permute-start.19
  36.6 3.5 %collective-permute-start.13 = (bf16[256,128]{1,0:T(8,128)(2,1)S(1)}, bf16[256,128]{1,0:T(8,128)(2,1)S(1)}, u32[]{:S(2)}, u32[]{:S(2)}) collective-permute-start(bf16[256,128]{1,0:T(8,128)(2,1)S(1)} %shard_map.147.refs_0_), channel_id=1, source_target_pairs={{0,24},{4,28},{8,16},{12,20},{16,8},{20,12},{24,0},{28,4},{1,25},{... | collective-permute-start | bytes 196616 | tf_op jit(solution)/shard_map/ppermute | solution.py:16
  40.2 0.1 collective-permute-start.15
  40.3 1.2 %collective-permute-start.16 = (bf16[256,128]{1,0:T(8,128)(2,1)S(1)}, bf16[256,128]{1,0:T(8,128)(2,1)S(1)}, u32[]{:S(2)}, u32[]{:S(2)}) collective-permute-start(bf16[256,128]{1,0:T(8,128)(2,1)S(1)} %shard_map.149.refs_0_), channel_id=1, source_target_pairs={{0,8},{4,12},{8,0},{12,4},{16,24},{20,28},{24,16},{28,20},{1,9},{5... | collective-permute-start | bytes 196616 | tf_op jit(solution)/shard_map/ppermute | solution.py:16
  41.6 1.1 %collective-permute-start.20 = (bf16[144,256]{1,0:T(8,128)(2,1)S(1)}, bf16[144,256]{1,0:T(8,128)(2,1)S(1)}, u32[]{:S(2)}, u32[]{:S(2)}) collective-permute-start(bf16[144,256]{1,0:T(8,128)(2,1)S(1)} %shard_map.154.kept), channel_id=1, source_target_pairs={{0,4},{4,0},{8,12},{12,8},{16,20},{20,16},{24,28},{28,24},{1,5},{5... | collective-permute-start | bytes 221192 | tf_op jit(solution)/shard_map/ppermute | solution.py:16
  42.7 0.3 collective-permute-done.13.refs_0_
  43.0 3.0 %collective-permute-done.15.refs_1_ = bf16[256,128]{1,0:T(8,128)(2,1)S(1)} collective-permute-done((bf16[256,128]{1,0:T(8,128)(2,1)S(1)}, bf16[256,128]{1,0:T(8,128)(2,1)S(1)}, u32[]{:S(2)}, u32[]{:S(2)}) %collective-permute-start.15) | collective-permute-done | bytes 65568 | tf_op jit(solution)/shard_map/ppermute | solution.py:16
  46.0 0.0 collective-permute-done.20.arrived
  46.0 0.1 collective-permute-start.21
  46.1 0.7 %shard_map.150 = bf16[256,128]{1,0:T(8,128)(2,1)} custom-call(f32[256,128]{1,0:T(8,128)S(1)} %get-tuple-element.77.own, bf16[512,128]{1,0:T(8,128)(2,1)S(1)} %collective-permute-done.11.message, bf16[256,128]{1,0:T(8,128)(2,1)S(1)} %collective-permute-done.13.refs_0_, bf16[256,128]{1,0:T(8,128)(2,1)S(1)} %collective-permute-done.15.refs_1_, ...), custom_call_target="tpu_custom_call" | custom-call | bytes 524288 | tf_op jit(solution)/shard_map/pallas_call | solution.py:25
  46.8 0.7 %collective-permute-done.21.other = f32[128,256]{1,0:T(8,128)S(1)} collective-permute-done((f32[128,256]{1,0:T(8,128)S(1)}, f32[128,256]{1,0:T(8,128)S(1)}, u32[]{:S(2)}, u32[]{:S(2)}) %collective-permute-start.21) | collective-permute-done | bytes 131104 | tf_op jit(solution)/shard_map/ppermute | solution.py:16
  47.4 0.7 %shard_map.157 = (f32[128,256]{1,0:T(8,128)}, f32[128,256]{1,0:T(8,128)}, f32[1,256]{1,0:T(1,128)}) custom-call(f32[144,256]{1,0:T(8,128)S(1)} %shard_map.156.weights, f32[128,256]{1,0:T(8,128)S(1)} %collective-permute-done.21.other), custom_call_target="tpu_custom_call" | custom-call | bytes 541696 | tf_op jit(solution)/shard_map/pallas_call | solution.py:25
  (26 shorter events, 0.2 us)
Async XLA Ops:
  0.6 14.5 %copy-start = (bf16[256,128]{1,0:T(8,128)(2,1)S(1)}, bf16[256,128]{1,0:T(8,128)(2,1)}, u32[]{:S(2)}) copy-start(bf16[256,128]{1,0:T(8,128)(2,1)} %refs_9_.1) | copy-start | bytes 196612
  0.6 12.0 %collective-permute-start.2 = (bf16[256,128]{1,0:T(8,128)(2,1)}, bf16[256,128]{1,0:T(8,128)(2,1)S(1)}, u32[]{:S(2)}, u32[]{:S(2)}) collective-permute-start(bf16[256,128]{1,0:T(8,128)(2,1)} %refs_9_.1), channel_id=1, source_target_pairs={{0,24},{4,28},{8,16},{12,20},{16,8},{20,12},{24,0},{28,4},{1,25},{... | collective-permute-start | bytes 196616 | tf_op jit(solution)/shard_map/ppermute | solution.py:16
  5.8 6.9 %collective-permute-start.1 = (bf16[256,128]{1,0:T(8,128)(2,1)}, bf16[256,128]{1,0:T(8,128)(2,1)S(1)}, u32[]{:S(2)}, u32[]{:S(2)}) collective-permute-start(bf16[256,128]{1,0:T(8,128)(2,1)} %refs_9_.1), channel_id=1, source_target_pairs={{0,16},{4,20},{8,24},{12,28},{16,0},{20,4},{24,8},{28,12},{1,17},{... | collective-permute-start | bytes 196616 | tf_op jit(solution)/shard_map/ppermute | solution.py:16
  5.8 6.9 %collective-permute-start = (bf16[256,128]{1,0:T(8,128)(2,1)}, bf16[256,128]{1,0:T(8,128)(2,1)S(1)}, u32[]{:S(2)}, u32[]{:S(2)}) collective-permute-start(bf16[256,128]{1,0:T(8,128)(2,1)} %refs_9_.1), channel_id=1, source_target_pairs={{0,8},{4,12},{8,0},{12,4},{16,24},{20,28},{24,16},{28,20},{1,9},{5... | collective-permute-start | bytes 196616 | tf_op jit(solution)/shard_map/ppermute | solution.py:16
  6.4 6.3 %collective-permute-start.3 = (bf16[256,128]{1,0:T(8,128)(2,1)}, bf16[256,128]{1,0:T(8,128)(2,1)S(1)}, u32[]{:S(2)}, u32[]{:S(2)}) collective-permute-start(bf16[256,128]{1,0:T(8,128)(2,1)} %refs_9_.1), channel_id=1, source_target_pairs={{0,4},{4,0},{8,12},{12,8},{16,20},{20,16},{24,28},{28,24},{1,5},{5... | collective-permute-start | bytes 196616 | tf_op jit(solution)/shard_map/ppermute | solution.py:16
  11.0 9.7 %collective-permute-start.8 = (bf16[256,512]{1,0:T(8,128)(2,1)S(1)}, bf16[256,512]{1,0:T(8,128)(2,1)S(1)}, u32[]{:S(2)}, u32[]{:S(2)}) collective-permute-start(bf16[256,512]{1,0:T(8,128)(2,1)S(1)} %get-tuple-element.63.refs_0_), channel_id=1, source_target_pairs={{0,2},{1,3},{2,0},{3,1},{4,6},{5,7},{6,4},{7,5},{8,10},{9,11},{10,... | collective-permute-start | bytes 786440 | tf_op jit(solution)/shard_map/ppermute | solution.py:16
  12.7 4.7 %collective-permute-start.6 = (bf16[256,128]{1,0:T(8,128)(2,1)S(1)}, bf16[256,128]{1,0:T(8,128)(2,1)S(1)}, u32[]{:S(2)}, u32[]{:S(2)}) collective-permute-start(bf16[256,128]{1,0:T(8,128)(2,1)S(1)} %collective-permute-done.refs_8_), channel_id=1, source_target_pairs={{0,4},{4,0},{8,12},{12,8},{16,20},{20,16},{24,28},{28,24},{1,5},{5... | collective-permute-start | bytes 196616 | tf_op jit(solution)/shard_map/ppermute | solution.py:16
  13.1 5.0 %collective-permute-start.5 = (bf16[256,128]{1,0:T(8,128)(2,1)S(1)}, bf16[256,128]{1,0:T(8,128)(2,1)S(1)}, u32[]{:S(2)}, u32[]{:S(2)}) collective-permute-start(bf16[256,128]{1,0:T(8,128)(2,1)S(1)} %collective-permute-done.1.refs_7_), channel_id=1, source_target_pairs={{0,4},{4,0},{8,12},{12,8},{16,20},{20,16},{24,28},{28,24},{1,5},{5... | collective-permute-start | bytes 196616 | tf_op jit(solution)/shard_map/ppermute | solution.py:16
  14.8 4.3 %collective-permute-start.4 = (bf16[256,128]{1,0:T(8,128)(2,1)S(1)}, bf16[256,128]{1,0:T(8,128)(2,1)S(1)}, u32[]{:S(2)}, u32[]{:S(2)}) collective-permute-start(bf16[256,128]{1,0:T(8,128)(2,1)S(1)} %collective-permute-done.2.refs_6_), channel_id=1, source_target_pairs={{0,4},{4,0},{8,12},{12,8},{16,20},{20,16},{24,28},{28,24},{1,5},{5... | collective-permute-start | bytes 196616 | tf_op jit(solution)/shard_map/ppermute | solution.py:16
  15.1 11.3 %copy-start.1 = (bf16[128,256]{1,0:T(8,128)(2,1)S(1)}, bf16[128,256]{1,0:T(8,128)(2,1)}, u32[]{:S(2)}) copy-start(bf16[128,256]{1,0:T(8,128)(2,1)} %refs_7_.1) | copy-start | bytes 196612
  15.1 11.3 %copy-start.2 = (bf16[128,256]{1,0:T(8,128)(2,1)S(1)}, bf16[128,256]{1,0:T(8,128)(2,1)}, u32[]{:S(2)}) copy-start(bf16[128,256]{1,0:T(8,128)(2,1)} %w_neigh.1) | copy-start | bytes 196612
  15.1 11.3 %copy-start.3 = (f32[256]{0:T(256)S(1)}, f32[256]{0:T(256)}, u32[]{:S(2)}) copy-start(f32[256]{0:T(256)} %param.13) | copy-start | bytes 3076
  19.3 1.4 %collective-permute-start.7 = (bf16[512,128]{1,0:T(8,128)(2,1)S(1)}, bf16[512,128]{1,0:T(8,128)(2,1)S(1)}, u32[]{:S(2)}, u32[]{:S(2)}) collective-permute-start(bf16[512,128]{1,0:T(8,128)(2,1)S(1)} %get-tuple-element.60), channel_id=1, source_target_pairs={{0,1},{1,0},{2,3},{3,2},{4,5},{5,4},{6,7},{7,6},{8,9},{9,8},{10,11... | collective-permute-start | bytes 393224 | tf_op jit(solution)/shard_map/ppermute | solution.py:16
  20.8 5.6 %collective-permute-start.9 = (bf16[512,128]{1,0:T(8,128)(2,1)S(1)}, bf16[512,128]{1,0:T(8,128)(2,1)S(1)}, u32[]{:S(2)}, u32[]{:S(2)}) collective-permute-start(bf16[512,128]{1,0:T(8,128)(2,1)S(1)} %shard_map.142.total), channel_id=1, source_target_pairs={{0,2},{1,3},{2,0},{3,1},{4,6},{5,7},{6,4},{7,5},{8,10},{9,11},{10,... | collective-permute-start | bytes 393224 | tf_op jit(solution)/shard_map/ppermute | solution.py:16
  27.0 1.4 %collective-permute-start.10 = (bf16[512,128]{1,0:T(8,128)(2,1)S(1)}, bf16[512,128]{1,0:T(8,128)(2,1)S(1)}, u32[]{:S(2)}, u32[]{:S(2)}) collective-permute-start(bf16[512,128]{1,0:T(8,128)(2,1)S(1)} %get-tuple-element.65.refs_4_), channel_id=1, source_target_pairs={{0,1},{1,0},{2,3},{3,2},{4,5},{5,4},{6,7},{7,6},{8,9},{9,8},{10,11... | collective-permute-start | bytes 393224 | tf_op jit(solution)/shard_map/ppermute | solution.py:16
  27.3 2.2 %collective-permute-start.17 = (f32[144,256]{1,0:T(8,128)S(1)}, f32[144,256]{1,0:T(8,128)S(1)}, u32[]{:S(2)}, u32[]{:S(2)}) collective-permute-start(f32[144,256]{1,0:T(8,128)S(1)} %get-tuple-element.83), channel_id=1, source_target_pairs={{0,1},{1,0},{2,3},{3,2},{4,5},{5,4},{6,7},{7,6},{8,9},{9,8},{10,11... | collective-permute-start | bytes 442376 | tf_op jit(solution)/shard_map/ppermute | solution.py:16
  28.8 11.5 %collective-permute-start.11 = (bf16[512,128]{1,0:T(8,128)(2,1)S(1)}, bf16[512,128]{1,0:T(8,128)(2,1)S(1)}, u32[]{:S(2)}, u32[]{:S(2)}) collective-permute-start(bf16[512,128]{1,0:T(8,128)(2,1)S(1)} %get-tuple-element.72), channel_id=1, source_target_pairs={{0,4},{4,0},{8,12},{12,8},{16,20},{20,16},{24,28},{28,24},{1,5},{5... | collective-permute-start | bytes 393224 | tf_op jit(solution)/shard_map/ppermute | solution.py:16
  29.6 6.8 %collective-permute-start.18 = (bf16[144,256]{1,0:T(8,128)(2,1)S(1)}, bf16[144,256]{1,0:T(8,128)(2,1)S(1)}, u32[]{:S(2)}, u32[]{:S(2)}) collective-permute-start(bf16[144,256]{1,0:T(8,128)(2,1)S(1)} %shard_map.152.kept), channel_id=1, source_target_pairs={{0,16},{4,20},{8,24},{12,28},{16,0},{20,4},{24,8},{28,12},{1,17},{... | collective-permute-start | bytes 221192 | tf_op jit(solution)/shard_map/ppermute | solution.py:16
  31.7 4.9 %collective-permute-start.12 = (bf16[256,128]{1,0:T(8,128)(2,1)S(1)}, bf16[256,128]{1,0:T(8,128)(2,1)S(1)}, u32[]{:S(2)}, u32[]{:S(2)}) collective-permute-start(bf16[256,128]{1,0:T(8,128)(2,1)S(1)} %get-tuple-element.70), channel_id=1, source_target_pairs={{0,4},{4,0},{8,12},{12,8},{16,20},{20,16},{24,28},{28,24},{1,5},{5... | collective-permute-start | bytes 196616 | tf_op jit(solution)/shard_map/ppermute | solution.py:16
  33.0 7.2 %collective-permute-start.14 = (bf16[256,128]{1,0:T(8,128)(2,1)S(1)}, bf16[256,128]{1,0:T(8,128)(2,1)S(1)}, u32[]{:S(2)}, u32[]{:S(2)}) collective-permute-start(bf16[256,128]{1,0:T(8,128)(2,1)S(1)} %get-tuple-element.71), channel_id=1, source_target_pairs={{0,4},{4,0},{8,12},{12,8},{16,20},{20,16},{24,28},{28,24},{1,5},{5... | collective-permute-start | bytes 196616 | tf_op jit(solution)/shard_map/ppermute | solution.py:16
  36.3 5.2 %collective-permute-start.19 = (bf16[144,256]{1,0:T(8,128)(2,1)S(1)}, bf16[144,256]{1,0:T(8,128)(2,1)S(1)}, u32[]{:S(2)}, u32[]{:S(2)}) collective-permute-start(bf16[144,256]{1,0:T(8,128)(2,1)S(1)} %shard_map.153.kept), channel_id=1, source_target_pairs={{0,8},{4,12},{8,0},{12,4},{16,24},{20,28},{24,16},{28,20},{1,9},{5... | collective-permute-start | bytes 221192 | tf_op jit(solution)/shard_map/ppermute | solution.py:16
  36.6 6.3 %collective-permute-start.13 = (bf16[256,128]{1,0:T(8,128)(2,1)S(1)}, bf16[256,128]{1,0:T(8,128)(2,1)S(1)}, u32[]{:S(2)}, u32[]{:S(2)}) collective-permute-start(bf16[256,128]{1,0:T(8,128)(2,1)S(1)} %shard_map.147.refs_0_), channel_id=1, source_target_pairs={{0,24},{4,28},{8,16},{12,20},{16,8},{20,12},{24,0},{28,4},{1,25},{... | collective-permute-start | bytes 196616 | tf_op jit(solution)/shard_map/ppermute | solution.py:16
  40.2 5.8 %collective-permute-start.15 = (bf16[256,128]{1,0:T(8,128)(2,1)S(1)}, bf16[256,128]{1,0:T(8,128)(2,1)S(1)}, u32[]{:S(2)}, u32[]{:S(2)}) collective-permute-start(bf16[256,128]{1,0:T(8,128)(2,1)S(1)} %shard_map.148.refs_0_), channel_id=1, source_target_pairs={{0,16},{4,20},{8,24},{12,28},{16,0},{20,4},{24,8},{28,12},{1,17},{... | collective-permute-start | bytes 196616 | tf_op jit(solution)/shard_map/ppermute | solution.py:16
  40.3 5.6 %collective-permute-start.16 = (bf16[256,128]{1,0:T(8,128)(2,1)S(1)}, bf16[256,128]{1,0:T(8,128)(2,1)S(1)}, u32[]{:S(2)}, u32[]{:S(2)}) collective-permute-start(bf16[256,128]{1,0:T(8,128)(2,1)S(1)} %shard_map.149.refs_0_), channel_id=1, source_target_pairs={{0,8},{4,12},{8,0},{12,4},{16,24},{20,28},{24,16},{28,20},{1,9},{5... | collective-permute-start | bytes 196616 | tf_op jit(solution)/shard_map/ppermute | solution.py:16
  41.6 4.4 %collective-permute-start.20 = (bf16[144,256]{1,0:T(8,128)(2,1)S(1)}, bf16[144,256]{1,0:T(8,128)(2,1)S(1)}, u32[]{:S(2)}, u32[]{:S(2)}) collective-permute-start(bf16[144,256]{1,0:T(8,128)(2,1)S(1)} %shard_map.154.kept), channel_id=1, source_target_pairs={{0,4},{4,0},{8,12},{12,8},{16,20},{20,16},{24,28},{28,24},{1,5},{5... | collective-permute-start | bytes 221192 | tf_op jit(solution)/shard_map/ppermute | solution.py:16
  46.0 1.4 %collective-permute-start.21 = (f32[128,256]{1,0:T(8,128)S(1)}, f32[128,256]{1,0:T(8,128)S(1)}, u32[]{:S(2)}, u32[]{:S(2)}) collective-permute-start(f32[128,256]{1,0:T(8,128)S(1)} %slice.4), channel_id=1, source_target_pairs={{0,1},{1,0},{2,3},{3,2},{4,5},{5,4},{6,7},{7,6},{8,9},{9,8},{10,11... | collective-permute-start | bytes 393224 | tf_op jit(solution)/shard_map/ppermute | solution.py:16

commit v5 on v4

--- a/solution.py
+++ b/solution.py
@@ -62,11 +62,11 @@
     sub_bits = sub_blocks.bit_length() - 1
     moves = [(dst_far, dst), (src_far, src), (live_far, live)]
     if packs:
-        width = sides[0].shape[1]
+        rows, width = sides[0].shape
         moves += [
             (sides[1], degree),
-            (sides[0], bundle.at[:, pl.ds(0, width)]),
-            (sides[2], bundle.at[:, pl.ds(2 * width, bundle.shape[1] - 2 * width)]),
+            (sides[0], bundle.at[pl.ds(0, rows), pl.ds(0, width)]),
+            (sides[2], bundle.at[pl.ds(0, rows), pl.ds(width, bundle.shape[1] - width)]),
         ]
     moves = [pltpu.make_async_copy(far, near, read.at[k]) for k, (far, near) in enumerate(moves)]
     for move in moves:
@@ -100,8 +100,8 @@
     if packs:
         for move in moves[3:]:
             move.wait()
-        degree_f = jnp.broadcast_to(degree[...].astype(jnp.float32), (width, bundle.shape[0]))
-        bundle[:, width : 2 * width] = degree_f.T.astype(jnp.bfloat16)
+        degree_rows = jnp.broadcast_to(degree[...].astype(jnp.float32), (16, rows))
+        bundle[rows:, :rows] = degree_rows.astype(jnp.bfloat16)
     for k in backward:
 
         def finish(slot, carry):
@@ -184,15 +184,16 @@
     flip, total, term, w_self, w_neigh, bias, *refs
 ):
     bundles, (output, grad_pre, aggregate, grad_agg) = refs[:-4], refs[-4:]
-    row_count, width = bundles[0].shape[0], w_neigh.shape[0]
+    row_count, width = bundles[0].shape[0] - 16, w_neigh.shape[0]
     for j, bundle in enumerate(bundles):
         rows = slice(j * row_count, (j + 1) * row_count)
         there = slice((j ^ flip) * row_count, ((j ^ flip) + 1) * row_count)
-        degree_f = bundle[:, width : width + 1].astype(jnp.float32)
+        degree_row = bundle[row_count : row_count + 1, :row_count].astype(jnp.float32)
+        degree_f = jnp.broadcast_to(degree_row, (width, row_count)).T[:, :1]
         agg = (
             (total[rows, :].astype(jnp.float32) + term[there, :].astype(jnp.float32)) / degree_f
         ).astype(jnp.bfloat16)
-        features = bundle[:, :width]
+        features = bundle[:row_count, :width]
         preact = (
             jnp.dot(
                 jnp.concatenate([features, agg], axis=1),
@@ -203,7 +204,7 @@
         )
         sigmoid_val = jax.nn.sigmoid(preact)
         grad = (
-            bundle[:, 2 * width :].astype(jnp.float32)
+            bundle[:row_count, width:].astype(jnp.float32)
             * sigmoid_val
             * (1.0 + preact * (1.0 - sigmoid_val))
         ).astype(jnp.bfloat16)
@@ -219,7 +220,7 @@
 
 def weight_kernel(scale, aggregate, grad_pre, *refs):
     bundles, (keep, send) = refs[:-2], refs[-2:]
-    row_count, width = bundles[0].shape[0], aggregate.shape[1]
+    row_count, width = bundles[0].shape[0] - 16, aggregate.shape[1]
     parts = []
     for j, bundle in enumerate(bundles):
         rows = slice(j * row_count, (j + 1) * row_count)
@@ -228,7 +229,7 @@
             lax.dot_general(
                 a, grad, (((0,), (0,)), ((), ())), preferred_element_type=jnp.float32
             )
-            for a in (bundle[:, :width], aggregate[rows, :])
+            for a in (bundle[:row_count, :width], aggregate[rows, :])
         ]
         parts.append((*grads, jnp.sum(grad.astype(jnp.float32), axis=0, keepdims=True)))
     while len(parts) > 1:
@@ -377,7 +378,7 @@
     def place(masks, far, packs):
         near_count = 0 if far else len(masks)
         kind = pltpu.HBM if far else jax.ShapeDtypeStruct
-        bundle = [bf16((row_count, 2 * feat_width + hidden))] if packs else []
+        bundle = [bf16((row_count + 16, feat_width + hidden))] if packs else []
         operands = graph + sides if packs else graph
         placed = pl.pallas_call(
             functools.partial(place_kernel, near_count, masks, rep_count, sub_blocks, packs),

time: 48.5 us -> 48.6 us (level)
  transfers between devices with their start and end apart: 22 -> 22, of which waited for: 10 -> 11; matrix products, arithmetic and copies ran while one was open for 0% -> 0% of each run, Pallas kernels for 15% -> 15%
where the time goes in v5:
time: 48.6 us; the launch traced here: 48.3 us
  starting transfers between devices  24.6 us (51%)
  waiting for transfers between devices  14.4 us (30%)
  Pallas kernels  8.53 us (18%)
  between operations  0.82 us (2%)
    ppermute x22, starting transfers between devices, swap(): lax.ppermute(block, axis, [(i, i ^ mask) for i in range(lax.axis_size(axi...  24.6 us
    ppermute x22, waiting for transfers between devices, swap(): lax.ppermute(block, axis, [(i, i ^ mask) for i in range(lax.axis_size(axi...  14.4 us
    pallas_call x18, Pallas kernels, call(): pl.pallas_call(kernel, out_shape=list(out_shape), in_specs=in_specs, out_...  4.07 us
    pallas_call x1, Pallas kernels, place(): pl.pallas_call(functools.partial(place_kernel, near_count, masks, rep_cou...  2.92 us
  transfers between devices with their start and end apart: 22, of which 11 were waited for; matrix products, arithmetic and copies ran while one was open for 0% of the time, Pallas kernels for 15%

profile of v5, /device:TPU:0, one launch (start us, length us, event | category | flops | bytes accessed | tf_op | source)
XLA Modules:
  0.0 48.3 jit_solution(14590384556589861655)
XLA Ops:
  0.6 5.1 %collective-permute-start.2 = (bf16[256,128]{1,0:T(8,128)(2,1)}, bf16[256,128]{1,0:T(8,128)(2,1)S(1)}, u32[]{:S(2)}, u32[]{:S(2)}) collective-permute-start(bf16[256,128]{1,0:T(8,128)(2,1)} %refs_9_.1), channel_id=1, source_target_pairs={{0,24},{4,28},{8,16},{12,20},{16,8},{20,12},{24,0},{28,4},{1,25},{... | collective-permute-start | bytes 196616 | tf_op jit(solution)/shard_map/ppermute | solution.py:16
  5.8 0.6 %collective-permute-start = (bf16[256,128]{1,0:T(8,128)(2,1)}, bf16[256,128]{1,0:T(8,128)(2,1)S(1)}, u32[]{:S(2)}, u32[]{:S(2)}) collective-permute-start(bf16[256,128]{1,0:T(8,128)(2,1)} %refs_9_.1), channel_id=1, source_target_pairs={{0,8},{4,12},{8,0},{12,4},{16,24},{20,28},{24,16},{28,20},{1,9},{5... | collective-permute-start | bytes 196616 | tf_op jit(solution)/shard_map/ppermute | solution.py:16
  6.4 1.7 %collective-permute-start.3 = (bf16[256,128]{1,0:T(8,128)(2,1)}, bf16[256,128]{1,0:T(8,128)(2,1)S(1)}, u32[]{:S(2)}, u32[]{:S(2)}) collective-permute-start(bf16[256,128]{1,0:T(8,128)(2,1)} %refs_9_.1), channel_id=1, source_target_pairs={{0,4},{4,0},{8,12},{12,8},{16,20},{20,16},{24,28},{28,24},{1,5},{5... | collective-permute-start | bytes 196616 | tf_op jit(solution)/shard_map/ppermute | solution.py:16
  8.1 2.9 %shard_map.137 = (bf16[1024,256]{1,0:T(8,128)(2,1)S(1)}, bf16[1024,256]{1,0:T(8,128)(2,1)S(1)}, bf16[1024,256]{1,0:T(8,128)(2,1)S(1)}, bf16[1024,256]{1,0:T(8,12...) custom-call(s32[8,16]{1,0:T(8,128)} %bitcast.9, ...), custom_call_target="tpu_custom_call" | custom-call | bytes 8388608 | tf_op jit(solution)/shard_map/pallas_call | solution.py:383
  11.0 1.8 %collective-permute-start.8 = (bf16[272,384]{1,0:T(8,128)(2,1)S(1)}, bf16[272,384]{1,0:T(8,128)(2,1)S(1)}, u32[]{:S(2)}, u32[]{:S(2)}) collective-permute-start(bf16[272,384]{1,0:T(8,128)(2,1)S(1)} %get-tuple-element.63.refs_0_), channel_id=1, source_target_pairs={{0,2},{1,3},{2,0},{3,1},{4,6},{5,7},{6,4},{7,5},{8,10},{9,11},{10,... | collective-permute-start | bytes 626696 | tf_op jit(solution)/shard_map/ppermute | solution.py:16
  12.8 0.0 collective-permute-done.2.refs_6_
  12.8 0.0 collective-permute-done.1.refs_7_
  12.8 0.0 collective-permute-done.refs_8_
  12.8 0.7 %collective-permute-start.6 = (bf16[256,128]{1,0:T(8,128)(2,1)S(1)}, bf16[256,128]{1,0:T(8,128)(2,1)S(1)}, u32[]{:S(2)}, u32[]{:S(2)}) collective-permute-start(bf16[256,128]{1,0:T(8,128)(2,1)S(1)} %collective-permute-done.refs_8_), channel_id=1, source_target_pairs={{0,4},{4,0},{8,12},{12,8},{16,20},{20,16},{24,28},{28,24},{1,5},{5... | collective-permute-start | bytes 196616 | tf_op jit(solution)/shard_map/ppermute | solution.py:16
  13.5 1.4 %collective-permute-start.5 = (bf16[256,128]{1,0:T(8,128)(2,1)S(1)}, bf16[256,128]{1,0:T(8,128)(2,1)S(1)}, u32[]{:S(2)}, u32[]{:S(2)}) collective-permute-start(bf16[256,128]{1,0:T(8,128)(2,1)S(1)} %collective-permute-done.1.refs_7_), channel_id=1, source_target_pairs={{0,4},{4,0},{8,12},{12,8},{16,20},{20,16},{24,28},{28,24},{1,5},{5... | collective-permute-start | bytes 196616 | tf_op jit(solution)/shard_map/ppermute | solution.py:16
  14.9 0.6 %collective-permute-start.4 = (bf16[256,128]{1,0:T(8,128)(2,1)S(1)}, bf16[256,128]{1,0:T(8,128)(2,1)S(1)}, u32[]{:S(2)}, u32[]{:S(2)}) collective-permute-start(bf16[256,128]{1,0:T(8,128)(2,1)S(1)} %collective-permute-done.2.refs_6_), channel_id=1, source_target_pairs={{0,4},{4,0},{8,12},{12,8},{16,20},{20,16},{24,28},{28,24},{1,5},{5... | collective-permute-start | bytes 196616 | tf_op jit(solution)/shard_map/ppermute | solution.py:16
  15.6 0.9 %shard_map.138.so_far = f32[1024,128]{1,0:T(8,128)S(1)} custom-call(bf16[1024,256]{1,0:T(8,128)(2,1)S(1)} %get-tuple-element.57.refs_0_.refs_3_, bf16[1024,256]{1,0:T(8,128)(2,1)S(1)} %get-tuple-element.46.refs_1_.refs_0_, bf16[1024,256]{1,0:T(8,128)(2,1)S(1)} %get-tuple-element.47.refs_2_.refs_1_, bf16[1024,256]{1,0:T(8,128)(2,1)S(1)} %get-tuple-element.48.refs_3_.refs_2_, ...), custom_call_target="tpu_custom_call" | custom-call | flops 335544320 | tf_op jit(solution)/shard_map/pallas_call | solution.py:416
  16.4 0.9 %collective-permute-done.6.panel = bf16[256,128]{1,0:T(8,128)(2,1)S(1)} collective-permute-done((bf16[256,128]{1,0:T(8,128)(2,1)S(1)}, bf16[256,128]{1,0:T(8,128)(2,1)S(1)}, u32[]{:S(2)}, u32[]{:S(2)}) %collective-permute-start.6) | collective-permute-done | bytes 65568 | tf_op jit(solution)/shard_map/ppermute | solution.py:16
  17.4 0.3 shard_map.139.so_far
  17.6 0.4 collective-permute-done.5.panel
  18.1 0.3 shard_map.140.refs_2_
  18.4 0.8 %collective-permute-done.4.refs_1_ = bf16[256,128]{1,0:T(8,128)(2,1)S(1)} collective-permute-done((bf16[256,128]{1,0:T(8,128)(2,1)S(1)}, bf16[256,128]{1,0:T(8,128)(2,1)S(1)}, u32[]{:S(2)}, u32[]{:S(2)}) %collective-permute-start.4) | collective-permute-done | bytes 65568 | tf_op jit(solution)/shard_map/ppermute | solution.py:16
  19.2 0.3 shard_map.141
  19.5 0.1 collective-permute-start.7
  19.5 1.3 %collective-permute-done.7.arrived = bf16[512,128]{1,0:T(8,128)(2,1)S(1)} collective-permute-done((bf16[512,128]{1,0:T(8,128)(2,1)S(1)}, bf16[512,128]{1,0:T(8,128)(2,1)S(1)}, u32[]{:S(2)}, u32[]{:S(2)}) %collective-permute-start.7) | collective-permute-done | bytes 131104 | tf_op jit(solution)/shard_map/ppermute | solution.py:16
  20.9 1.1 %collective-permute-start.9 = (bf16[512,128]{1,0:T(8,128)(2,1)S(1)}, bf16[512,128]{1,0:T(8,128)(2,1)S(1)}, u32[]{:S(2)}, u32[]{:S(2)}) collective-permute-start(bf16[512,128]{1,0:T(8,128)(2,1)S(1)} %shard_map.142.total), channel_id=1, source_target_pairs={{0,2},{1,3},{2,0},{3,1},{4,6},{5,7},{6,4},{7,5},{8,10},{9,11},{10,... | collective-permute-start | bytes 393224 | tf_op jit(solution)/shard_map/ppermute | solution.py:16
  22.1 4.5 %collective-permute-done.9.term = bf16[512,128]{1,0:T(8,128)(2,1)S(1)} collective-permute-done((bf16[512,128]{1,0:T(8,128)(2,1)S(1)}, bf16[512,128]{1,0:T(8,128)(2,1)S(1)}, u32[]{:S(2)}, u32[]{:S(2)}) %collective-permute-start.9) | collective-permute-done | bytes 131104 | tf_op jit(solution)/shard_map/ppermute | solution.py:16
  26.6 0.7 %shard_map.143 = (bf16[256,256]{1,0:T(8,128)(2,1)S(1)}, bf16[512,256]{1,0:T(8,128)(2,1)S(1)}, bf16[512,128]{1,0:T(8,128)(2,1)S(1)}, bf16[512,128]{1,0:T(8,128)(2,1)S(1)}) custom-call(bf16[512,128]{1,0:T(8,128)(2,1)S(1)} %shard_map.142.total, bf16[512,128]{1,0:T(8,128)(2,1)S(1)} %collective-permute-done.9.term, bf16[128,256]{1,0:T(8,128)(2,1)S(1)} %copy-done.1, ...), custom_call_target="tpu_custom_call" | custom-call | flops 67108864 | bytes 1467392 | tf_op jit(solution)/shard_map/pallas_call | solution.py:25
  27.2 0.1 collective-permute-start.10
  27.3 0.3 shard_map.151
  27.6 0.6 %collective-permute-start.17 = (f32[144,256]{1,0:T(8,128)S(1)}, f32[144,256]{1,0:T(8,128)S(1)}, u32[]{:S(2)}, u32[]{:S(2)}) collective-permute-start(f32[144,256]{1,0:T(8,128)S(1)} %get-tuple-element.83), channel_id=1, source_target_pairs={{0,1},{1,0},{2,3},{3,2},{4,5},{5,4},{6,7},{7,6},{8,9},{9,8},{10,11... | collective-permute-start | bytes 442376 | tf_op jit(solution)/shard_map/ppermute | solution.py:16
  28.1 0.3 shard_map.144
  28.5 0.2 collective-permute-done.10.refs_8_.refs_5_
  28.6 0.4 shard_map.145
  29.0 0.8 %collective-permute-start.11 = (bf16[512,128]{1,0:T(8,128)(2,1)S(1)}, bf16[512,128]{1,0:T(8,128)(2,1)S(1)}, u32[]{:S(2)}, u32[]{:S(2)}) collective-permute-start(bf16[512,128]{1,0:T(8,128)(2,1)S(1)} %get-tuple-element.72), channel_id=1, source_target_pairs={{0,4},{4,0},{8,12},{12,8},{16,20},{20,16},{24,28},{28,24},{1,5},{5... | collective-permute-start | bytes 393224 | tf_op jit(solution)/shard_map/ppermute | solution.py:16
  29.8 0.0 collective-permute-done.17.arrived
  29.8 2.0 %collective-permute-start.18 = (bf16[144,256]{1,0:T(8,128)(2,1)S(1)}, bf16[144,256]{1,0:T(8,128)(2,1)S(1)}, u32[]{:S(2)}, u32[]{:S(2)}) collective-permute-start(bf16[144,256]{1,0:T(8,128)(2,1)S(1)} %shard_map.152.kept), channel_id=1, source_target_pairs={{0,16},{4,20},{8,24},{12,28},{16,0},{20,4},{24,8},{28,12},{1,17},{... | collective-permute-start | bytes 221192 | tf_op jit(solution)/shard_map/ppermute | solution.py:16
  31.9 1.3 %collective-permute-start.12 = (bf16[256,128]{1,0:T(8,128)(2,1)S(1)}, bf16[256,128]{1,0:T(8,128)(2,1)S(1)}, u32[]{:S(2)}, u32[]{:S(2)}) collective-permute-start(bf16[256,128]{1,0:T(8,128)(2,1)S(1)} %get-tuple-element.70), channel_id=1, source_target_pairs={{0,4},{4,0},{8,12},{12,8},{16,20},{20,16},{24,28},{28,24},{1,5},{5... | collective-permute-start | bytes 196616 | tf_op jit(solution)/shard_map/ppermute | solution.py:16
  33.2 0.7 %collective-permute-start.14 = (bf16[256,128]{1,0:T(8,128)(2,1)S(1)}, bf16[256,128]{1,0:T(8,128)(2,1)S(1)}, u32[]{:S(2)}, u32[]{:S(2)}) collective-permute-start(bf16[256,128]{1,0:T(8,128)(2,1)S(1)} %get-tuple-element.71), channel_id=1, source_target_pairs={{0,4},{4,0},{8,12},{12,8},{16,20},{20,16},{24,28},{28,24},{1,5},{5... | collective-permute-start | bytes 196616 | tf_op jit(solution)/shard_map/ppermute | solution.py:16
  33.9 0.7 %shard_map.146 = (bf16[256,128]{1,0:T(8,128)(2,1)S(1)}, bf16[256,128]{1,0:T(8,128)(2,1)S(1)}, bf16[256,128]{1,0:T(8,128)(2,1)S(1)}, f32[256,128]{1,0:T(8,128)S(1)}, bf16[256,256]{1,0:T(8,128)(2,1)}) custom-call(bf16[1024,256]{1,0:T(8,128)(2,1)S(1)} %get-tuple-element.46.refs_1_.refs_0_, bf16[1024,256]{1,0:T(8,128)(2,1)S(1)} %get-tuple-element.47.refs_2_.refs_1_, ...), custom_call_target="tpu_custom_call" | custom-call | flops 268435456 | tf_op jit(solution)/shard_map/pallas_call | solution.py:503
  34.6 1.8 %collective-permute-done.18.arrived = bf16[144,256]{1,0:T(8,128)(2,1)S(1)} collective-permute-done((bf16[144,256]{1,0:T(8,128)(2,1)S(1)}, bf16[144,256]{1,0:T(8,128)(2,1)S(1)}, u32[]{:S(2)}, u32[]{:S(2)}) %collective-permute-start.18) | collective-permute-done | bytes 73760 | tf_op jit(solution)/shard_map/ppermute | solution.py:16
  36.4 0.1 collective-permute-start.19
  36.6 0.2 collective-permute-done.12.message
  36.8 3.0 %collective-permute-start.13 = (bf16[256,128]{1,0:T(8,128)(2,1)S(1)}, bf16[256,128]{1,0:T(8,128)(2,1)S(1)}, u32[]{:S(2)}, u32[]{:S(2)}) collective-permute-start(bf16[256,128]{1,0:T(8,128)(2,1)S(1)} %shard_map.147.refs_0_), channel_id=1, source_target_pairs={{0,24},{4,28},{8,16},{12,20},{16,8},{20,12},{24,0},{28,4},{1,25},{... | collective-permute-start | bytes 196616 | tf_op jit(solution)/shard_map/ppermute | solution.py:16
  39.9 0.3 collective-permute-start.15
  40.2 1.2 %collective-permute-start.16 = (bf16[256,128]{1,0:T(8,128)(2,1)S(1)}, bf16[256,128]{1,0:T(8,128)(2,1)S(1)}, u32[]{:S(2)}, u32[]{:S(2)}) collective-permute-start(bf16[256,128]{1,0:T(8,128)(2,1)S(1)} %shard_map.149.refs_0_), channel_id=1, source_target_pairs={{0,8},{4,12},{8,0},{12,4},{16,24},{20,28},{24,16},{28,20},{1,9},{5... | collective-permute-start | bytes 196616 | tf_op jit(solution)/shard_map/ppermute | solution.py:16
  41.5 1.2 %collective-permute-start.20 = (bf16[144,256]{1,0:T(8,128)(2,1)S(1)}, bf16[144,256]{1,0:T(8,128)(2,1)S(1)}, u32[]{:S(2)}, u32[]{:S(2)}) collective-permute-start(bf16[144,256]{1,0:T(8,128)(2,1)S(1)} %shard_map.154.kept), channel_id=1, source_target_pairs={{0,4},{4,0},{8,12},{12,8},{16,20},{20,16},{24,28},{28,24},{1,5},{5... | collective-permute-start | bytes 221192 | tf_op jit(solution)/shard_map/ppermute | solution.py:16
  42.6 0.5 %collective-permute-done.13.refs_0_ = bf16[256,128]{1,0:T(8,128)(2,1)S(1)} collective-permute-done((bf16[256,128]{1,0:T(8,128)(2,1)S(1)}, bf16[256,128]{1,0:T(8,128)(2,1)S(1)}, u32[]{:S(2)}, u32[]{:S(2)}) %collective-permute-start.13) | collective-permute-done | bytes 65568 | tf_op jit(solution)/shard_map/ppermute | solution.py:16
  43.1 3.0 %collective-permute-done.15.refs_1_ = bf16[256,128]{1,0:T(8,128)(2,1)S(1)} collective-permute-done((bf16[256,128]{1,0:T(8,128)(2,1)S(1)}, bf16[256,128]{1,0:T(8,128)(2,1)S(1)}, u32[]{:S(2)}, u32[]{:S(2)}) %collective-permute-start.15) | collective-permute-done | bytes 65568 | tf_op jit(solution)/shard_map/ppermute | solution.py:16
  46.2 0.1 collective-permute-start.21
  46.2 0.7 %shard_map.150 = bf16[256,128]{1,0:T(8,128)(2,1)} custom-call(f32[256,128]{1,0:T(8,128)S(1)} %get-tuple-element.77.own, bf16[512,128]{1,0:T(8,128)(2,1)S(1)} %collective-permute-done.11.message, bf16[256,128]{1,0:T(8,128)(2,1)S(1)} %collective-permute-done.13.refs_0_, bf16[256,128]{1,0:T(8,128)(2,1)S(1)} %collective-permute-done.15.refs_1_, ...), custom_call_target="tpu_custom_call" | custom-call | bytes 524288 | tf_op jit(solution)/shard_map/pallas_call | solution.py:25
  46.9 0.7 %collective-permute-done.21.other = f32[128,256]{1,0:T(8,128)S(1)} collective-permute-done((f32[128,256]{1,0:T(8,128)S(1)}, f32[128,256]{1,0:T(8,128)S(1)}, u32[]{:S(2)}, u32[]{:S(2)}) %collective-permute-start.21) | collective-permute-done | bytes 131104 | tf_op jit(solution)/shard_map/ppermute | solution.py:16
  47.6 0.7 %shard_map.157 = (f32[128,256]{1,0:T(8,128)}, f32[128,256]{1,0:T(8,128)}, f32[1,256]{1,0:T(1,128)}) custom-call(f32[144,256]{1,0:T(8,128)S(1)} %shard_map.156.weights, f32[128,256]{1,0:T(8,128)S(1)} %collective-permute-done.21.other), custom_call_target="tpu_custom_call" | custom-call | bytes 541696 | tf_op jit(solution)/shard_map/pallas_call | solution.py:25
  (26 shorter events, 0.2 us)
Async XLA Ops:
  0.6 14.9 %copy-start = (bf16[256,128]{1,0:T(8,128)(2,1)S(1)}, bf16[256,128]{1,0:T(8,128)(2,1)}, u32[]{:S(2)}) copy-start(bf16[256,128]{1,0:T(8,128)(2,1)} %refs_9_.1) | copy-start | bytes 196612
  0.6 12.2 %collective-permute-start.2 = (bf16[256,128]{1,0:T(8,128)(2,1)}, bf16[256,128]{1,0:T(8,128)(2,1)S(1)}, u32[]{:S(2)}, u32[]{:S(2)}) collective-permute-start(bf16[256,128]{1,0:T(8,128)(2,1)} %refs_9_.1), channel_id=1, source_target_pairs={{0,24},{4,28},{8,16},{12,20},{16,8},{20,12},{24,0},{28,4},{1,25},{... | collective-permute-start | bytes 196616 | tf_op jit(solution)/shard_map/ppermute | solution.py:16
  5.8 7.0 %collective-permute-start.1 = (bf16[256,128]{1,0:T(8,128)(2,1)}, bf16[256,128]{1,0:T(8,128)(2,1)S(1)}, u32[]{:S(2)}, u32[]{:S(2)}) collective-permute-start(bf16[256,128]{1,0:T(8,128)(2,1)} %refs_9_.1), channel_id=1, source_target_pairs={{0,16},{4,20},{8,24},{12,28},{16,0},{20,4},{24,8},{28,12},{1,17},{... | collective-permute-start | bytes 196616 | tf_op jit(solution)/shard_map/ppermute | solution.py:16
  5.8 7.0 %collective-permute-start = (bf16[256,128]{1,0:T(8,128)(2,1)}, bf16[256,128]{1,0:T(8,128)(2,1)S(1)}, u32[]{:S(2)}, u32[]{:S(2)}) collective-permute-start(bf16[256,128]{1,0:T(8,128)(2,1)} %refs_9_.1), channel_id=1, source_target_pairs={{0,8},{4,12},{8,0},{12,4},{16,24},{20,28},{24,16},{28,20},{1,9},{5... | collective-permute-start | bytes 196616 | tf_op jit(solution)/shard_map/ppermute | solution.py:16
  6.4 6.4 %collective-permute-start.3 = (bf16[256,128]{1,0:T(8,128)(2,1)}, bf16[256,128]{1,0:T(8,128)(2,1)S(1)}, u32[]{:S(2)}, u32[]{:S(2)}) collective-permute-start(bf16[256,128]{1,0:T(8,128)(2,1)} %refs_9_.1), channel_id=1, source_target_pairs={{0,4},{4,0},{8,12},{12,8},{16,20},{20,16},{24,28},{28,24},{1,5},{5... | collective-permute-start | bytes 196616 | tf_op jit(solution)/shard_map/ppermute | solution.py:16
  11.0 9.9 %collective-permute-start.8 = (bf16[272,384]{1,0:T(8,128)(2,1)S(1)}, bf16[272,384]{1,0:T(8,128)(2,1)S(1)}, u32[]{:S(2)}, u32[]{:S(2)}) collective-permute-start(bf16[272,384]{1,0:T(8,128)(2,1)S(1)} %get-tuple-element.63.refs_0_), channel_id=1, source_target_pairs={{0,2},{1,3},{2,0},{3,1},{4,6},{5,7},{6,4},{7,5},{8,10},{9,11},{10,... | collective-permute-start | bytes 626696 | tf_op jit(solution)/shard_map/ppermute | solution.py:16
  12.8 4.5 %collective-permute-start.6 = (bf16[256,128]{1,0:T(8,128)(2,1)S(1)}, bf16[256,128]{1,0:T(8,128)(2,1)S(1)}, u32[]{:S(2)}, u32[]{:S(2)}) collective-permute-start(bf16[256,128]{1,0:T(8,128)(2,1)S(1)} %collective-permute-done.refs_8_), channel_id=1, source_target_pairs={{0,4},{4,0},{8,12},{12,8},{16,20},{20,16},{24,28},{28,24},{1,5},{5... | collective-permute-start | bytes 196616 | tf_op jit(solution)/shard_map/ppermute | solution.py:16
  13.5 4.5 %collective-permute-start.5 = (bf16[256,128]{1,0:T(8,128)(2,1)S(1)}, bf16[256,128]{1,0:T(8,128)(2,1)S(1)}, u32[]{:S(2)}, u32[]{:S(2)}) collective-permute-start(bf16[256,128]{1,0:T(8,128)(2,1)S(1)} %collective-permute-done.1.refs_7_), channel_id=1, source_target_pairs={{0,4},{4,0},{8,12},{12,8},{16,20},{20,16},{24,28},{28,24},{1,5},{5... | collective-permute-start | bytes 196616 | tf_op jit(solution)/shard_map/ppermute | solution.py:16
  14.9 4.3 %collective-permute-start.4 = (bf16[256,128]{1,0:T(8,128)(2,1)S(1)}, bf16[256,128]{1,0:T(8,128)(2,1)S(1)}, u32[]{:S(2)}, u32[]{:S(2)}) collective-permute-start(bf16[256,128]{1,0:T(8,128)(2,1)S(1)} %collective-permute-done.2.refs_6_), channel_id=1, source_target_pairs={{0,4},{4,0},{8,12},{12,8},{16,20},{20,16},{24,28},{28,24},{1,5},{5... | collective-permute-start | bytes 196616 | tf_op jit(solution)/shard_map/ppermute | solution.py:16
  15.6 11.0 %copy-start.1 = (bf16[128,256]{1,0:T(8,128)(2,1)S(1)}, bf16[128,256]{1,0:T(8,128)(2,1)}, u32[]{:S(2)}) copy-start(bf16[128,256]{1,0:T(8,128)(2,1)} %refs_7_.1) | copy-start | bytes 196612
  15.6 11.0 %copy-start.2 = (bf16[128,256]{1,0:T(8,128)(2,1)S(1)}, bf16[128,256]{1,0:T(8,128)(2,1)}, u32[]{:S(2)}) copy-start(bf16[128,256]{1,0:T(8,128)(2,1)} %w_neigh.1) | copy-start | bytes 196612
  15.6 11.0 %copy-start.3 = (f32[256]{0:T(256)S(1)}, f32[256]{0:T(256)}, u32[]{:S(2)}) copy-start(f32[256]{0:T(256)} %param.13) | copy-start | bytes 3076
  19.5 1.4 %collective-permute-start.7 = (bf16[512,128]{1,0:T(8,128)(2,1)S(1)}, bf16[512,128]{1,0:T(8,128)(2,1)S(1)}, u32[]{:S(2)}, u32[]{:S(2)}) collective-permute-start(bf16[512,128]{1,0:T(8,128)(2,1)S(1)} %get-tuple-element.60), channel_id=1, source_target_pairs={{0,1},{1,0},{2,3},{3,2},{4,5},{5,4},{6,7},{7,6},{8,9},{9,8},{10,11... | collective-permute-start | bytes 393224 | tf_op jit(solution)/shard_map/ppermute | solution.py:16
  20.9 5.6 %collective-permute-start.9 = (bf16[512,128]{1,0:T(8,128)(2,1)S(1)}, bf16[512,128]{1,0:T(8,128)(2,1)S(1)}, u32[]{:S(2)}, u32[]{:S(2)}) collective-permute-start(bf16[512,128]{1,0:T(8,128)(2,1)S(1)} %shard_map.142.total), channel_id=1, source_target_pairs={{0,2},{1,3},{2,0},{3,1},{4,6},{5,7},{6,4},{7,5},{8,10},{9,11},{10,... | collective-permute-start | bytes 393224 | tf_op jit(solution)/shard_map/ppermute | solution.py:16
  27.2 1.4 %collective-permute-start.10 = (bf16[512,128]{1,0:T(8,128)(2,1)S(1)}, bf16[512,128]{1,0:T(8,128)(2,1)S(1)}, u32[]{:S(2)}, u32[]{:S(2)}) collective-permute-start(bf16[512,128]{1,0:T(8,128)(2,1)S(1)} %get-tuple-element.65.refs_4_), channel_id=1, source_target_pairs={{0,1},{1,0},{2,3},{3,2},{4,5},{5,4},{6,7},{7,6},{8,9},{9,8},{10,11... | collective-permute-start | bytes 393224 | tf_op jit(solution)/shard_map/ppermute | solution.py:16
  27.6 2.2 %collective-permute-start.17 = (f32[144,256]{1,0:T(8,128)S(1)}, f32[144,256]{1,0:T(8,128)S(1)}, u32[]{:S(2)}, u32[]{:S(2)}) collective-permute-start(f32[144,256]{1,0:T(8,128)S(1)} %get-tuple-element.83), channel_id=1, source_target_pairs={{0,1},{1,0},{2,3},{3,2},{4,5},{5,4},{6,7},{7,6},{8,9},{9,8},{10,11... | collective-permute-start | bytes 442376 | tf_op jit(solution)/shard_map/ppermute | solution.py:16
  29.0 11.1 %collective-permute-start.11 = (bf16[512,128]{1,0:T(8,128)(2,1)S(1)}, bf16[512,128]{1,0:T(8,128)(2,1)S(1)}, u32[]{:S(2)}, u32[]{:S(2)}) collective-permute-start(bf16[512,128]{1,0:T(8,128)(2,1)S(1)} %get-tuple-element.72), channel_id=1, source_target_pairs={{0,4},{4,0},{8,12},{12,8},{16,20},{20,16},{24,28},{28,24},{1,5},{5... | collective-permute-start | bytes 393224 | tf_op jit(solution)/shard_map/ppermute | solution.py:16
  29.8 6.6 %collective-permute-start.18 = (bf16[144,256]{1,0:T(8,128)(2,1)S(1)}, bf16[144,256]{1,0:T(8,128)(2,1)S(1)}, u32[]{:S(2)}, u32[]{:S(2)}) collective-permute-start(bf16[144,256]{1,0:T(8,128)(2,1)S(1)} %shard_map.152.kept), channel_id=1, source_target_pairs={{0,16},{4,20},{8,24},{12,28},{16,0},{20,4},{24,8},{28,12},{1,17},{... | collective-permute-start | bytes 221192 | tf_op jit(solution)/shard_map/ppermute | solution.py:16
  31.9 4.9 %collective-permute-start.12 = (bf16[256,128]{1,0:T(8,128)(2,1)S(1)}, bf16[256,128]{1,0:T(8,128)(2,1)S(1)}, u32[]{:S(2)}, u32[]{:S(2)}) collective-permute-start(bf16[256,128]{1,0:T(8,128)(2,1)S(1)} %get-tuple-element.70), channel_id=1, source_target_pairs={{0,4},{4,0},{8,12},{12,8},{16,20},{20,16},{24,28},{28,24},{1,5},{5... | collective-permute-start | bytes 196616 | tf_op jit(solution)/shard_map/ppermute | solution.py:16
  33.2 6.6 %collective-permute-start.14 = (bf16[256,128]{1,0:T(8,128)(2,1)S(1)}, bf16[256,128]{1,0:T(8,128)(2,1)S(1)}, u32[]{:S(2)}, u32[]{:S(2)}) collective-permute-start(bf16[256,128]{1,0:T(8,128)(2,1)S(1)} %get-tuple-element.71), channel_id=1, source_target_pairs={{0,4},{4,0},{8,12},{12,8},{16,20},{20,16},{24,28},{28,24},{1,5},{5... | collective-permute-start | bytes 196616 | tf_op jit(solution)/shard_map/ppermute | solution.py:16
  36.4 5.0 %collective-permute-start.19 = (bf16[144,256]{1,0:T(8,128)(2,1)S(1)}, bf16[144,256]{1,0:T(8,128)(2,1)S(1)}, u32[]{:S(2)}, u32[]{:S(2)}) collective-permute-start(bf16[144,256]{1,0:T(8,128)(2,1)S(1)} %shard_map.153.kept), channel_id=1, source_target_pairs={{0,8},{4,12},{8,0},{12,4},{16,24},{20,28},{24,16},{28,20},{1,9},{5... | collective-permute-start | bytes 221192 | tf_op jit(solution)/shard_map/ppermute | solution.py:16
  36.8 6.4 %collective-permute-start.13 = (bf16[256,128]{1,0:T(8,128)(2,1)S(1)}, bf16[256,128]{1,0:T(8,128)(2,1)S(1)}, u32[]{:S(2)}, u32[]{:S(2)}) collective-permute-start(bf16[256,128]{1,0:T(8,128)(2,1)S(1)} %shard_map.147.refs_0_), channel_id=1, source_target_pairs={{0,24},{4,28},{8,16},{12,20},{16,8},{20,12},{24,0},{28,4},{1,25},{... | collective-permute-start | bytes 196616 | tf_op jit(solution)/shard_map/ppermute | solution.py:16
  39.9 6.2 %collective-permute-start.15 = (bf16[256,128]{1,0:T(8,128)(2,1)S(1)}, bf16[256,128]{1,0:T(8,128)(2,1)S(1)}, u32[]{:S(2)}, u32[]{:S(2)}) collective-permute-start(bf16[256,128]{1,0:T(8,128)(2,1)S(1)} %shard_map.148.refs_0_), channel_id=1, source_target_pairs={{0,16},{4,20},{8,24},{12,28},{16,0},{20,4},{24,8},{28,12},{1,17},{... | collective-permute-start | bytes 196616 | tf_op jit(solution)/shard_map/ppermute | solution.py:16
  40.2 5.9 %collective-permute-start.16 = (bf16[256,128]{1,0:T(8,128)(2,1)S(1)}, bf16[256,128]{1,0:T(8,128)(2,1)S(1)}, u32[]{:S(2)}, u32[]{:S(2)}) collective-permute-start(bf16[256,128]{1,0:T(8,128)(2,1)S(1)} %shard_map.149.refs_0_), channel_id=1, source_target_pairs={{0,8},{4,12},{8,0},{12,4},{16,24},{20,28},{24,16},{28,20},{1,9},{5... | collective-permute-start | bytes 196616 | tf_op jit(solution)/shard_map/ppermute | solution.py:16
  41.5 4.7 %collective-permute-start.20 = (bf16[144,256]{1,0:T(8,128)(2,1)S(1)}, bf16[144,256]{1,0:T(8,128)(2,1)S(1)}, u32[]{:S(2)}, u32[]{:S(2)}) collective-permute-start(bf16[144,256]{1,0:T(8,128)(2,1)S(1)} %shard_map.154.kept), channel_id=1, source_target_pairs={{0,4},{4,0},{8,12},{12,8},{16,20},{20,16},{24,28},{28,24},{1,5},{5... | collective-permute-start | bytes 221192 | tf_op jit(solution)/shard_map/ppermute | solution.py:16
  46.2 1.4 %collective-permute-start.21 = (f32[128,256]{1,0:T(8,128)S(1)}, f32[128,256]{1,0:T(8,128)S(1)}, u32[]{:S(2)}, u32[]{:S(2)}) collective-permute-start(f32[128,256]{1,0:T(8,128)S(1)} %slice.4), channel_id=1, source_target_pairs={{0,1},{1,0},{2,3},{3,2},{4,5},{5,4},{6,7},{7,6},{8,9},{9,8},{10,11... | collective-permute-start | bytes 393224 | tf_op jit(solution)/shard_map/ppermute | solution.py:16
